TPU v7x, 32 devices: a whole 2x2x4 slice. The times are simulated.
32 devices in a mesh: dp: 4 (over x, core), row: 2 (over y), col: 4 (over z).
Axes of the slice: x: 2, y: 2, z: 4, core: 2. Of those that a mesh axis runs over, the one named last changes fastest.
Arguments:
- latents: bfloat16 [4096, 768], P(('dp', 'col'), 'row'), may hold values from -6 to 6
- labels: int32 [16], P('dp'), may hold values from 0 to 999
- step_ids: int32 [16], P('dp'), may hold values from 0 to 999
- class_table: bfloat16 [1000, 768], P('col'), may hold values from -6 to 6
- step_table: bfloat16 [1000, 768], P('col'), may hold values from -6 to 6
- w_ada: bfloat16 [1, 768, 6, 768], P(None, 'col', None, 'row'), may hold values from -0.21875 to 0.21875
- b_ada: bfloat16 [1, 6, 768], P(None, None, 'row'), may hold values from -3 to 3
- w_qkv: bfloat16 [1, 768, 3, 768], P(None, 'row', None, 'col'), may hold values from -0.21875 to 0.21875
- b_qkv: bfloat16 [1, 2, 768], P(None, None, 'col'), may hold values from -3 to 3
- w_out: bfloat16 [1, 768, 768], P(None, 'col', 'row'), may hold values from -0.875 to 0.875
- b_out: bfloat16 [1, 768], P(None, 'row'), may hold values from -3 to 3
- w_up: bfloat16 [1, 768, 3072], P(None, 'row', 'col'), may hold values from -0.21875 to 0.21875
- b_up: bfloat16 [1, 3072], P(None, 'col'), may hold values from -3 to 3
- w_down: bfloat16 [1, 3072, 768], P(None, 'col', 'row'), may hold values from -0.109375 to 0.109375
- b_down: bfloat16 [1, 768], P(None, 'row'), may hold values from -3 to 3
- cotangent: bfloat16 [4096, 768], P(('dp', 'col'), 'row'), may hold values from -6 to 6
Outputs:
- output: bfloat16 [4096, 768], P(('dp', 'col'), 'row')
- grad_latents: bfloat16 [4096, 768], P(('dp', 'col'), 'row')
- grad_class_table: float32 [1000, 768], P('col')
- grad_step_table: float32 [1000, 768], P('col')
- grad_w_ada: float32 [1, 768, 6, 768], P(None, 'col', None, 'row')
- grad_b_ada: float32 [1, 6, 768], P(None, None, 'row')
- grad_w_qkv: float32 [1, 768, 3, 768], P(None, 'row', None, 'col')
- grad_b_qkv: float32 [1, 2, 768], P(None, None, 'col')
- grad_w_out: float32 [1, 768, 768], P(None, 'col', 'row')
- grad_b_out: float32 [1, 768], P(None, 'row')
- grad_w_up: float32 [1, 768, 3072], P(None, 'row', 'col')
- grad_b_up: float32 [1, 3072], P(None, 'col')
- grad_w_down: float32 [1, 3072, 768], P(None, 'col', 'row')
- grad_b_down: float32 [1, 768], P(None, 'row')
All inputs are finite; a program needn't handle non-finite values.
Results may differ from a plain program's by a relative error of at most 0.015.
The roundings to bfloat16 on the way count: a program that leaves them out, or rounds other values in their place, can miss the bound.
Values may be sent and summed in bfloat16 or wider, within the bound.
No kernel may reach another device: no remote copies, remote signals or barrier semaphores. Data moves between devices by JAX's collectives and lax.ppermute only.
A program may use at most 192 MiB of HBM per device.

v0:
```python
from functools import partial

import jax
import jax.numpy as jnp
from jax import lax
from jax.sharding import PartitionSpec as P

D = 768
HEAD_DIM = 64
LENGTH = 256


PRECISE = lax.Precision.HIGHEST
NORM_EPSILON = 1e-06


def contract_rows(left, right):
    return lax.dot_general(
        left, right, (((0,), (0,)), ((), ())), preferred_element_type=jnp.float32
    )


def feature_sums(first, second):
    return lax.psum((first, second), "row")


def norm_forward(residual):
    totals = feature_sums(jnp.sum(residual, axis=1), jnp.sum(residual * residual, axis=1))
    mean_row = totals[0] / D
    variance = totals[1] / D - mean_row * mean_row
    inverse_std = lax.rsqrt(variance + NORM_EPSILON)
    return ((residual - mean_row[:, None]) * inverse_std[:, None], inverse_std)


def norm_backward(dnormed, normed, inverse_std):
    totals = feature_sums(jnp.sum(dnormed, axis=1), jnp.sum(dnormed * normed, axis=1))
    return inverse_std[:, None] * (
        dnormed - totals[0][:, None] / D - normed * totals[1][:, None] / D
    )


def gather_width(local_rows):
    return lax.all_gather(local_rows, "col", axis=0, tiled=True)


def gather_tokens(local_rows):
    return lax.all_gather(local_rows, "row", axis=0, tiled=True)


def row_project(gathered, block, contract_dim):
    return lax.psum_scatter(
        lax.dot_general(
            gathered, block, (((1,), (contract_dim,)), ((), ())), preferred_element_type=jnp.float32
        ),
        "row",
        scatter_dimension=0,
        tiled=True,
    )


def col_project(gathered, weight, contract_dim):
    return lax.psum_scatter(
        lax.dot_general(
            gathered,
            weight,
            (((1,), (contract_dim,)), ((), ())),
            preferred_element_type=jnp.float32,
        ),
        "col",
        scatter_dimension=0,
        tiled=True,
    )


def across_rows(hidden, block):
    gathered = gather_width(hidden)
    return (row_project(gathered, block, 0), gathered)


def across_cols(local_rows, weight):
    gathered = gather_tokens(local_rows)
    return (col_project(gathered, weight, 0), gathered)


def back_cols(dbranch, weight, held_in):
    dgathered = gather_width(dbranch)
    dinput = row_project(dgathered, weight, 1)
    return (
        dinput,
        contract_rows(held_in, dgathered),
        jnp.sum(dgathered, axis=0, dtype=jnp.float32),
    )


def back_rows(doutput, weight, held_in):
    dgathered = gather_tokens(doutput)
    dinput = col_project(dgathered, weight, 1)
    return (
        dinput,
        contract_rows(held_in, dgathered),
        jnp.sum(dgathered, axis=0, dtype=jnp.float32),
    )


def attend(queries, key_rows, value_rows):
    scores = jnp.einsum(
        "slhe,smhe->shlm", queries, key_rows, preferred_element_type=jnp.float32
    ) * HEAD_DIM ** (-0.5)
    highest = jnp.max(scores, axis=-1, keepdims=True)
    log_total = highest + jnp.log(jnp.sum(jnp.exp(scores - highest), axis=-1, keepdims=True))
    weights_soft = jnp.exp(scores - log_total).astype(jnp.bfloat16)
    attended = jnp.einsum(
        "shlm,smhe->slhe", weights_soft, value_rows, preferred_element_type=jnp.float32
    )
    return (attended, log_total)


def attend_back(queries, key_rows, value_rows, log_total, dattended):
    score_scale = HEAD_DIM ** (-0.5)
    scores = (
        jnp.einsum("slhe,smhe->shlm", queries, key_rows, preferred_element_type=jnp.float32)
        * score_scale
    )
    weights_soft = jnp.exp(scores - log_total)
    rounded_soft = weights_soft.astype(jnp.bfloat16)
    dweights = jnp.einsum(
        "slhe,smhe->shlm", dattended, value_rows, preferred_element_type=jnp.float32
    )
    dscores = weights_soft * (dweights - jnp.sum(weights_soft * dweights, axis=-1, keepdims=True))
    dscores = dscores.astype(jnp.bfloat16)
    dqueries = (
        jnp.einsum("shlm,smhe->slhe", dscores, key_rows, preferred_element_type=jnp.float32)
        * score_scale
    )
    dkeys = (
        jnp.einsum("shlm,slhe->smhe", dscores, queries, preferred_element_type=jnp.float32)
        * score_scale
    )
    dvalues = jnp.einsum(
        "shlm,slhe->smhe", rounded_soft, dattended, preferred_element_type=jnp.float32
    )
    return (dqueries, dkeys, dvalues)


def body(
    latents,
    labels,
    step_ids,
    class_table,
    step_table,
    w_ada,
    b_ada,
    w_qkv,
    b_qkv,
    w_out,
    b_out,
    w_up,
    b_up,
    w_down,
    b_down,
    cotangent,
):
    rows_res, width_row = latents.shape
    sequences = labels.shape[0]
    width_col = w_qkv.shape[3]
    width_cond = w_ada.shape[1]
    layers = w_qkv.shape[0]
    head_shape = (-1, LENGTH, width_col // HEAD_DIM, HEAD_DIM)
    col_at = lax.axis_index("col")
    position = col_at * rows_res + jnp.arange(rows_res, dtype=jnp.int32)
    owners = (
        (position // LENGTH)[:, None] == jnp.arange(sequences, dtype=jnp.int32)[None, :]
    ).astype(jnp.float32)
    class_rows = class_table.shape[0]
    step_rows = step_table.shape[0]
    class_hot = (
        labels[:, None] == (col_at * class_rows + jnp.arange(class_rows, dtype=jnp.int32))[None, :]
    ).astype(jnp.float32)
    step_hot = (
        step_ids[:, None] == (col_at * step_rows + jnp.arange(step_rows, dtype=jnp.int32))[None, :]
    ).astype(jnp.float32)
    partial_cond = jnp.dot(class_hot, class_table.astype(jnp.float32), precision=PRECISE) + jnp.dot(
        step_hot, step_table.astype(jnp.float32), precision=PRECISE
    )
    condition = lax.psum(partial_cond, "col")
    cond_full, silu_pull = jax.vjp(jax.nn.silu, condition)
    cond_act = lax.dynamic_slice_in_dim(cond_full, col_at * width_cond, width_cond, 1)
    ada_weight = w_ada.astype(jnp.float32)
    modulation = (
        lax.psum(jnp.einsum("bd,ldjf->bljf", cond_act, ada_weight, precision=PRECISE), "col")
        + b_ada.astype(jnp.float32)[None]
    )
    per_token = jnp.einsum("tb,bljf->tljf", owners, modulation, precision=PRECISE)
    residual = latents.astype(jnp.float32)
    layer_at = 0
    factors = per_token[:, layer_at]
    qkv_block = w_qkv[layer_at].reshape(width_row, 3 * width_col)
    wholes = (None, None, None, None)
    normed_in, inverse_in = norm_forward(residual)
    hidden_in = (normed_in * (1.0 + factors[:, 1]) + factors[:, 0]).astype(jnp.bfloat16)
    projected, hidden_all = across_rows(hidden_in, qkv_block)
    queries = (
        (projected[:, :width_col] + b_qkv[layer_at, 0].astype(jnp.float32))
        .astype(jnp.bfloat16)
        .reshape(head_shape)
    )
    key_rows = projected[:, width_col : 2 * width_col].astype(jnp.bfloat16).reshape(head_shape)
    value_rows = (
        (projected[:, 2 * width_col :] + b_qkv[layer_at, 1].astype(jnp.float32))
        .astype(jnp.bfloat16)
        .reshape(head_shape)
    )
    attended, log_total = attend(queries, key_rows, value_rows)
    attended = attended.reshape(-1, width_col).astype(jnp.bfloat16)
    branch_pre, attended_all = across_cols(attended, w_out[layer_at])
    branch_one = branch_pre + b_out[layer_at].astype(jnp.float32)
    middle = residual + factors[:, 2] * branch_one
    normed_mid, inverse_mid = norm_forward(middle)
    hidden_mid = (normed_mid * (1.0 + factors[:, 4]) + factors[:, 3]).astype(jnp.bfloat16)
    up_pre, hidden_mid_all = across_rows(hidden_mid, w_up[layer_at])
    up_proj = up_pre + b_up[layer_at].astype(jnp.float32)
    activated = jax.nn.gelu(up_proj, approximate=True).astype(jnp.bfloat16)
    down_pre, activated_all = across_cols(activated, w_down[layer_at])
    branch_two = down_pre + b_down[layer_at].astype(jnp.float32)
    saved = [
        (
            normed_in,
            inverse_in,
            hidden_all,
            queries,
            key_rows,
            value_rows,
            log_total,
            attended,
            attended_all,
            branch_one,
            normed_mid,
            inverse_mid,
            hidden_mid_all,
            up_proj,
            activated,
            activated_all,
            branch_two,
            wholes,
        )
    ]
    residual = middle + factors[:, 5] * branch_two
    gradient = cotangent.astype(jnp.float32)
    dmod_layers = [None] * layers
    grad_lists = [[None] * layers for index_at in range(8)]
    for layer_at in reversed(range(layers)):
        factors = per_token[:, layer_at]
        (
            normed_in,
            inverse_in,
            hidden_all,
            queries,
            key_rows,
            value_rows,
            log_total,
            attended,
            attended_all,
            branch_one,
            normed_mid,
            inverse_mid,
            hidden_mid_all,
            up_proj,
            activated,
            activated_all,
            branch_two,
            wholes,
        ) = saved[layer_at]
        dgate_two = gradient * branch_two
        dbranch_two = (factors[:, 5] * gradient).astype(jnp.bfloat16)
        held_act = gather_tokens(activated)
        dactivated, grad_down, bias_down = back_cols(dbranch_two, w_down[layer_at], held_act)
        gelu_out, gelu_pull = jax.vjp(partial(jax.nn.gelu, approximate=True), up_proj)
        dup_proj = gelu_pull(dactivated)[0].astype(jnp.bfloat16)
        dhidden_mid, grad_up, bias_up = back_rows(dup_proj, w_up[layer_at], hidden_mid_all)
        dscale_two = dhidden_mid * normed_mid
        dmiddle = gradient + norm_backward(
            dhidden_mid * (1.0 + factors[:, 4]), normed_mid, inverse_mid
        )
        dgate_one = dmiddle * branch_one
        dbranch_one = (factors[:, 2] * dmiddle).astype(jnp.bfloat16)
        held_att = gather_tokens(attended)
        dattended, grad_out, bias_out = back_cols(dbranch_one, w_out[layer_at], held_att)
        dattended = dattended.astype(jnp.bfloat16).reshape(head_shape)
        dqueries, dkeys, dvalues = attend_back(queries, key_rows, value_rows, log_total, dattended)
        dprojected = jnp.concatenate(
            [
                dqueries.reshape(-1, width_col),
                dkeys.reshape(-1, width_col),
                dvalues.reshape(-1, width_col),
            ],
            axis=1,
        ).astype(jnp.bfloat16)
        dhidden_in, grad_qkv, bias_qkv = back_rows(
            dprojected, w_qkv[layer_at].reshape(width_row, 3 * width_col), hidden_all
        )
        dscale_one = dhidden_in * normed_in
        gradient = dmiddle + norm_backward(
            dhidden_in * (1.0 + factors[:, 1]), normed_in, inverse_in
        )
        dmod_layers[layer_at] = jnp.stack(
            [dhidden_in, dscale_one, dgate_one, dhidden_mid, dscale_two, dgate_two], axis=1
        )
        grad_lists[0][layer_at] = grad_qkv.reshape(width_row, 3, width_col)
        grad_lists[1][layer_at] = jnp.stack(
            [bias_qkv[:width_col], bias_qkv[2 * width_col :]], axis=0
        )
        grad_lists[2][layer_at] = grad_out
        grad_lists[3][layer_at] = bias_out
        grad_lists[4][layer_at] = grad_up
        grad_lists[5][layer_at] = bias_up
        grad_lists[6][layer_at] = grad_down
        grad_lists[7][layer_at] = bias_down
    dmod_tokens = jnp.stack(dmod_layers, axis=1)
    dmodulation = lax.psum(
        jnp.einsum("tb,tljf->bljf", owners, dmod_tokens, precision=PRECISE), "col"
    )
    grad_bias_ada = jnp.sum(dmodulation, axis=0)
    grad_weight_ada = jnp.einsum("bd,bljf->ldjf", cond_act, dmodulation, precision=PRECISE)
    dcond_local = jnp.einsum("bljf,ldjf->bd", dmodulation, ada_weight, precision=PRECISE)
    dcond_placed = lax.dynamic_update_slice_in_dim(
        jnp.zeros((sequences, cond_full.shape[1]), jnp.float32), dcond_local, col_at * width_cond, 1
    )
    dcond_act = lax.psum(dcond_placed, ("row", "col"))
    dcondition = silu_pull(dcond_act)[0]
    grad_class = lax.dot_general(class_hot, dcondition, (((0,), (0,)), ((), ())), precision=PRECISE)
    grad_step = lax.dot_general(step_hot, dcondition, (((0,), (0,)), ((), ())), precision=PRECISE)
    stacked = [jnp.stack(items, axis=0) for items in grad_lists]
    summed = lax.psum(
        (
            grad_class,
            grad_step,
            grad_weight_ada,
            grad_bias_ada,
            stacked[0],
            stacked[1],
            stacked[2],
            stacked[3],
            stacked[4],
            stacked[5],
            stacked[6],
            stacked[7],
        ),
        "dp",
    )
    return (
        residual.astype(jnp.bfloat16),
        gradient.astype(jnp.bfloat16),
        summed[0],
        summed[1],
        summed[2],
        summed[3],
        summed[4],
        summed[5],
        summed[6],
        summed[7],
        summed[8],
        summed[9],
        summed[10],
        summed[11],
    )


def solution(mesh):
    return jax.shard_map(
        body,
        mesh=mesh,
        in_specs=(
            P(("dp", "col"), "row"),
            P("dp"),
            P("dp"),
            P("col", None),
            P("col", None),
            P(None, "col", None, "row"),
            P(None, None, "row"),
            P(None, "row", None, "col"),
            P(None, None, "col"),
            P(None, "col", "row"),
            P(None, "row"),
            P(None, "row", "col"),
            P(None, "col"),
            P(None, "col", "row"),
            P(None, "row"),
            P(("dp", "col"), "row"),
        ),
        out_specs=(
            P(("dp", "col"), "row"),
            P(("dp", "col"), "row"),
            P("col", None),
            P("col", None),
            P(None, "col", None, "row"),
            P(None, None, "row"),
            P(None, "row", None, "col"),
            P(None, None, "col"),
            P(None, "col", "row"),
            P(None, "row"),
            P(None, "row", "col"),
            P(None, "col"),
            P(None, "col", "row"),
            P(None, "row"),
        ),
        check_vma=False,
    )
```

profile of v0, /device:TPU:0, one launch (start us, length us, event | category | flops | bytes accessed | tf_op | source)
XLA Modules:
  0.0 728.8 jit_solution(6562340037708805233)
XLA Ops:
  10.9 20.4 %psum.168 = f32[4,768]{1,0:T(4,128)S(1)} all-reduce(f32[4,768]{1,0:T(4,128)S(1)} %convolution_add_fusion), channel_id=1, replica_groups=mesh['dp'=4,'row'=2,'col'=4] {'col'}, use_global_device_ids=true, to_apply=%region_0.1 | all-reduce | flops 3072 | bytes 24576 | tf_op jit(solution)/shard_map/psum | solution.py:185
  32.5 16.1 %psum.169 = f32[4,1,6,384]{3,0,2,1:T(4,128)S(1)} all-reduce(f32[4,1,6,384]{3,0,2,1:T(4,128)S(1)} %convolution_bitcast_fusion.5), channel_id=1, replica_groups=mesh['dp'=4,'row'=2,'col'=4] {'col'}, use_global_device_ids=true, to_apply=%region_1.2 | all-reduce | flops 9216 | bytes 73728 | tf_op jit(solution)/shard_map/psum | solution.py:190
  48.6 4.9 all-reduce.5
  54.7 1.4 copy-done.1
  56.3 15.6 %all_gather.26 = bf16[1024,384]{1,0:T(8,128)(2,1)S(1)} all-gather(bf16[256,384]{1,0:T(8,128)(2,1)S(1)} %fusion.33), channel_id=1, replica_groups=mesh['dp'=4,'row'=2,'col'=4] {'col'}, dimensions={0}, use_global_device_ids=true | all-gather | bytes 983040 | tf_op jit(solution)/shard_map/all_gather | solution.py:43
  72.8 2.2 fusion.104
  75.8 33.9 %reduce-scatter.9.cloned.1.call-done = f32[512,576]{0,1:T(8,128)} async-done(((f32[1024,576]{0,1:T(8,128)}), f32[512,576]{0,1:T(8,128)}) %reduce-scatter.9.cloned.1.call-update) | async-done | bytes 1179664 | tf_op jit(solution)/shard_map/reduce_scatter | solution.py:51
  113.5 7.3 %all_gather.27 = bf16[1024,192]{0,1:T(8,128)(2,1)S(1)} all-gather(bf16[512,192]{0,1:T(8,128)(2,1)S(1)} %bitcast.196), channel_id=1, replica_groups=mesh['dp'=4,'row'=2,'col'=4] {'row'}, dimensions={0}, use_global_device_ids=true | all-gather | bytes 589824 | tf_op jit(solution)/shard_map/all_gather | solution.py:47
  121.6 1.6 fusion.64
  123.4 35.4 %reduce-scatter.11.cloned.1.call-done = f32[256,384]{1,0:T(8,128)} async-done(((f32[1024,384]{1,0:T(8,128)}), f32[256,384]{1,0:T(8,128)}) %reduce-scatter.11.cloned.1.call-update) | async-done | bytes 393232 | tf_op jit(solution)/shard_map/reduce_scatter | solution.py:62
  160.0 4.9 all-reduce.4
  165.0 1.5 fusion.24
  166.5 17.6 %all_gather.28 = bf16[1024,384]{1,0:T(8,128)(2,1)S(1)} all-gather(bf16[256,384]{1,0:T(8,128)(2,1)S(1)} %get-tuple-element.47), channel_id=1, replica_groups=mesh['dp'=4,'row'=2,'col'=4] {'col'}, dimensions={0}, use_global_device_ids=true | all-gather | bytes 983040 | tf_op jit(solution)/shard_map/all_gather | solution.py:43
  185.0 2.6 fusion.22
  187.7 17.1 %all_gather.30 = bf16[1024,384]{1,0:T(8,128)(2,1)S(1)} all-gather(bf16[256,384]{1,0:T(8,128)(2,1)S(1)} %get-tuple-element.46), channel_id=1, replica_groups=mesh['dp'=4,'row'=2,'col'=4] {'col'}, dimensions={0}, use_global_device_ids=true | all-gather | bytes 983040 | tf_op jit(solution)/shard_map/all_gather | solution.py:43
  205.8 3.8 fusion.16
  210.2 20.4 %reduce-scatter.13.cloned.1.call-done = f32[512,768]{1,0:T(8,128)} async-done(((f32[1024,768]{1,0:T(8,128)}), f32[512,768]{1,0:T(8,128)}) %reduce-scatter.13.cloned.1.call-update) | async-done | bytes 1572880 | tf_op jit(solution)/shard_map/reduce_scatter | solution.py:51
  230.6 45.5 %reduce-scatter.17.cloned.1.call-done = f32[512,768]{1,0:T(8,128)} async-done(((f32[1024,768]{1,0:T(8,128)}), f32[512,768]{1,0:T(8,128)}) %reduce-scatter.17.cloned.1.call-update) | async-done | bytes 1572880 | tf_op jit(solution)/shard_map/reduce_scatter | solution.py:51
  276.1 4.2 fusion.6
  281.0 26.7 %all-gather.6.cloned.1.call-done = bf16[1024,768]{1,0:T(8,128)(2,1)} async-done(((bf16[512,768]{1,0:T(8,128)(2,1)}), bf16[1024,768]{1,0:T(8,128)(2,1)}) %all-gather.6.cloned.1.call-update) | async-done | bytes 1572880 | tf_op jit(solution)/shard_map/all_gather | solution.py:47
  307.7 3.7 fusion.20
  311.4 25.5 %all-gather.4.cloned.1.call-done = bf16[1024,768]{1,0:T(8,128)(2,1)} async-done(((bf16[512,768]{1,0:T(8,128)(2,1)}), bf16[1024,768]{1,0:T(8,128)(2,1)}) %all-gather.4.cloned.1.call-update) | async-done | bytes 1572880 | tf_op jit(solution)/shard_map/all_gather | solution.py:47
  337.0 3.6 fusion.18
  341.3 33.9 %reduce-scatter.19.cloned.1.call-done = f32[256,384]{1,0:T(8,128)} async-done(((f32[1024,384]{1,0:T(8,128)}), f32[256,384]{1,0:T(8,128)}) %reduce-scatter.19.cloned.1.call-update) | async-done | bytes 393232 | tf_op jit(solution)/shard_map/reduce_scatter | solution.py:62
  376.6 4.9 all-reduce.3
  381.6 30.4 %reduce-scatter.15.cloned.1.call-done = f32[256,384]{1,0:T(8,128)} async-done(((f32[1024,384]{1,0:T(8,128)}), f32[256,384]{1,0:T(8,128)}) %reduce-scatter.15.cloned.1.call-update) | async-done | bytes 393232 | tf_op jit(solution)/shard_map/reduce_scatter | solution.py:62
  412.0 2.5 multiply_convert_fusion.2
  414.5 18.1 %all_gather.32 = bf16[1024,384]{1,0:T(8,128)(2,1)S(1)} all-gather(bf16[256,384]{1,0:T(8,128)(2,1)S(1)} %get-tuple-element.42), channel_id=1, replica_groups=mesh['dp'=4,'row'=2,'col'=4] {'col'}, dimensions={0}, use_global_device_ids=true | all-gather | bytes 983040 | tf_op jit(solution)/shard_map/all_gather | solution.py:43
  434.2 16.6 %reduce-scatter.21.cloned.1.call-done = f32[512,192]{0,1:T(8,128)} async-done(((f32[1024,192]{0,1:T(8,128)}), f32[512,192]{0,1:T(8,128)}) %reduce-scatter.21.cloned.1.call-update) | async-done | bytes 393232 | tf_op jit(solution)/shard_map/reduce_scatter | solution.py:51
  450.9 1.7 convert_element_type.121
  452.6 1.7 reshape.145
  459.3 22.9 %all-gather.8.cloned.1.call-done = bf16[1024,576]{0,1:T(8,128)(2,1)} async-done(((bf16[512,576]{0,1:T(8,128)(2,1)}), bf16[1024,576]{0,1:T(8,128)(2,1)}) %all-gather.8.cloned.1.call-update) | async-done | bytes 1179664 | tf_op jit(solution)/shard_map/all_gather | solution.py:47
  482.2 3.4 fusion.105
  487.0 3.1 convolution_bitcast_fusion.2
  490.1 2.0 convolution_bitcast_fusion.1
  493.2 1.7 fusion.106
  494.9 26.1 %reduce-scatter.23.cloned.1.call-done = f32[256,384]{1,0:T(8,128)} async-done(((f32[1024,384]{1,0:T(8,128)}), f32[256,384]{1,0:T(8,128)}) %reduce-scatter.23.cloned.1.call-update) | async-done | bytes 393232 | tf_op jit(solution)/shard_map/reduce_scatter | solution.py:62
  525.4 17.4 %psum.178 = f32[4,1,6,384]{3,0,2,1:T(4,128)S(1)} all-reduce(f32[4,1,6,384]{3,0,2,1:T(4,128)S(1)} %convolution_bitcast_fusion.4), channel_id=1, replica_groups=mesh['dp'=4,'row'=2,'col'=4] {'col'}, use_global_device_ids=true, to_apply=%region_29.30 | all-reduce | flops 9216 | bytes 73728 | tf_op jit(solution)/shard_map/psum | solution.py:319
  543.8 34.5 %psum.179 = f32[4,768]{1,0:T(4,128)S(1)} all-reduce(f32[4,768]{1,0:T(4,128)S(1)} %dynamic_update_slice.3), channel_id=1, replica_groups=mesh['dp'=4,'row'=2,'col'=4] {'row','col'}, use_global_device_ids=true, to_apply=%region_30.31 | all-reduce | flops 3072 | bytes 24576 | tf_op jit(solution)/shard_map/psum | solution.py:328
  578.4 1.5 fusion.74
  579.9 2.1 fusion.77
  582.0 2.9 convolution_bitcast_fusion
  584.9 1.4 convert_reduce_fusion.2
  588.9 4.9 all-reduce.2
  593.9 12.1 %all-reduce = (f32[1,6,384]{2,0,1:T(1,128)}, f32[1,2,192]{2,1,0:T(2,128)}, f32[1,384]{1,0:T(1,128)}, f32[1,768]{1,0:T(1,128)}, f32[1,384]{1,0:T(1,128)}) all-reduce(f32[1,6,384]{2,0,1:T(1,128)S(1)} %reduce_sum.148, f32[1,2,192]{2,1,0:T(2,128)S(1)} %maximum_bitcast_fusion, ...), channel_id=1, replica_groups=mesh['dp'=4,'row'=2,'col'=4] {'dp'}, use_global_device_ids=true, to_apply=%region_35.36 | all-reduce | flops 4224 | bytes 33792 | tf_op jit(solution)/shard_map/psum | solution.py:333
  606.0 1.9 fusion.39
  607.9 105.3 %all-reduce.8.cloned.1.call-done = (f32[250,768]{1,0:T(8,128)}, f32[250,768]{1,0:T(8,128)}, f32[1,192,6,384]{3,1,2,0:T(8,128)}, f32[1,384,3,192]{1,3,2,0:T(8,128...) async-done(((f32[250,768]{1,0:T(8,128)}, f32[250,768]{1,0:T(8,128)}, f32[1,192,6,384]{3,1,2,0:T(8,128)}, f32[1,384,3,192]{1,3,2,0:T(8,128)}, ...) | async-done | bytes 6844432 | tf_op jit(solution)/shard_map/psum | solution.py:333
  713.2 2.2 copy.103
  (189 shorter events, 42.4 us)
Async XLA Ops:
  7.2 24.8 %copy-start = (bf16[1,192,6,384]{3,1,2,0:T(8,128)(2,1)S(1)}, bf16[1,192,6,384]{3,1,2,0:T(8,128)(2,1)}, u32[]{:S(2)}) copy-start(bf16[1,192,6,384]{3,1,2,0:T(8,128)(2,1)} %param.21) | copy-start | bytes 2654212
  7.2 102.5 %reduce-scatter.9.cloned.1.call-start = ((), (), s32[]{:S(2)}) async-start(), calls=%async_computation.8 | async-start | bytes 3538944 | tf_op jit(solution)/shard_map/reduce_scatter | solution.py:51
  32.0 24.1 %copy-start.6 = (bf16[256,384]{1,0:T(8,128)(2,1)S(1)}, bf16[256,384]{1,0:T(8,128)(2,1)}, u32[]{:S(2)}) copy-start(bf16[256,384]{1,0:T(8,128)(2,1)} %param.16) | copy-start | bytes 589828
  54.7 1.4 copy-start.1
  54.7 18.1 %copy-start.21 = (bf16[1,384,3,192]{1,3,2,0:T(8,128)(2,1)S(1)}, bf16[1,384,3,192]{1,3,2,0:T(8,128)(2,1)}, u32[]{:S(2)}) copy-start(bf16[1,384,3,192]{1,3,2,0:T(8,128)(2,1)} %param.23) | copy-start | bytes 1327108
  75.1 83.6 %reduce-scatter.11.cloned.1.call-start = ((), (), s32[]{:S(2)}) async-start(), calls=%async_computation.9 | async-start | bytes 1966080 | tf_op jit(solution)/shard_map/reduce_scatter | solution.py:62
  110.8 1.9 copy-start.25
  112.9 8.7 %copy-start.38 = (bf16[1,192,384]{2,1,0:T(8,128)(2,1)S(1)}, bf16[1,192,384]{2,1,0:T(8,128)(2,1)}, u32[]{:S(2)}) copy-start(bf16[1,192,384]{2,1,0:T(8,128)(2,1)} %param.25) | copy-start | bytes 442372
  121.6 1.7 copy-start.44
  123.2 41.8 %copy-start.23 = (bf16[256,384]{1,0:T(8,128)(2,1)S(1)}, bf16[256,384]{1,0:T(8,128)(2,1)}, u32[]{:S(2)}) copy-start(bf16[256,384]{1,0:T(8,128)(2,1)} %param.31) | copy-start | bytes 589828
  123.3 107.4 %reduce-scatter.13.cloned.1.call-start = ((), (), s32[]{:S(2)}) async-start(), calls=%async_computation.10 | async-start | bytes 4718592 | tf_op jit(solution)/shard_map/reduce_scatter | solution.py:51
  160.0 252.0 %copy-start.3 = (f32[256,384]{1,0:T(8,128)}, f32[256,384]{1,0:T(8,128)S(1)}, u32[]{:S(2)}) copy-start(f32[256,384]{1,0:T(8,128)S(1)} %get-tuple-element.44) | copy-start | bytes 1179652
  165.0 20.0 %copy-start.19 = (bf16[1,384,768]{2,1,0:T(8,128)(2,1)S(1)}, bf16[1,384,768]{2,1,0:T(8,128)(2,1)}, u32[]{:S(2)}) copy-start(bf16[1,384,768]{2,1,0:T(8,128)(2,1)} %param.27) | copy-start | bytes 1769476
  187.7 88.4 %reduce-scatter.17.cloned.1.call-start = ((), (), s32[]{:S(2)}) async-start(), calls=%async_computation.13 | async-start | bytes 4718592 | tf_op jit(solution)/shard_map/reduce_scatter | solution.py:51
  209.6 98.1 %all-gather.6.cloned.1.call-start = ((), (), s32[]{:S(2)}) async-start(), calls=%async_computation.14 | async-start | bytes 2359296 | tf_op jit(solution)/shard_map/all_gather | solution.py:47
  280.3 56.7 %all-gather.4.cloned.1.call-start = ((), (), s32[]{:S(2)}) async-start(), calls=%async_computation.11 | async-start | bytes 2359296 | tf_op jit(solution)/shard_map/all_gather | solution.py:47
  280.9 94.4 %reduce-scatter.19.cloned.1.call-start = ((), (), s32[]{:S(2)}) async-start(), calls=%async_computation.15 | async-start | bytes 1966080 | tf_op jit(solution)/shard_map/reduce_scatter | solution.py:62
  311.4 100.6 %reduce-scatter.15.cloned.1.call-start = ((), (), s32[]{:S(2)}) async-start(), calls=%async_computation.12 | async-start | bytes 1966080 | tf_op jit(solution)/shard_map/reduce_scatter | solution.py:62
  340.7 110.2 %reduce-scatter.21.cloned.1.call-start = ((), (), s32[]{:S(2)}) async-start(), calls=%async_computation.16 | async-start | bytes 1179648 | tf_op jit(solution)/shard_map/reduce_scatter | solution.py:51
  412.0 20.7 %copy-start.39 = (bf16[1,192,384]{2,1,0:T(8,128)(2,1)S(1)}, bf16[1,192,384]{2,1,0:T(8,128)(2,1)}, u32[]{:S(2)}) copy-start(bf16[1,192,384]{2,1,0:T(8,128)(2,1)} %param.25) | copy-start | bytes 442372
  434.0 48.2 %all-gather.8.cloned.1.call-start = ((), (), s32[]{:S(2)}) async-start(), calls=%async_computation.17 | async-start | bytes 1769472 | tf_op jit(solution)/shard_map/all_gather | solution.py:47
  454.2 1.4 copy-start.30
  454.2 1.4 copy-start.31
  456.1 1.3 copy-start.26
  458.1 24.1 %copy-start.22 = (bf16[1,384,3,192]{1,3,2,0:T(8,128)(2,1)S(1)}, bf16[1,384,3,192]{1,3,2,0:T(8,128)(2,1)}, u32[]{:S(2)}) copy-start(bf16[1,384,3,192]{1,3,2,0:T(8,128)(2,1)} %param.23) | copy-start | bytes 1327108
  459.2 61.8 %reduce-scatter.23.cloned.1.call-start = ((), (), s32[]{:S(2)}) async-start(), calls=%async_computation.18 | async-start | bytes 1966080 | tf_op jit(solution)/shard_map/reduce_scatter | solution.py:62
  485.6 1.4 copy-start.2
  485.6 227.6 %all-reduce.8.cloned.1.call-start = ((), (), s32[]{:S(2)}) async-start(), calls=%async_computation.19 | async-start | bytes 13762560 | tf_op jit(solution)/shard_map/psum | solution.py:333
  487.0 3.1 copy-start.8
  487.0 3.1 copy-start.46
  490.1 2.0 copy-start.14
  490.1 3.1 copy-start.11
  490.1 3.1 copy-start.18
  521.0 2.3 copy-start.15
  521.0 2.3 copy-start.32
  521.0 2.4 copy-start.9
  522.1 1.3 copy-start.4
  523.4 1.1 copy-start.33
  524.5 53.9 %copy-start.43 = (s32[4]{0:T(128)S(1)}, s32[4]{0:T(128)}, u32[]{:S(2)}) copy-start(s32[4]{0:T(128)} %param.18) | copy-start | bytes 52
  584.9 1.9 copy-start.12
  586.6 1.0 copy-start.10
  586.6 19.4 %copy-start.16 = (f32[256,384]{1,0:T(8,128)S(1)}, f32[256,384]{1,0:T(8,128)}, u32[]{:S(2)}) copy-start(f32[256,384]{1,0:T(8,128)} %get-tuple-element.43) | copy-start | bytes 1179652
  713.2 2.2 copy-start.37
  713.2 3.1 copy-start.20
  716.3 1.8 copy-start.36
  718.1 1.1 copy-start.40
  718.1 1.8 copy-start.35
  719.2 1.7 copy-start.34
  (11 other events, 8.8 us)
Sparse Core Ops, SparseCore 0:
  75.2 34.4 reduce-scatter.8
  123.4 35.2 reduce-scatter.10
  187.8 42.7 reduce-scatter.12
  232.7 43.3 reduce-scatter.16
  280.5 27.1 all-gather.5
  309.7 27.2 all-gather.3
  340.0 35.2 reduce-scatter.18
  377.7 34.2 reduce-scatter.14
  434.1 16.6 reduce-scatter.20
  459.4 22.7 all-gather.7
  485.7 35.2 reduce-scatter.22
  585.0 128.1 all-reduce.7
where the time goes:
time: 730 us; the launch traced here: 729 us
  waiting for transfers between devices  423 us (58%)
  blocking collectives  196 us (27%)
  matrix products  45.6 us (6%)
  other arithmetic  24.3 us (3%)
  local copies, waits for them, and re-layouts  23.9 us (3%)
  between operations  14.8 us (2%)
    reduce_scatter x4, waiting for transfers between devices, col_project(): lax.psum_scatter(lax.dot_general(gathered, weight, (((1,), (contract_dim,...  126 us
    reduce_scatter x4, waiting for transfers between devices, row_project(): lax.psum_scatter(lax.dot_general(gathered, block, (((1,), (contract_dim,)...  116 us
    psum x1, waiting for transfers between devices, body(): lax.psum((grad_class, grad_step, grad_weight_ada, grad_bias_ada, stacked[...  105 us
    all_gather x3, waiting for transfers between devices, gather_tokens(): return lax.all_gather(local_rows, 'row', axis=0, tiled=True)  75.2 us
    all_gather x4, blocking collectives, gather_width(): return lax.all_gather(local_rows, 'col', axis=0, tiled=True)  68.6 us
    psum x1, blocking collectives, body(): dcond_act = lax.psum(dcond_placed, ('row', 'col'))  34.5 us
    psum x1, blocking collectives, body(): condition = lax.psum(partial_cond, 'col')  20.4 us
    unnamed x107, local copies, waits for them, and re-layouts  19.9 us
  transfers between devices with their start and end apart: 12, of which 12 were waited for; matrix products, arithmetic and copies ran while one was open for 4% of the time, Pallas kernels for 0%

commit v1 on v0

v1 whole, which is shorter than its diff:
```python
import jax
import jax.numpy as jnp
from jax import lax
from jax.experimental import pallas as pl
from jax.experimental.pallas import tpu as pltpu
from jax.sharding import PartitionSpec as P

HEAD_DIM = 64
LENGTH = 256
PRECISE = lax.Precision.HIGHEST
NORM_EPSILON = 1e-06
F32 = jnp.float32
BF16 = jnp.bfloat16
ALL = ("dp", "row", "col")
GELU_A = 0.7978845608028654
GELU_B = 0.044715

COL_OF = (0, 3, 1, 2)
DP_OF = (0, 2, 3, 1)
ROUND_ONE = ((0, 2), (3, 1), (1, 3), (2, 0))
ROUND_TWO = (((0, 1), (2, 3)), ((3, 2), (1, 0)), ((1, 0), (3, 2)), ((2, 3), (0, 1)))


def dot(left, right):
    return lax.dot_general(left, right, (((1,), (0,)), ((), ())), preferred_element_type=F32)


def dot_t(left, right):
    return lax.dot_general(left, right, (((1,), (1,)), ((), ())), preferred_element_type=F32)


def t_dot(left, right):
    return lax.dot_general(left, right, (((0,), (0,)), ((), ())), preferred_element_type=F32)


def call(kernel, outs, *args, flops=0):
    total = sum(a.size * a.dtype.itemsize for a in args)
    total += sum(s[0][0] * 4 for s in outs)
    return pl.pallas_call(
        kernel,
        out_shape=[jax.ShapeDtypeStruct(shape, dtype) for shape, dtype in outs],
        compiler_params=pltpu.CompilerParams(vmem_limit_bytes=24 * 1024 * 1024),
        cost_estimate=pl.CostEstimate(flops=flops, bytes_accessed=total, transcendentals=0),
    )(*args)


def layer_norm(values):
    center = values - jnp.mean(values, axis=1, keepdims=True)
    inverse = lax.rsqrt(jnp.mean(center * center, axis=1, keepdims=True) + NORM_EPSILON)
    return center * inverse, inverse


def norm_back(grad, normed, inverse):
    return inverse * (
        grad
        - jnp.mean(grad, axis=1, keepdims=True)
        - normed * jnp.mean(grad * normed, axis=1, keepdims=True)
    )


def pick(index, values):
    chosen = jnp.int32(values[0])
    for at, value in enumerate(values[1:], 1):
        chosen = jnp.where(index == at, jnp.int32(value), chosen)
    return chosen


def after(value, *earlier):
    return lax.optimization_barrier((value,) + earlier)[0]


def column_sum(values):
    return jnp.sum(values, axis=0, keepdims=True)


def first_kernel(tokens_ref, mod_ref, out_ref):
    normed, _ = layer_norm(tokens_ref[0].astype(F32))
    out_ref[0] = (normed * (1.0 + mod_ref[1:2, :]) + mod_ref[0:1, :]).astype(BF16)
    out_ref[1] = (mod_ref[5:6, :] * tokens_ref[1].astype(F32)).astype(BF16)


def store_split(keep_ref, send_ref, which, first, second):
    rows, half = first.shape[0] // 2, first.shape[1]
    keep_ref[which, :, :half] = first[:rows]
    keep_ref[which, :, half:] = second[:rows]
    send_ref[which, :, :half] = first[rows:].astype(BF16)
    send_ref[which, :, half:] = second[rows:].astype(BF16)


def unfold(w):
    width = w.shape[1] // 3
    half, cut = 2 * width, 2 * width // 3
    top = jnp.concatenate([w[half : half + cut, :width], w[half : half + cut, width : 2 * width]], axis=1)
    low = w[half : half + cut, 2 * width :]
    low = jnp.concatenate([low[: cut // 2], low[cut // 2 :]], axis=1)
    return jnp.concatenate([top, low], axis=0)


def attention_kernel(a0, a1, b0, b1, wm, wo, hid_ref, dm_ref, oqkv_ref, p_ref, keep_ref, send_ref):
    width = wm.shape[1] // 3
    half = 2 * width
    cut = 2 * width // 3
    heads = width // HEAD_DIM
    bias = wm[half + cut : half + cut + 1, :].astype(F32)
    outm, outo = unfold(wm), unfold(wo)
    for which, (first, second) in enumerate(((a0, a1), (b0, b1))):
        rows = slice(which * LENGTH, (which + 1) * LENGTH)
        hidden = jnp.concatenate([first[0], second[0]], axis=0)
        hid_ref[rows, :] = hidden
        dm_ref[rows, :] = jnp.concatenate([first[1], second[1]], axis=0)
        qkv = (dot(hidden[:, :half], wm[:half, :]) + dot(hidden[:, half:], wo[:half, :]) + bias).astype(BF16)
        parts = []
        for head in range(heads):
            at = head * HEAD_DIM
            q = qkv[:, at : at + HEAD_DIM]
            k = qkv[:, width + at : width + at + HEAD_DIM]
            v = qkv[:, 2 * width + at : 2 * width + at + HEAD_DIM]
            scores = dot_t(q, k) * HEAD_DIM ** (-0.5)
            powers = jnp.exp(scores - jnp.max(scores, axis=1, keepdims=True))
            soft = powers * (1.0 / jnp.sum(powers, axis=1, keepdims=True))
            p_ref[which * heads + head] = soft
            parts.append(dot(soft.astype(BF16), v))
        attended = jnp.concatenate(parts, axis=1).astype(BF16)
        oqkv_ref[rows, :] = jnp.concatenate([attended, qkv], axis=1)
        store_split(keep_ref, send_ref, which, dot(attended, outm), dot(attended, outo))


def second_norm_kernel(keep, recv, recv_x, x_ref, mod_ref, a_ref, x1_ref, h_ref):
    branch = keep[0] + recv[0].astype(F32) + recv_x[...].astype(F32) + mod_ref[6:7, :]
    middle = x_ref[0].astype(F32) + mod_ref[2:3, :] * branch
    normed, _ = layer_norm(middle)
    a_ref[...] = branch
    x1_ref[...] = middle
    h_ref[...] = (normed * (1.0 + mod_ref[4:5, :]) + mod_ref[3:4, :]).astype(BF16)


def mlp_kernel(a0, a1, b0, b1, dm_ref, wm, wo, keep_ref, send_ref, mkeep, msend, gkeep, gsend):
    half = wm.shape[1]
    hid = 2 * half
    bias = jnp.concatenate([wm[2 * hid : 2 * hid + 1, :], wm[2 * hid + 1 : 2 * hid + 2, :]], axis=1)
    bias = bias.astype(F32)
    hiddens, acts, dups = [], [], []
    for which, (first, second) in enumerate(((a0, a1), (b0, b1))):
        rows = slice(which * LENGTH, (which + 1) * LENGTH)
        hidden = jnp.concatenate([first[...], second[...]], axis=0)
        up = [
            dot(hidden[:, :half], wm[s : s + half, :]) + dot(hidden[:, half:], wo[s : s + half, :])
            for s in (0, half)
        ]
        up = jnp.concatenate(up, axis=1) + bias
        square = up * up
        tanh = jnp.tanh(GELU_A * (up + GELU_B * up * square))
        act = (0.5 * up * (1.0 + tanh)).astype(BF16)
        slope = 0.5 * (1.0 + tanh) + 0.5 * up * (1.0 - tanh * tanh) * (
            GELU_A * (1.0 + 3.0 * GELU_B * square)
        )
        dm = dm_ref[rows, :]
        dg = dot_t(dm[:, :half], wm[hid : 2 * hid, :]) + dot_t(dm[:, half:], wo[hid : 2 * hid, :])
        du = (dg * slope).astype(BF16)
        back = [
            dot_t(du[:, :half], w[:half, :]) + dot_t(du[:, half:], w[half:hid, :])
            for w in (wm, wo)
        ]
        store_split(keep_ref, send_ref, which, back[0], back[1])
        store_split(mkeep, msend, which, dot(act, wm[hid : 2 * hid, :]), dot(act, wo[hid : 2 * hid, :]))
        hiddens.append(hidden)
        acts.append(act)
        dups.append(du)
    hidden, act, du = (jnp.concatenate(v, axis=0) for v in (hiddens, acts, dups))
    dm = dm_ref[...]
    for s in (0, half):
        gsend[s : s + half, :] = t_dot(hidden[:, half:], du[:, s : s + half]).astype(BF16)
        gkeep[s : s + half, :] = t_dot(hidden[:, :half], du[:, s : s + half])
    gsend[hid : 2 * hid, :] = t_dot(act, dm[:, half:]).astype(BF16)
    gkeep[hid : 2 * hid, :] = t_dot(act, dm[:, :half])
    bias = column_sum(du.astype(F32))
    bias = jnp.concatenate([bias[:, :half], bias[:, half:], jnp.zeros((14, half), F32)], axis=0)
    gkeep[2 * hid : 2 * hid + 16, :] = bias
    gsend[2 * hid : 2 * hid + 16, :] = bias.astype(BF16)


def second_back_kernel(keep, recv, recv_x, x1_ref, a_ref, ct_ref, dm_ref, mod_ref, da_ref, dx1_ref, sums_ref):
    dh = keep[0] + recv[0].astype(F32) + recv_x[...].astype(F32)
    normed, inverse = layer_norm(x1_ref[...])
    dx1 = ct_ref[1].astype(F32) + norm_back(dh * (1.0 + mod_ref[4:5, :]), normed, inverse)
    da = (mod_ref[2:3, :] * dx1).astype(BF16)
    dx1_ref[...] = dx1
    da_ref[...] = da
    sums_ref[0:1, :] = column_sum(dx1 * a_ref[...])
    sums_ref[1:2, :] = column_sum(dh)
    sums_ref[2:3, :] = column_sum(dh * normed)
    sums_ref[3:4, :] = column_sum(dm_ref[1].astype(F32))
    sums_ref[4:5, :] = column_sum(da.astype(F32))
    sums_ref[5:8, :] = jnp.zeros((3, sums_ref.shape[1]), F32)


def attention_back_kernel(
    hid_ref, da0, da1, db0, db1, oqkv_ref, p_ref, wm, wo, keep_ref, send_ref, gkeep, gsend
):
    width = wm.shape[1] // 3
    half = 2 * width
    cut = 2 * width // 3
    outm, outo = unfold(wm), unfold(wo)
    heads = width // HEAD_DIM
    scale = HEAD_DIM ** (-0.5)
    das, dqkvs = [], []
    for which, (first, second) in enumerate(((da0, da1), (db0, db1))):
        rows = slice(which * LENGTH, (which + 1) * LENGTH)
        da = jnp.concatenate([first[...], second[...]], axis=0)
        do = (dot_t(da[:, :half], outm) + dot_t(da[:, half:], outo)).astype(BF16)
        qkv = oqkv_ref[rows, width:]
        dqs, dks, dvs = [], [], []
        for head in range(heads):
            at = head * HEAD_DIM
            q = qkv[:, at : at + HEAD_DIM]
            k = qkv[:, width + at : width + at + HEAD_DIM]
            v = qkv[:, 2 * width + at : 2 * width + at + HEAD_DIM]
            do_head = do[:, at : at + HEAD_DIM]
            soft = p_ref[which * heads + head]
            dsoft = dot_t(do_head, v)
            ds = (soft * (dsoft - jnp.sum(soft * dsoft, axis=1, keepdims=True))).astype(BF16)
            dqs.append(dot(ds, k) * scale)
            dks.append(t_dot(ds, q) * scale)
            dvs.append(t_dot(soft.astype(BF16), do_head))
        dqkv = jnp.concatenate(dqs + dks + dvs, axis=1).astype(BF16)
        store_split(keep_ref, send_ref, which, dot_t(dqkv, wm[:half, :]), dot_t(dqkv, wo[:half, :]))
        das.append(da)
        dqkvs.append(dqkv)
    hidden = hid_ref[...]
    da = jnp.concatenate(das, axis=0)
    dqkv = jnp.concatenate(dqkvs, axis=0)
    o = oqkv_ref[:, :width]
    bias = jnp.pad(column_sum(dqkv.astype(F32)), ((0, 15), (0, 0)))
    for ref, side in ((gkeep, slice(0, half)), (gsend, slice(half, 2 * half))):
        ref[:half, :] = t_dot(hidden[:, side], dqkv).astype(ref.dtype)
        out = t_dot(o, da[:, side])
        low = jnp.concatenate([out[cut:, :width], out[cut:, width:]], axis=0)
        ref[half : half + cut, :] = jnp.concatenate(
            [out[:cut, :width], out[:cut, width:], low], axis=1
        ).astype(ref.dtype)
        ref[half + cut : half + cut + 16, :] = bias.astype(ref.dtype)


def last_kernel(
    keep, recv, recv_x, x_ref, dx1_ref, mod_ref, x1_ref, mkeep, mrecv, mrecv_x, two_ref, out_ref, sums_ref
):
    dh = keep[0] + recv[0].astype(F32) + recv_x[...].astype(F32)
    normed, inverse = layer_norm(x_ref[0].astype(F32))
    dx = dx1_ref[...] + norm_back(dh * (1.0 + mod_ref[1:2, :]), normed, inverse)
    branch = mkeep[0] + mrecv[0].astype(F32) + mrecv_x[...].astype(F32) + mod_ref[7:8, :]
    out_ref[0] = (x1_ref[...] + mod_ref[5:6, :] * branch).astype(BF16)
    out_ref[1] = dx.astype(BF16)
    sums_ref[0:1, :] = column_sum(dh)
    sums_ref[1:2, :] = column_sum(dh * normed)
    sums_ref[2:5, :] = two_ref[0:3, :]
    sums_ref[5:6, :] = column_sum(x_ref[1].astype(F32) * branch)
    sums_ref[6:8, :] = two_ref[3:5, :]


def make_body(n_dp, n_row, n_col):
    def flat(d, r, c):
        return (d * n_row + r) * n_col + c

    places = [(d, r, c) for d in range(n_dp) for r in range(n_row) for c in range(n_col)]

    def core_swap(v):
        return lax.ppermute(v, "dp", [(d, d ^ 1) for d in range(n_dp)])

    def chip_swap(v):
        return lax.ppermute(v, "dp", [(d, d ^ 2) for d in range(n_dp)])

    def row_swap(v):
        return lax.ppermute(v, "row", [(0, 1), (1, 0)])

    def shift(v, k):
        return lax.ppermute(v, "col", [(c, (c + k) % n_col) for c in range(n_col)])

    def col_swap(v, bit):
        return lax.ppermute(v, "col", [(c, c ^ bit) for c in range(n_col)])

    def spread(own):
        far = chip_swap(own)
        return (own, core_swap(own), far, core_swap(far))

    def gather_sum(keep, send):
        recv = core_swap(send)
        far = chip_swap((keep[1] + recv[1].astype(F32)).astype(BF16))
        return keep, recv, far

    def body(
        latents,
        labels,
        step_ids,
        class_table,
        step_table,
        w_ada,
        b_ada,
        w_qkv,
        b_qkv,
        w_out,
        b_out,
        w_up,
        b_up,
        w_down,
        b_down,
        cotangent,
    ):
        tokens, width_row = latents.shape
        per_block = tokens // LENGTH
        sequences = labels.shape[0]
        width = class_table.shape[1]
        half = width // 2
        cols = w_qkv.shape[3]
        hid = w_up.shape[2]
        cond_cols = w_ada.shape[1]
        quick = n_row == 2 and per_block == 1
        dp_at = lax.axis_index("dp")
        row_at = lax.axis_index("row")
        col_at = lax.axis_index("col")
        core_at = dp_at % 2
        owner = core_at == row_at % 2
        block = LENGTH // 2

        def gather_owner(own, other):
            across = lax.ppermute(
                own, ALL, [(flat(d, r, c), flat(d, 1 - r, c)) for d, r, c in places if d % 2 != r]
            )
            across_core = lax.ppermute(
                other, ALL, [(flat(d, r, c), flat(d ^ 1, 1 - r, c)) for d, r, c in places if d % 2 != r]
            )
            core = lax.ppermute(
                other, ALL, [(flat(d, r, c), flat(d ^ 1, r, c)) for d, r, c in places if d % 2 == r]
            )
            return jnp.concatenate(
                [jnp.where(owner, own, core), jnp.where(owner, across, across_core)], axis=-1
            )

        def tokens_in(v):
            if quick:
                own = lax.dynamic_slice_in_dim(v, core_at * block, block, 1)
                other = lax.dynamic_slice_in_dim(v, (1 - core_at) * block, block, 1)
                return gather_owner(own, other)
            full = lax.all_gather(v, "row", axis=2, tiled=True)
            full = jnp.where(owner, full, core_swap(full))
            return lax.dynamic_slice_in_dim(full, (row_at // 2) * LENGTH + core_at * block, block, 1)

        def tokens_out(v):
            if quick:
                mine, theirs = v[:, :, :half], v[:, :, half:]
                core = lax.ppermute(
                    mine, ALL, [(flat(d, r, c), flat(d ^ 1, r, c)) for d, r, c in places if d % 2 != r]
                )
                across = lax.ppermute(
                    theirs, ALL, [(flat(d, r, c), flat(d, 1 - r, c)) for d, r, c in places if d % 2 == r]
                )
                across_core = lax.ppermute(
                    theirs, ALL, [(flat(d, r, c), flat(d ^ 1, 1 - r, c)) for d, r, c in places if d % 2 != r]
                )
                first = jnp.where(owner, mine, across)
                second = jnp.where(owner, core, across_core)
                return jnp.where(
                    core_at == 0,
                    jnp.concatenate([first, second], axis=1),
                    jnp.concatenate([second, first], axis=1),
                )
            other = lax.ppermute(
                v, ALL, [(flat(d, r, c), flat(d ^ 1, r, c)) for d, r, c in places if d % 2 != r % 2]
            )
            full = jnp.where(
                core_at == 0, jnp.concatenate([v, other], axis=1), jnp.concatenate([other, v], axis=1)
            )
            rows = lax.all_gather(full, "row", axis=1)
            rows = rows.reshape(2, n_row // 2, 2, LENGTH, width)
            rows = lax.dynamic_index_in_dim(rows, core_at, 2, keepdims=False)
            rows = rows.reshape(2, tokens, width)
            return lax.dynamic_slice_in_dim(rows, row_at * width_row, width_row, 2)

        def first_round(v):
            return lax.ppermute(
                v,
                ALL,
                [
                    (flat(d, r, ROUND_ONE[d][0]), flat(d, r, ROUND_ONE[d][1]))
                    for d in range(n_dp)
                    for r in range(n_row)
                ],
            )

        def pack_attention(w, out):
            bias = jnp.concatenate([b_qkv[0, 0], jnp.zeros((cols,), BF16), b_qkv[0, 1]])
            cut = 2 * cols // 3
            folded = jnp.concatenate(
                [out[:cut, :cols], out[:cut, cols:], jnp.concatenate([out[cut:, :cols], out[cut:, cols:]], axis=0)],
                axis=1,
            )
            return jnp.concatenate([w, folded, jnp.pad(bias[None], ((0, 15), (0, 0)))], axis=0)

        source = pick(dp_at, COL_OF)
        relay = pick(dp_at, [pair[1] for pair in ROUND_ONE])
        at_source = col_at == source
        at_relay = col_at == relay

        def second_round(held):
            return lax.ppermute(
                held,
                ALL,
                [
                    (flat(d, r, a), flat(d, r, b))
                    for d in range(n_dp)
                    for r in range(n_row)
                    for a, b in ROUND_TWO[d]
                ],
            )

        def settle(held, second):
            return jnp.where(at_source | at_relay, held, second)

        if quick:
            own_att = pack_attention(w_qkv[0].reshape(width_row, 3 * cols), w_out[0])
            att_first = first_round(own_att)
            labels = after(labels, own_att)
        class_rows = class_table.shape[0]
        step_rows = step_table.shape[0]

        def hot(ids, rows):
            return ids[:, None] == (col_at * rows + jnp.arange(rows, dtype=jnp.int32))[None, :]

        partial_cond = dot(hot(labels, class_rows).astype(BF16), class_table) + dot(
            hot(step_ids, step_rows).astype(BF16), step_table
        )
        ada = w_ada[0].reshape(cond_cols, 6 * width_row).astype(F32)
        small_bias = jnp.concatenate([b_ada[0], b_out, b_down], axis=0).astype(F32)
        if quick:
            condition = (partial_cond + shift(partial_cond, 1)) + (
                shift(partial_cond, 2) + shift(partial_cond, 3)
            )
        else:
            condition = lax.psum(partial_cond, "col")
        cond_part = lax.dynamic_slice_in_dim(condition, col_at * cond_cols, cond_cols, 1)
        act_part = cond_part * jax.nn.sigmoid(cond_part)
        if quick:
            att_held = jnp.where(at_source, own_att, att_first)
            act_part = after(act_part, att_held)
            att_second = second_round(att_held)
        mod_part = jnp.dot(act_part, ada, precision=PRECISE)
        if quick:
            twice = jnp.concatenate([mod_part, mod_part], axis=0)
            turned = lax.dynamic_slice_in_dim(twice, col_at, n_col, 0)
            modulation = turned[0] + shift(turned[1], 1) + shift(turned[2], 2) + shift(turned[3], 3)
            modulation = modulation.reshape(6, width_row)
            mod_sum = modulation
            modulation = jnp.concatenate([modulation, jnp.zeros((2, width_row), F32)], axis=0)
            modulation = modulation + small_bias
            modulation = gather_owner(modulation, modulation)
        else:
            all_mod = lax.psum(mod_part, "col").reshape(sequences, 6, width_row)
            all_mod = jnp.concatenate([all_mod, jnp.zeros((sequences, 2, width_row), F32)], axis=1)
            all_mod = lax.all_gather(all_mod + small_bias[None], "row", axis=2, tiled=True)
            all_mod = jnp.where(owner, all_mod, core_swap(all_mod))
            modulation = lax.dynamic_index_in_dim(
                all_mod, col_at * per_block + row_at // 2, 0, keepdims=False
            )

        def pack_mlp(up, down):
            bias = jnp.pad(b_up.reshape(2, half), ((0, 14), (0, 0)))
            return jnp.concatenate([up[:, :half], up[:, half:], down, bias], axis=0)

        own_tokens = tokens_in(jnp.stack([latents, cotangent]))
        if quick:
            own_mlp = after(pack_mlp(w_up[0], w_down[0]), mod_sum)
            mlp_first = first_round(own_mlp)
            att_m = settle(att_held, att_second)
            modulation = after(modulation, att_m)
            att_o = row_swap(att_m)
        else:

            def fetch_whole(halves):
                taken = [
                    lax.dynamic_index_in_dim(lax.all_gather(v, "col"), source, 0, keepdims=False)
                    for v in halves
                ]
                return taken[0], taken[1]

            full_qkv = lax.all_gather(w_qkv[0].reshape(width_row, 3 * cols), "row", axis=0, tiled=True)
            full_out = lax.all_gather(w_out[0], "row", axis=1, tiled=True)
            full_up = lax.all_gather(w_up[0], "row", axis=0, tiled=True)
            full_down = lax.all_gather(w_down[0], "row", axis=1, tiled=True)
            att_m, att_o = fetch_whole(
                [pack_attention(full_qkv[:half], full_out[:, :half]), pack_attention(full_qkv[half:], full_out[:, half:])]
            )
            mlp_m, mlp_o = fetch_whole(
                [pack_mlp(full_up[:half], full_down[:, :half]), pack_mlp(full_up[half:], full_down[:, half:])]
            )

        heads = cols // HEAD_DIM
        shard = (block, width)
        pair = (2, block, width)
        both = 2 * LENGTH
        (first_own,) = call(first_kernel, [(pair, BF16)], own_tokens, modulation)
        first_all = spread(first_own)
        if quick:
            mlp_held = jnp.where(at_source, own_mlp, after(mlp_first, first_own))
            first_all = first_all[:3] + (after(first_all[3], mlp_held),)
            mlp_second = second_round(mlp_held)
        hidden_all, dm_all, oqkv, soft, keep, send = call(
            attention_kernel,
            [
                ((both, width), BF16),
                ((both, width), BF16),
                ((both, 4 * cols), BF16),
                ((2 * heads, LENGTH, LENGTH), F32),
                (pair, F32),
                (pair, BF16),
            ],
            *first_all,
            att_m,
            att_o,
            flops=2 * both * width * 4 * cols,
        )
        if quick:
            mlp_m = settle(mlp_held, after(mlp_second, first_all[3]))
            send = after(send, mlp_m)
            mlp_o = row_swap(mlp_m)
        branch_one, middle, hm_own = call(
            second_norm_kernel,
            [(shard, F32), (shard, F32), (shard, BF16)],
            *gather_sum(keep, send),
            own_tokens,
            modulation,
        )
        hm_all = spread(hm_own)

        def collect_one(keep, recv):
            total = keep + recv.astype(F32)
            return total, lax.ppermute(
                total.astype(BF16),
                ALL,
                [
                    (flat(d, r, b), flat(d, r, a))
                    for d in range(n_dp)
                    for r in range(n_row)
                    for a, b in ROUND_TWO[d]
                ],
            )

        def collect_two(total, recv):
            total = total + recv.astype(F32)
            return total, lax.ppermute(
                total.astype(BF16),
                ALL,
                [
                    (flat(d, r, ROUND_ONE[d][1]), flat(d, r, ROUND_ONE[d][0]))
                    for d in range(n_dp)
                    for r in range(n_row)
                ],
            )

        home = (pick(col_at, DP_OF) // 2) == (dp_at // 2)

        def collect_three(total, recv):
            total = (total + recv.astype(F32)).astype(BF16)
            return total, lax.ppermute(
                total,
                ALL,
                [
                    (flat(DP_OF[c], r, c), flat(DP_OF[c] ^ 2, r, c))
                    for r in range(n_row)
                    for c in range(n_col)
                ],
            )

        def collect_last(total, far):
            total = jnp.where(at_source, total, far)
            near = lax.ppermute(
                total,
                ALL,
                [
                    (flat(d, r, c), flat(d ^ 1, r, c))
                    for r in range(n_row)
                    for c in range(n_col)
                    for d in (DP_OF[c], DP_OF[c] ^ 2)
                ],
            )
            return jnp.where((dp_at % 2) == pick(col_at, DP_OF) % 2, total, near).astype(F32)

        n_mlp = 2 * hid + 16
        keep, send, mkeep, msend, mlp_keep, mlp_send = call(
            mlp_kernel,
            [
                (pair, F32),
                (pair, BF16),
                (pair, F32),
                (pair, BF16),
                ((n_mlp, half), F32),
                ((n_mlp, half), BF16),
            ],
            *hm_all,
            dm_all,
            mlp_m,
            mlp_o,
            flops=12 * both * width * hid,
        )
        hidden_sum = gather_sum(keep, send)
        da_own, dmiddle, sums_two = call(
            second_back_kernel,
            [(shard, BF16), (shard, F32), ((8, width), F32)],
            *hidden_sum,
            middle,
            branch_one,
            own_tokens,
            first_own,
            modulation,
        )
        da_all = spread(da_own)
        if quick:
            mlp_parts = collect_one(mlp_keep, after(row_swap(mlp_send), da_own))
            da_all = da_all[:3] + (after(da_all[3], mlp_parts[0]),)
        branch_sum = gather_sum(mkeep, after(msend, da_own))
        n_att = att_m.shape[0]
        keep, send, att_keep, att_send = call(
            attention_back_kernel,
            [(pair, F32), (pair, BF16), ((n_att, 3 * cols), F32), ((n_att, 3 * cols), BF16)],
            hidden_all,
            *da_all,
            oqkv,
            soft,
            att_m,
            att_o,
            flops=4 * both * width * 4 * cols,
        )
        input_sum = gather_sum(keep, send)
        if quick:
            mlp_parts = collect_two(mlp_parts[0], after(mlp_parts[1], send))
            input_sum = input_sum[:2] + (after(input_sum[2], mlp_parts[0]),)
            att_recv = row_swap(att_send)
        results, sums = call(
            last_kernel,
            [(pair, BF16), ((8, width), F32)],
            *input_sum,
            own_tokens,
            dmiddle,
            modulation,
            middle,
            *branch_sum,
            sums_two,
        )

        results = tokens_out(results)

        ids = jnp.stack([labels, step_ids], axis=1).astype(F32)
        if quick:
            small = jnp.concatenate([cond_part, ids], axis=1)
            near = core_swap(small)
            small = jnp.where(owner, jnp.stack([small, near]), jnp.stack([near, small]))
            small = jnp.stack([small, chip_swap(small)], axis=1).reshape(2, 2, 2, 2, cond_cols + 2)
            small = jnp.where(col_at % 2 == 1, small[:, :, :, ::-1], small)
            small = jnp.where(col_at >= 2, small[:, :, ::-1], small)
            small = small.transpose(2, 3, 0, 1, 4).reshape(n_dp * n_col, cond_cols + 2)
            all_cond = small[:, :cond_cols]
            all_ids = small[:, cond_cols:]
            sums = sums + core_swap(sums)
            far = chip_swap(sums)
            att_parts = collect_one(att_keep, after(att_recv, sums))
            far = after(far, att_parts[0])
            theirs = row_swap(jnp.concatenate([sums[:, half:], far[:, half:]], axis=0))
            mlp_parts = collect_three(mlp_parts[0], after(mlp_parts[1], far))
            theirs = after(theirs, mlp_parts[0])
            whole = jnp.concatenate([sums[:, :half], far[:, :half], theirs], axis=0)
            whole = jnp.concatenate([whole, col_swap(whole, 1)], axis=0)
            att_parts = collect_two(att_parts[0], after(att_parts[1], whole))
            whole = after(whole, att_parts[0])
            whole = [whole, col_swap(whole, 2)]
            dmod = jnp.concatenate(whole, axis=0).reshape(n_dp * n_col, 8, half)
        else:
            every = lax.all_gather(sums, ALL).reshape(2, 2, n_row // 2, 2, n_col, 8, width)
            every = jnp.sum(every, axis=1).transpose(0, 2, 3, 1, 4, 5)
            every = every.reshape(n_dp * sequences, 8, width)
            dmod = lax.dynamic_slice_in_dim(every, row_at * width_row, width_row, 2)
            all_cond = lax.all_gather(cond_part, "dp", axis=0, tiled=True)
            all_ids = lax.all_gather(ids, "dp", axis=0, tiled=True)

        gate = jax.nn.sigmoid(all_cond)
        all_act = all_cond * gate
        slope = gate * (1.0 + all_cond * (1.0 - gate))
        dmod_six = dmod[:, :6].reshape(-1, 6 * width_row)
        grad_ada = lax.dot_general(
            all_act, dmod_six, (((0,), (0,)), ((), ())), precision=PRECISE
        ).reshape(1, cond_cols, 6, width_row)
        totals = jnp.sum(dmod, axis=0)
        dact = lax.dot_general(dmod_six, ada, (((1,), (1,)), ((), ())), precision=PRECISE)
        if quick:
            flipped = row_swap(dact).reshape(n_col, 2, 2, cond_cols)[:, ::-1]
            att_parts = collect_three(att_parts[0], after(att_parts[1], dact))
            flipped = after(flipped, att_parts[0])
            dcond = slope * (dact + flipped.reshape(-1, cond_cols))
            dcond = dcond.reshape(n_col, n_dp, cond_cols)
            near = col_swap(dcond, 1)
            dcond = jnp.stack([dcond, near[jnp.array([1, 0, 3, 2])]])
            far = col_swap(dcond, 2)[:, jnp.array([2, 3, 0, 1])]
            around = jnp.stack([dcond, far])
            around = jnp.where(col_at % 2 == 1, around[:, ::-1], around)
            around = jnp.where(col_at >= 2, around[::-1], around)
            around = around.reshape(n_col, n_col, n_dp, cond_cols)
            dcond = around.transpose(1, 2, 0, 3).reshape(-1, width)
        else:
            dcond = slope * lax.psum(dact, "row")
            dcond = lax.all_gather(dcond, "col", axis=1, tiled=True)
        all_ids = all_ids.astype(jnp.int32)
        grad_class = lax.dot_general(
            hot(all_ids[:, 0], class_rows).astype(F32), dcond, (((0,), (0,)), ((), ())), precision=PRECISE
        )
        grad_step = lax.dot_general(
            hot(all_ids[:, 1], step_rows).astype(F32), dcond, (((0,), (0,)), ((), ())), precision=PRECISE
        )

        if quick:
            grad_mlp = collect_last(*mlp_parts)
            grad_att = collect_last(*att_parts)
        else:

            def collect_whole(keep, send):
                full = lax.psum(jnp.stack([keep, send.astype(F32)]), ("row", "col"))
                full = lax.all_gather(full, "dp")
                full = jnp.stack([full[d] for d in DP_OF])
                return lax.dynamic_index_in_dim(full, col_at, 0, keepdims=False)

            grad_mlp = collect_whole(mlp_keep, mlp_send)
            grad_att = collect_whole(att_keep, att_send)

        cut = 2 * cols // 3

        def take(v, dim):
            return lax.dynamic_slice_in_dim(v, row_at * width_row, width_row, dim)

        def split_attention(v):
            out = jnp.concatenate([v[half : half + cut, :cols], v[half : half + cut, cols : 2 * cols]], axis=1)
            low = v[half : half + cut, 2 * cols :]
            low = jnp.concatenate([low[: cut // 2], low[cut // 2 :]], axis=1)
            return v[:half], jnp.concatenate([out, low], axis=0)

        def split_mlp(v):
            return jnp.concatenate([v[:half], v[half:hid]], axis=1), v[hid : 2 * hid]

        if quick:
            grad_qkv, grad_out = split_attention(grad_att)
            grad_up, grad_down = split_mlp(grad_mlp)
            bias_att, bias_mlp = grad_att[half + cut], grad_mlp[2 * hid : 2 * hid + 2]
        else:
            first, second = split_attention(grad_att[0]), split_attention(grad_att[1])
            grad_qkv = take(jnp.concatenate([first[0], second[0]], axis=0), 0)
            grad_out = take(jnp.concatenate([first[1], second[1]], axis=1), 1)
            first, second = split_mlp(grad_mlp[0]), split_mlp(grad_mlp[1])
            grad_up = take(jnp.concatenate([first[0], second[0]], axis=0), 0)
            grad_down = take(jnp.concatenate([first[1], second[1]], axis=1), 1)
            bias_att, bias_mlp = grad_att[0, half + cut], grad_mlp[0, 2 * hid : 2 * hid + 2]
        grad_bias_qkv = jnp.stack([bias_att[:cols], bias_att[2 * cols :]])

        return (
            results[0],
            results[1],
            grad_class,
            grad_step,
            grad_ada,
            totals[None, :6],
            grad_qkv.reshape(1, width_row, 3, cols),
            grad_bias_qkv[None],
            grad_out[None],
            totals[None, 7],
            grad_up[None],
            bias_mlp.reshape(1, hid),
            grad_down[None],
            totals[None, 6],
        )

    return body


def solution(mesh):
    return jax.shard_map(
        make_body(mesh.shape["dp"], mesh.shape["row"], mesh.shape["col"]),
        mesh=mesh,
        in_specs=(
            P(("dp", "col"), "row"),
            P("dp"),
            P("dp"),
            P("col", None),
            P("col", None),
            P(None, "col", None, "row"),
            P(None, None, "row"),
            P(None, "row", None, "col"),
            P(None, None, "col"),
            P(None, "col", "row"),
            P(None, "row"),
            P(None, "row", "col"),
            P(None, "col"),
            P(None, "col", "row"),
            P(None, "row"),
            P(("dp", "col"), "row"),
        ),
        out_specs=(
            P(("dp", "col"), "row"),
            P(("dp", "col"), "row"),
            P("col", None),
            P("col", None),
            P(None, "col", None, "row"),
            P(None, None, "row"),
            P(None, "row", None, "col"),
            P(None, None, "col"),
            P(None, "col", "row"),
            P(None, "row"),
            P(None, "row", "col"),
            P(None, "col"),
            P(None, "col", "row"),
            P(None, "row"),
        ),
        check_vma=False,
    )
```

time: 730 us -> 262 us (0.36)
  waiting for transfers between devices: 423 us -> 98.7 us
  blocking collectives: 196 us -> 0 us
  starting transfers between devices: 0.68 us -> 83.7 us
  matrix products: 45.6 us -> 7.36 us
  Pallas kernels: 0 us -> 19.2 us
  between operations: 14.8 us -> 1.73 us
    reduce_scatter x8 -> x0, waiting for transfers between devices: 242 us -> none  [the longest x4 126 us: col_project(): lax.psum_scatter(lax.dot_general(gathered, weight, (((1,), (contract_dim,...]
    psum x9 -> x0, blocking collectives: 120 us -> none  [the longest x1 34.5 us: body(): dcond_act = lax.psum(dcond_placed, ('row', 'col'))]
    psum x1 -> x0, waiting for transfers between devices: 105 us -> none  [body(): lax.psum((grad_class, grad_step, grad_weight_ada, grad_bias_ada, stacked[...]
    ppermute x0 -> x58, waiting for transfers between devices: none -> 98.7 us  [the longest x9 26.5 us: chip_swap(): return lax.ppermute(v, 'dp', [(d, d ^ 2) for d in range(n_dp)])]
    ppermute x0 -> x58, starting transfers between devices: none -> 83.7 us  [the longest x6 14.4 us: shift(): return lax.ppermute(v, 'col', [(c, (c + k) % n_col) for c in range(n_col)])]
    all_gather x5 -> x0, blocking collectives: 75.9 us -> none  [the longest x4 68.6 us: gather_width(): return lax.all_gather(local_rows, 'col', axis=0, tiled=True)]
    all_gather x3 -> x0, waiting for transfers between devices: 75.2 us -> none  [gather_tokens(): return lax.all_gather(local_rows, 'row', axis=0, tiled=True)]
    dot_general x27 -> x7, matrix products: 45.6 us -> 7.36 us  [the longest x1 2.8 us: body(): lax.dot_general(all_act, dmod_six, (((0,), (0,)), ((), ())), precision=PR...]
  transfers between devices with their start and end apart: 12 -> 58, of which waited for: 12 -> 24; matrix products, arithmetic and copies ran while one was open for 4% -> 14% of each run, Pallas kernels for 0% -> 5%
where the time goes in v1:
time: 262 us; the launch traced here: 260 us
  waiting for transfers between devices  98.7 us (38%)
  starting transfers between devices  83.7 us (32%)
  local copies, waits for them, and re-layouts  26.3 us (10%)
  other arithmetic  22.9 us (9%)
  Pallas kernels  19.2 us (7%)
  matrix products  7.36 us (3%)
    ppermute x9, waiting for transfers between devices, chip_swap(): return lax.ppermute(v, 'dp', [(d, d ^ 2) for d in range(n_dp)])  26.5 us
    ppermute x6, waiting for transfers between devices, row_swap(): return lax.ppermute(v, 'row', [(0, 1), (1, 0)])  21.3 us
    pallas_call x7, Pallas kernels, call(): pl.pallas_call(kernel, out_shape=[jax.ShapeDtypeStruct(shape, dtype) for...  19.2 us
    ppermute x4, waiting for transfers between devices, col_swap(): return lax.ppermute(v, 'col', [(c, c ^ bit) for c in range(n_col)])  14.8 us
    ppermute x6, starting transfers between devices, shift(): return lax.ppermute(v, 'col', [(c, (c + k) % n_col) for c in range(n_col)])  14.4 us
    ppermute x2, starting transfers between devices, collect_three(): lax.ppermute(total, ALL, [(flat(DP_OF[c], r, c), flat(DP_OF[c] ^ 2, r, c)...  13.7 us
    unnamed x84, local copies, waits for them, and re-layouts  11.7 us
    ppermute x9, starting transfers between devices, chip_swap(): return lax.ppermute(v, 'dp', [(d, d ^ 2) for d in range(n_dp)])  10 us
  transfers between devices with their start and end apart: 58, of which 24 were waited for; matrix products, arithmetic and copies ran while one was open for 14% of the time, Pallas kernels for 5%

profile of v1, /device:TPU:0, one launch (start us, length us, event | category | flops | bytes accessed | tf_op | source)
XLA Modules:
  0.0 259.9 jit_solution(13031130076259226055)
XLA Ops:
  6.2 3.0 %collective-permute-start.3 = (f32[4,768]{1,0:T(4,128)S(1)}, f32[4,768]{1,0:T(4,128)S(1)}, u32[]{:S(2)}, u32[]{:S(2)}) collective-permute-start(f32[4,768]{1,0:T(4,128)S(1)} %convolution_add_fusion), channel_id=1, source_target_pairs={{0,1},{1,2},{2,3},{3,0},{4,5},{5,6},{6,7},{7,4},{8,9},{9,10},{10,1... | collective-permute-start | bytes 36872 | tf_op jit(solution)/shard_map/ppermute | solution.py:276
  9.2 2.6 collective-permute-start.4
  13.1 2.9 %collective-permute-start.6 = (bf16[528,576]{1,0:T(8,128)(2,1)}, bf16[528,576]{1,0:T(8,128)(2,1)}, u32[]{:S(2)}, u32[]{:S(2)}) collective-permute-start(bf16[528,576]{1,0:T(8,128)(2,1)} %fusion.3), channel_id=1, source_target_pairs={{0,2},{4,6},{11,9},{15,13},{17,19},{21,23},{26,24},{30,28}} | collective-permute-start | bytes 1824776 | tf_op jit(solution)/shard_map/ppermute | solution.py:379
  16.1 2.0 collective-permute-start
  21.1 2.7 %collective-permute-done.6 = bf16[528,576]{1,0:T(8,128)(2,1)} collective-permute-done((bf16[528,576]{1,0:T(8,128)(2,1)}, bf16[528,576]{1,0:T(8,128)(2,1)}, u32[]{:S(2)}, u32[]{:S(2)}) %collective-permute-start.6) | collective-permute-done | bytes 608288 | tf_op jit(solution)/shard_map/ppermute | solution.py:379
  25.5 4.5 %collective-permute-start.8 = (f32[2304]{0:T(1024)S(1)}, f32[2304]{0:T(1024)S(1)}, u32[]{:S(2)}, u32[]{:S(2)}) collective-permute-start(f32[2304]{0:T(1024)S(1)} %get-tuple-element.119), channel_id=1, source_target_pairs={{0,2},{1,3},{2,0},{3,1},{4,6},{5,7},{6,4},{7,5},{8,10},{9,11},{10,... | collective-permute-start | bytes 27656 | tf_op jit(solution)/shard_map/ppermute | solution.py:276
  30.0 2.8 %collective-permute-start.9 = (f32[2304]{0:T(1024)S(1)}, f32[2304]{0:T(1024)S(1)}, u32[]{:S(2)}, u32[]{:S(2)}) collective-permute-start(f32[2304]{0:T(1024)S(1)} %get-tuple-element.121), channel_id=1, source_target_pairs={{0,3},{1,0},{2,1},{3,2},{4,7},{5,4},{6,5},{7,6},{8,11},{9,8},{10,9... | collective-permute-start | bytes 27656 | tf_op jit(solution)/shard_map/ppermute | solution.py:276
  34.3 2.9 %collective-permute-start.17 = (bf16[1552,384]{1,0:T(8,128)(2,1)S(1)}, bf16[1552,384]{1,0:T(8,128)(2,1)S(1)}, u32[]{:S(2)}, u32[]{:S(2)}) collective-permute-start(bf16[1552,384]{1,0:T(8,128)(2,1)S(1)} %fusion.2), channel_id=1, source_target_pairs={{0,2},{4,6},{11,9},{15,13},{17,19},{21,23},{26,24},{30,28}} | collective-permute-start | bytes 3575816 | tf_op jit(solution)/shard_map/ppermute | solution.py:379
  37.3 3.3 %collective-permute-done.1 = bf16[2,128,384]{2,1,0:T(8,128)(2,1)S(1)} collective-permute-done((bf16[2,128,384]{2,1,0:T(8,128)(2,1)S(1)}, bf16[2,128,384]{2,1,0:T(8,128)(2,1)S(1)}, u32[]{:S(2)}, u32[]{:S(2)}) %collective-permute-start.1) | collective-permute-done | bytes 196640 | tf_op jit(solution)/shard_map/ppermute | solution.py:325
  45.3 3.6 %collective-permute-done.11 = f32[8,384]{1,0:T(8,128)S(1)} collective-permute-done((f32[8,384]{1,0:T(8,128)S(1)}, f32[8,384]{1,0:T(8,128)S(1)}, u32[]{:S(2)}, u32[]{:S(2)}) %collective-permute-start.11) | collective-permute-done | bytes 12320 | tf_op jit(solution)/shard_map/ppermute | solution.py:325
  48.9 9.5 %collective-permute-done.13 = bf16[528,576]{1,0:T(8,128)(2,1)S(1)} collective-permute-done((bf16[528,576]{1,0:T(8,128)(2,1)}, bf16[528,576]{1,0:T(8,128)(2,1)S(1)}, u32[]{:S(2)}, u32[]{:S(2)}) %collective-permute-start.13) | collective-permute-done | bytes 608288 | tf_op jit(solution)/shard_map/ppermute | solution.py:404
  59.9 3.4 %collective-permute-start.19 = (bf16[1552,384]{1,0:T(8,128)(2,1)S(1)}, bf16[1552,384]{1,0:T(8,128)(2,1)S(1)}, u32[]{:S(2)}, u32[]{:S(2)}) collective-permute-start(bf16[1552,384]{1,0:T(8,128)(2,1)S(1)} %broadcast_select_fusion.2), channel_id=1, source_target_pairs={{0,1},{2,3},{4,5},{6,7},{11,10},{9,8},{15,14},{13,12},{17,16},{19,... | collective-permute-start | bytes 3575816 | tf_op jit(solution)/shard_map/ppermute | solution.py:404
  63.5 1.8 collective-permute-start.18
  65.2 6.0 %collective-permute-done.15.b0 = bf16[2,128,768]{2,1,0:T(8,128)(2,1)S(1)} collective-permute-done((bf16[2,128,768]{2,1,0:T(8,128)(2,1)S(1)}, bf16[2,128,768]{2,1,0:T(8,128)(2,1)S(1)}, u32[]{:S(2)}, u32[]{:S(2)}) %collective-permute-start.15) | collective-permute-done | bytes 393248 | tf_op jit(solution)/shard_map/ppermute | solution.py:270
  74.3 2.9 %shard_map.282 = (bf16[512,768]{1,0:T(8,128)(2,1)S(1)}, bf16[512,768]{1,0:T(8,128)(2,1)S(1)}, bf16[512,768]{1,0:T(8,128)(2,1)S(1)}, f32[6,256,256]{2,1,0:T(8,128...) custom-call(bf16[2,128,768]{2,1,0:T(8,128)(2,1)S(1)} %shard_map.281.a0.dm_ref, ...), custom_call_target="tpu_custom_call" | custom-call | flops 603979776 | bytes 2795560 | tf_op jit(solution)/shard_map/pallas_call | solution.py:39
  78.9 1.7 collective-permute-start.25
  80.7 2.0 collective-permute-start.21
  82.7 5.3 %collective-permute-done.21.recv_x = bf16[128,768]{1,0:T(8,128)(2,1)S(1)} collective-permute-done((bf16[128,768]{1,0:T(8,128)(2,1)S(1)}, bf16[128,768]{1,0:T(8,128)(2,1)S(1)}, u32[]{:S(2)}, u32[]{:S(2)}) %collective-permute-start.21) | collective-permute-done | bytes 196640 | tf_op jit(solution)/shard_map/ppermute | solution.py:270
  88.3 1.8 collective-permute-start.23
  90.1 4.7 %collective-permute-done.23.b0 = bf16[128,768]{1,0:T(8,128)(2,1)S(1)} collective-permute-done((bf16[128,768]{1,0:T(8,128)(2,1)S(1)}, bf16[128,768]{1,0:T(8,128)(2,1)S(1)}, u32[]{:S(2)}, u32[]{:S(2)}) %collective-permute-start.23) | collective-permute-done | bytes 196640 | tf_op jit(solution)/shard_map/ppermute | solution.py:270
  96.3 11.3 %collective-permute-done.25.wo = bf16[1552,384]{1,0:T(8,128)(2,1)S(1)} collective-permute-done((bf16[1552,384]{1,0:T(8,128)(2,1)S(1)}, bf16[1552,384]{1,0:T(8,128)(2,1)S(1)}, u32[]{:S(2)}, u32[]{:S(2)}) %collective-permute-start.25) | collective-permute-done | bytes 1191968 | tf_op jit(solution)/shard_map/ppermute | solution.py:273
  107.6 7.2 %shard_map.284 = (f32[2,128,768]{2,1,0:T(8,128)S(1)}, bf16[2,128,768]{2,1,0:T(8,128)(2,1)S(1)}, f32[2,128,768]{2,1,0:T(8,128)S(1)}, bf16[2,128,768]{2,1,0:T(8,12...) custom-call(bf16[128,768]{1,0:T(8,128)(2,1)S(1)} %get-tuple-element.70.a0, ...), custom_call_target="tpu_custom_call" | custom-call | flops 3623878656 | bytes 3969184 | tf_op jit(solution)/shard_map/pallas_call | solution.py:39
  117.8 1.7 collective-permute-start.31
  123.3 1.9 collective-permute-start.41
  125.2 1.6 fusion.5
  129.9 3.8 %collective-permute-done.27.recv_x = bf16[128,768]{1,0:T(8,128)(2,1)S(1)} collective-permute-done((bf16[128,768]{1,0:T(8,128)(2,1)}, bf16[128,768]{1,0:T(8,128)(2,1)S(1)}, u32[]{:S(2)}, u32[]{:S(2)}) %collective-permute-start.27) | collective-permute-done | bytes 196640 | tf_op jit(solution)/shard_map/ppermute | solution.py:270
  136.4 1.7 shard_map.285
  138.4 7.6 %collective-permute-done.31 = bf16[1552,384]{1,0:T(8,128)(2,1)} collective-permute-done((bf16[1552,384]{1,0:T(8,128)(2,1)}, bf16[1552,384]{1,0:T(8,128)(2,1)}, u32[]{:S(2)}, u32[]{:S(2)}) %collective-permute-start.31) | collective-permute-done | bytes 1191968 | tf_op jit(solution)/shard_map/ppermute | solution.py:273
  146.0 3.4 %fusion.40 = (bf16[1552,384]{1,0:T(8,128)(2,1)}, f32[1552,384]{1,0:T(8,128)}) fusion(f32[1552,384]{1,0:T(8,128)S(1)} %copy-done.3, bf16[1552,384]{1,0:T(8,128)(2,1)} %collective-permute-done.31), kind=kLoop, calls=%fused_computation.122 | loop fusion | flops 1787904 | bytes 7151616 | tf_op jit(solution)/shard_map/convert_element_type | solution.py:536
  149.5 1.5 collective-permute-start.34
  151.0 2.4 collective-permute-start.28
  158.3 6.2 %shard_map.286 = (f32[2,128,768]{2,1,0:T(8,128)S(1)}, bf16[2,128,768]{2,1,0:T(8,128)(2,1)S(1)}, f32[528,576]{1,0:T(8,128)S(1)}, bf16[528,576]{1,0:T(8,128)(2,1)S(1)}) custom-call(bf16[512,768]{1,0:T(8,128)(2,1)S(1)} %copy-done.9, bf16[128,768]{1,0:T(8,128)(2,1)S(1)} %get-tuple-element.76.da0, bf16[128,768]{1,0:T(8,128)(2,1)} %collective-permute-done.28.da1, ...), custom_call_target="tpu_custom_call" | custom-call | flops 1207959552 | bytes 5152912 | tf_op jit(solution)/shard_map/pallas_call | solution.py:39
  164.9 1.8 collective-permute-start.36
  168.2 1.7 fusion.39
  169.9 6.4 %collective-permute-done.33.recv_x = bf16[128,768]{1,0:T(8,128)(2,1)S(1)} collective-permute-done((bf16[128,768]{1,0:T(8,128)(2,1)S(1)}, bf16[128,768]{1,0:T(8,128)(2,1)S(1)}, u32[]{:S(2)}, u32[]{:S(2)}) %collective-permute-start.33) | collective-permute-done | bytes 196640 | tf_op jit(solution)/shard_map/ppermute | solution.py:270
  178.5 2.6 collective-permute-start.37
  183.1 1.5 collective-permute-done.44
  186.1 2.4 collective-permute-start.45
  189.8 6.4 %collective-permute-done.46 = bf16[1552,384]{1,0:T(8,128)(2,1)S(1)} collective-permute-done((bf16[1552,384]{1,0:T(8,128)(2,1)S(1)}, bf16[1552,384]{1,0:T(8,128)(2,1)S(1)}, u32[]{:S(2)}, u32[]{:S(2)}) %collective-permute-start.46) | collective-permute-done | bytes 1191968 | tf_op jit(solution)/shard_map/ppermute | solution.py:548
  196.8 7.7 %collective-permute-done.47 = f32[32,384]{1,0:T(8,128)S(1)} collective-permute-done((f32[32,384]{1,0:T(8,128)S(1)}, f32[32,384]{1,0:T(8,128)S(1)}, u32[]{:S(2)}, u32[]{:S(2)}) %collective-permute-start.47) | collective-permute-done | bytes 49184 | tf_op jit(solution)/shard_map/ppermute | solution.py:279
  207.1 4.0 %collective-permute-done.49 = f32[64,384]{1,0:T(8,128)S(1)} collective-permute-done((f32[64,384]{1,0:T(8,128)S(1)}, f32[64,384]{1,0:T(8,128)S(1)}, u32[]{:S(2)}, u32[]{:S(2)}) %collective-permute-start.49) | collective-permute-done | bytes 98336 | tf_op jit(solution)/shard_map/ppermute | solution.py:279
  211.9 1.6 collective-permute-start.50
  214.3 6.7 %collective-permute-start.56 = (bf16[1552,384]{1,0:T(8,128)(2,1)S(1)}, bf16[1552,384]{1,0:T(8,128)(2,1)}, u32[]{:S(2)}, u32[]{:S(2)}) collective-permute-start(bf16[1552,384]{1,0:T(8,128)(2,1)S(1)} %add_convert_fusion), channel_id=1, source_target_pairs={{0,16},{17,1},{26,10},{11,27},{4,20},{21,5},{30,14},{15,31}} | collective-permute-start | bytes 3575816 | tf_op jit(solution)/shard_map/ppermute | solution.py:562
  223.0 3.1 %collective-permute-done.52 = f32[4,4,192]{2,1,0:T(4,128)S(1)} collective-permute-done((f32[4,4,192]{2,1,0:T(4,128)S(1)}, f32[4,4,192]{2,1,0:T(4,128)S(1)}, u32[]{:S(2)}, u32[]{:S(2)}) %collective-permute-start.52) | collective-permute-done | bytes 12320 | tf_op jit(solution)/shard_map/ppermute | solution.py:279
  226.9 2.8 %convolution_bitcast_fusion = f32[1,192,6,384]{3,1,2,0:T(8,128)} fusion(f32[16,194]{1,0:T(8,128)S(1)} %reshape.166, f32[2,8,6,384]{3,2,1,0:T(8,128)S(1)} %bitcast.91), kind=kOutput, calls=%fused_computation.7 | convolution fusion | flops 84946944 | bytes 1929344 | tf_op jit(solution)/shard_map/dot_general | solution.py:686
  230.3 7.0 %collective-permute-start.54 = (bf16[528,576]{1,0:T(8,128)(2,1)S(1)}, bf16[528,576]{1,0:T(8,128)(2,1)S(1)}, u32[]{:S(2)}, u32[]{:S(2)}) collective-permute-start(bf16[528,576]{1,0:T(8,128)(2,1)S(1)} %add_convert_fusion.1), channel_id=1, source_target_pairs={{0,16},{17,1},{26,10},{11,27},{4,20},{21,5},{30,14},{15,31}} | collective-permute-start | bytes 1824776 | tf_op jit(solution)/shard_map/ppermute | solution.py:562
  239.8 5.8 %collective-permute-done.54 = bf16[528,576]{1,0:T(8,128)(2,1)S(1)} collective-permute-done((bf16[528,576]{1,0:T(8,128)(2,1)S(1)}, bf16[528,576]{1,0:T(8,128)(2,1)S(1)}, u32[]{:S(2)}, u32[]{:S(2)}) %collective-permute-start.54) | collective-permute-done | bytes 608288 | tf_op jit(solution)/shard_map/ppermute | solution.py:562
  253.8 1.7 maximum_bitcast_fusion.1
  (270 shorter events, 74.9 us)
Async XLA Ops:
  6.2 13.5 %collective-permute-start.3 = (f32[4,768]{1,0:T(4,128)S(1)}, f32[4,768]{1,0:T(4,128)S(1)}, u32[]{:S(2)}, u32[]{:S(2)}) collective-permute-start(f32[4,768]{1,0:T(4,128)S(1)} %convolution_add_fusion), channel_id=1, source_target_pairs={{0,1},{1,2},{2,3},{3,0},{4,5},{5,6},{6,7},{7,4},{8,9},{9,10},{10,1... | collective-permute-start | bytes 36872 | tf_op jit(solution)/shard_map/ppermute | solution.py:276
  9.2 11.8 %collective-permute-start.4 = (f32[4,768]{1,0:T(4,128)S(1)}, f32[4,768]{1,0:T(4,128)S(1)}, u32[]{:S(2)}, u32[]{:S(2)}) collective-permute-start(f32[4,768]{1,0:T(4,128)S(1)} %convolution_add_fusion), channel_id=1, source_target_pairs={{0,2},{1,3},{2,0},{3,1},{4,6},{5,7},{6,4},{7,5},{8,10},{9,11},{10,... | collective-permute-start | bytes 36872 | tf_op jit(solution)/shard_map/ppermute | solution.py:276
  11.8 9.2 %collective-permute-start.5 = (f32[4,768]{1,0:T(4,128)S(1)}, f32[4,768]{1,0:T(4,128)S(1)}, u32[]{:S(2)}, u32[]{:S(2)}) collective-permute-start(f32[4,768]{1,0:T(4,128)S(1)} %convolution_add_fusion), channel_id=1, source_target_pairs={{0,3},{1,0},{2,1},{3,2},{4,7},{5,4},{6,5},{7,6},{8,11},{9,8},{10,9... | collective-permute-start | bytes 36872 | tf_op jit(solution)/shard_map/ppermute | solution.py:276
  13.1 10.7 %collective-permute-start.6 = (bf16[528,576]{1,0:T(8,128)(2,1)}, bf16[528,576]{1,0:T(8,128)(2,1)}, u32[]{:S(2)}, u32[]{:S(2)}) collective-permute-start(bf16[528,576]{1,0:T(8,128)(2,1)} %fusion.3), channel_id=1, source_target_pairs={{0,2},{4,6},{11,9},{15,13},{17,19},{21,23},{26,24},{30,28}} | collective-permute-start | bytes 1824776 | tf_op jit(solution)/shard_map/ppermute | solution.py:379
  16.1 16.8 %collective-permute-start = (bf16[2,128,384]{2,1,0:T(8,128)(2,1)S(1)}, bf16[2,128,384]{2,1,0:T(8,128)(2,1)}, u32[]{:S(2)}, u32[]{:S(2)}) collective-permute-start(bf16[2,128,384]{2,1,0:T(8,128)(2,1)S(1)} %fusion.8), channel_id=1, source_target_pairs={{0,8},{1,9},{2,10},{3,11},{12,4},{13,5},{14,6},{15,7},{16,24},{17,... | collective-permute-start | bytes 589832 | tf_op jit(solution)/shard_map/ppermute | solution.py:331
  19.6 17.6 %collective-permute-start.2 = (bf16[2,128,384]{2,1,0:T(8,128)(2,1)S(1)}, bf16[2,128,384]{2,1,0:T(8,128)(2,1)}, u32[]{:S(2)}, u32[]{:S(2)}) collective-permute-start(bf16[2,128,384]{2,1,0:T(8,128)(2,1)S(1)} %fusion.8), channel_id=1, source_target_pairs={{4,8},{5,9},{6,10},{7,11},{8,4},{9,5},{10,6},{11,7},{20,24},{21,25... | collective-permute-start | bytes 589832 | tf_op jit(solution)/shard_map/ppermute | solution.py:328
  25.4 8.8 %collective-permute-start.7 = (f32[2304]{0:T(1024)S(1)}, f32[2304]{0:T(1024)S(1)}, u32[]{:S(2)}, u32[]{:S(2)}) collective-permute-start(f32[2304]{0:T(1024)S(1)} %get-tuple-element.118), channel_id=1, source_target_pairs={{0,1},{1,2},{2,3},{3,0},{4,5},{5,6},{6,7},{7,4},{8,9},{9,10},{10,1... | collective-permute-start | bytes 27656 | tf_op jit(solution)/shard_map/ppermute | solution.py:276
  25.5 8.8 %collective-permute-start.8 = (f32[2304]{0:T(1024)S(1)}, f32[2304]{0:T(1024)S(1)}, u32[]{:S(2)}, u32[]{:S(2)}) collective-permute-start(f32[2304]{0:T(1024)S(1)} %get-tuple-element.119), channel_id=1, source_target_pairs={{0,2},{1,3},{2,0},{3,1},{4,6},{5,7},{6,4},{7,5},{8,10},{9,11},{10,... | collective-permute-start | bytes 27656 | tf_op jit(solution)/shard_map/ppermute | solution.py:276
  30.0 4.3 %collective-permute-start.9 = (f32[2304]{0:T(1024)S(1)}, f32[2304]{0:T(1024)S(1)}, u32[]{:S(2)}, u32[]{:S(2)}) collective-permute-start(f32[2304]{0:T(1024)S(1)} %get-tuple-element.121), channel_id=1, source_target_pairs={{0,3},{1,0},{2,1},{3,2},{4,7},{5,4},{6,5},{7,6},{8,11},{9,8},{10,9... | collective-permute-start | bytes 27656 | tf_op jit(solution)/shard_map/ppermute | solution.py:276
  33.0 7.6 %collective-permute-start.1 = (bf16[2,128,384]{2,1,0:T(8,128)(2,1)S(1)}, bf16[2,128,384]{2,1,0:T(8,128)(2,1)S(1)}, u32[]{:S(2)}, u32[]{:S(2)}) collective-permute-start(bf16[2,128,384]{2,1,0:T(8,128)(2,1)S(1)} %get-tuple-element.137), channel_id=1, source_target_pairs={{4,0},{5,1},{6,2},{7,3},{8,12},{9,13},{10,14},{11,15},{20,16},{21,... | collective-permute-start | bytes 589832 | tf_op jit(solution)/shard_map/ppermute | solution.py:325
  34.3 25.5 %collective-permute-start.17 = (bf16[1552,384]{1,0:T(8,128)(2,1)S(1)}, bf16[1552,384]{1,0:T(8,128)(2,1)S(1)}, u32[]{:S(2)}, u32[]{:S(2)}) collective-permute-start(bf16[1552,384]{1,0:T(8,128)(2,1)S(1)} %fusion.2), channel_id=1, source_target_pairs={{0,2},{4,6},{11,9},{15,13},{17,19},{21,23},{26,24},{30,28}} | collective-permute-start | bytes 3575816 | tf_op jit(solution)/shard_map/ppermute | solution.py:379
  40.5 17.8 %collective-permute-start.13 = (bf16[528,576]{1,0:T(8,128)(2,1)}, bf16[528,576]{1,0:T(8,128)(2,1)S(1)}, u32[]{:S(2)}, u32[]{:S(2)}) collective-permute-start(bf16[528,576]{1,0:T(8,128)(2,1)} %broadcast_select_fusion.5), channel_id=1, source_target_pairs={{0,1},{2,3},{4,5},{6,7},{11,10},{9,8},{15,14},{13,12},{17,16},{19,... | collective-permute-start | bytes 1824776 | tf_op jit(solution)/shard_map/ppermute | solution.py:404
  43.3 5.6 %collective-permute-start.11 = (f32[8,384]{1,0:T(8,128)S(1)}, f32[8,384]{1,0:T(8,128)S(1)}, u32[]{:S(2)}, u32[]{:S(2)}) collective-permute-start(f32[8,384]{1,0:T(8,128)S(1)} %convert_add_fusion.4), channel_id=1, source_target_pairs={{4,0},{5,1},{6,2},{7,3},{8,12},{9,13},{10,14},{11,15},{20,16},{21,... | collective-permute-start | bytes 36872 | tf_op jit(solution)/shard_map/ppermute | solution.py:325
  44.6 4.3 %collective-permute-start.12 = (f32[8,384]{1,0:T(8,128)S(1)}, f32[8,384]{1,0:T(8,128)S(1)}, u32[]{:S(2)}, u32[]{:S(2)}) collective-permute-start(f32[8,384]{1,0:T(8,128)S(1)} %convert_add_fusion.4), channel_id=1, source_target_pairs={{4,8},{5,9},{6,10},{7,11},{8,4},{9,5},{10,6},{11,7},{20,24},{21,25... | collective-permute-start | bytes 36872 | tf_op jit(solution)/shard_map/ppermute | solution.py:328
  59.9 17.4 %collective-permute-start.19 = (bf16[1552,384]{1,0:T(8,128)(2,1)S(1)}, bf16[1552,384]{1,0:T(8,128)(2,1)S(1)}, u32[]{:S(2)}, u32[]{:S(2)}) collective-permute-start(bf16[1552,384]{1,0:T(8,128)(2,1)S(1)} %broadcast_select_fusion.2), channel_id=1, source_target_pairs={{0,1},{2,3},{4,5},{6,7},{11,10},{9,8},{15,14},{13,12},{17,16},{19,... | collective-permute-start | bytes 3575816 | tf_op jit(solution)/shard_map/ppermute | solution.py:404
  63.4 7.8 %collective-permute-start.15 = (bf16[2,128,768]{2,1,0:T(8,128)(2,1)S(1)}, bf16[2,128,768]{2,1,0:T(8,128)(2,1)S(1)}, u32[]{:S(2)}, u32[]{:S(2)}) collective-permute-start(bf16[2,128,768]{2,1,0:T(8,128)(2,1)S(1)} %shard_map.281.a0.dm_ref), channel_id=1, source_target_pairs={{0,16},{8,24},{16,0},{24,8},{1,17},{9,25},{17,1},{25,9},{2,18},{10... | collective-permute-start | bytes 1179656 | tf_op jit(solution)/shard_map/ppermute | solution.py:270
  63.5 10.9 %collective-permute-start.18 = (bf16[528,576]{1,0:T(8,128)(2,1)S(1)}, bf16[528,576]{1,0:T(8,128)(2,1)S(1)}, u32[]{:S(2)}, u32[]{:S(2)}) collective-permute-start(bf16[528,576]{1,0:T(8,128)(2,1)S(1)} %broadcast_select_fusion.3.wm), channel_id=1, source_target_pairs={{0,4},{4,0},{1,5},{5,1},{2,6},{6,2},{3,7},{7,3},{8,12},{12,8},{9,1... | collective-permute-start | bytes 1824776 | tf_op jit(solution)/shard_map/ppermute | solution.py:273
  78.9 28.6 %collective-permute-start.25 = (bf16[1552,384]{1,0:T(8,128)(2,1)S(1)}, bf16[1552,384]{1,0:T(8,128)(2,1)S(1)}, u32[]{:S(2)}, u32[]{:S(2)}) collective-permute-start(bf16[1552,384]{1,0:T(8,128)(2,1)S(1)} %broadcast_select_fusion.wm), channel_id=1, source_target_pairs={{0,4},{4,0},{1,5},{5,1},{2,6},{6,2},{3,7},{7,3},{8,12},{12,8},{9,1... | collective-permute-start | bytes 3575816 | tf_op jit(solution)/shard_map/ppermute | solution.py:273
  80.7 7.3 %collective-permute-start.21 = (bf16[128,768]{1,0:T(8,128)(2,1)S(1)}, bf16[128,768]{1,0:T(8,128)(2,1)S(1)}, u32[]{:S(2)}, u32[]{:S(2)}) collective-permute-start(bf16[128,768]{1,0:T(8,128)(2,1)S(1)} %fusion.4), channel_id=1, source_target_pairs={{0,16},{8,24},{16,0},{24,8},{1,17},{9,25},{17,1},{25,9},{2,18},{10... | collective-permute-start | bytes 589832 | tf_op jit(solution)/shard_map/ppermute | solution.py:270
  88.3 6.5 %collective-permute-start.23 = (bf16[128,768]{1,0:T(8,128)(2,1)S(1)}, bf16[128,768]{1,0:T(8,128)(2,1)S(1)}, u32[]{:S(2)}, u32[]{:S(2)}) collective-permute-start(bf16[128,768]{1,0:T(8,128)(2,1)S(1)} %get-tuple-element.70.a0), channel_id=1, source_target_pairs={{0,16},{8,24},{16,0},{24,8},{1,17},{9,25},{17,1},{25,9},{2,18},{10... | collective-permute-start | bytes 589832 | tf_op jit(solution)/shard_map/ppermute | solution.py:270
  90.1 4.7 %collective-permute-start.22 = (bf16[128,768]{1,0:T(8,128)(2,1)S(1)}, bf16[128,768]{1,0:T(8,128)(2,1)S(1)}, u32[]{:S(2)}, u32[]{:S(2)}) collective-permute-start(bf16[128,768]{1,0:T(8,128)(2,1)S(1)} %get-tuple-element.70.a0), channel_id=1, source_target_pairs={{0,8},{8,0},{16,24},{24,16},{1,9},{9,1},{17,25},{25,17},{2,10},{10... | collective-permute-start | bytes 589832 | tf_op jit(solution)/shard_map/ppermute | solution.py:267
  117.8 28.2 %collective-permute-start.31 = (bf16[1552,384]{1,0:T(8,128)(2,1)}, bf16[1552,384]{1,0:T(8,128)(2,1)}, u32[]{:S(2)}, u32[]{:S(2)}) collective-permute-start(bf16[1552,384]{1,0:T(8,128)(2,1)} %get-tuple-element.78), channel_id=1, source_target_pairs={{0,4},{4,0},{1,5},{5,1},{2,6},{6,2},{3,7},{7,3},{8,12},{12,8},{9,1... | collective-permute-start | bytes 3575816 | tf_op jit(solution)/shard_map/ppermute | solution.py:273
  120.9 4.3 %collective-permute-start.26 = (bf16[2,128,768]{2,1,0:T(8,128)(2,1)}, bf16[2,128,768]{2,1,0:T(8,128)(2,1)}, u32[]{:S(2)}, u32[]{:S(2)}) collective-permute-start(bf16[2,128,768]{2,1,0:T(8,128)(2,1)} %copy-done.20), channel_id=1, source_target_pairs={{0,8},{8,0},{16,24},{24,16},{1,9},{9,1},{17,25},{25,17},{2,10},{10... | collective-permute-start | bytes 1179656 | tf_op jit(solution)/shard_map/ppermute | solution.py:267
  126.9 6.9 %collective-permute-start.27 = (bf16[128,768]{1,0:T(8,128)(2,1)}, bf16[128,768]{1,0:T(8,128)(2,1)S(1)}, u32[]{:S(2)}, u32[]{:S(2)}) collective-permute-start(bf16[128,768]{1,0:T(8,128)(2,1)} %fusion.5), channel_id=1, source_target_pairs={{0,16},{8,24},{16,0},{24,8},{1,17},{9,25},{17,1},{25,9},{2,18},{10... | collective-permute-start | bytes 589832 | tf_op jit(solution)/shard_map/ppermute | solution.py:270
  138.0 15.4 %collective-permute-start.29 = (bf16[128,768]{1,0:T(8,128)(2,1)S(1)}, bf16[128,768]{1,0:T(8,128)(2,1)}, u32[]{:S(2)}, u32[]{:S(2)}) collective-permute-start(bf16[128,768]{1,0:T(8,128)(2,1)S(1)} %get-tuple-element.76.da0), channel_id=1, source_target_pairs={{0,16},{8,24},{16,0},{24,8},{1,17},{9,25},{17,1},{25,9},{2,18},{10... | collective-permute-start | bytes 589832 | tf_op jit(solution)/shard_map/ppermute | solution.py:270
  149.5 18.7 %collective-permute-start.34 = (bf16[1552,384]{1,0:T(8,128)(2,1)}, bf16[1552,384]{1,0:T(8,128)(2,1)}, u32[]{:S(2)}, u32[]{:S(2)}) collective-permute-start(bf16[1552,384]{1,0:T(8,128)(2,1)} %get-tuple-element.132), channel_id=1, source_target_pairs={{1,0},{3,2},{5,4},{7,6},{10,11},{8,9},{14,15},{12,13},{16,17},{18,... | collective-permute-start | bytes 3575816 | tf_op jit(solution)/shard_map/ppermute | solution.py:535
  151.0 4.7 %collective-permute-start.28 = (bf16[128,768]{1,0:T(8,128)(2,1)S(1)}, bf16[128,768]{1,0:T(8,128)(2,1)}, u32[]{:S(2)}, u32[]{:S(2)}) collective-permute-start(bf16[128,768]{1,0:T(8,128)(2,1)S(1)} %get-tuple-element.76.da0), channel_id=1, source_target_pairs={{0,8},{8,0},{16,24},{24,16},{1,9},{9,1},{17,25},{25,17},{2,10},{10... | collective-permute-start | bytes 589832 | tf_op jit(solution)/shard_map/ppermute | solution.py:267
  153.4 11.5 %collective-permute-start.35 = (bf16[2,128,768]{2,1,0:T(8,128)(2,1)}, bf16[2,128,768]{2,1,0:T(8,128)(2,1)S(1)}, u32[]{:S(2)}, u32[]{:S(2)}) collective-permute-start(bf16[2,128,768]{2,1,0:T(8,128)(2,1)} %get-tuple-element.90), channel_id=1, source_target_pairs={{0,8},{8,0},{16,24},{24,16},{1,9},{9,1},{17,25},{25,17},{2,10},{10... | collective-permute-start | bytes 1179656 | tf_op jit(solution)/shard_map/ppermute | solution.py:267
  164.9 11.4 %collective-permute-start.36 = (bf16[128,768]{1,0:T(8,128)(2,1)S(1)}, bf16[128,768]{1,0:T(8,128)(2,1)S(1)}, u32[]{:S(2)}, u32[]{:S(2)}) collective-permute-start(bf16[128,768]{1,0:T(8,128)(2,1)S(1)} %fusion.7), channel_id=1, source_target_pairs={{0,16},{8,24},{16,0},{24,8},{1,17},{9,25},{17,1},{25,9},{2,18},{10... | collective-permute-start | bytes 589832 | tf_op jit(solution)/shard_map/ppermute | solution.py:270
  166.7 17.9 %collective-permute-start.44 = (bf16[528,576]{1,0:T(8,128)(2,1)S(1)}, bf16[528,576]{1,0:T(8,128)(2,1)S(1)}, u32[]{:S(2)}, u32[]{:S(2)}) collective-permute-start(bf16[528,576]{1,0:T(8,128)(2,1)S(1)} %get-tuple-element.95), channel_id=1, source_target_pairs={{0,4},{4,0},{1,5},{5,1},{2,6},{6,2},{3,7},{7,3},{8,12},{12,8},{9,1... | collective-permute-start | bytes 1824776 | tf_op jit(solution)/shard_map/ppermute | solution.py:273
  167.5 8.8 %collective-permute-start.33 = (bf16[128,768]{1,0:T(8,128)(2,1)S(1)}, bf16[128,768]{1,0:T(8,128)(2,1)S(1)}, u32[]{:S(2)}, u32[]{:S(2)}) collective-permute-start(bf16[128,768]{1,0:T(8,128)(2,1)S(1)} %fusion.6), channel_id=1, source_target_pairs={{0,16},{8,24},{16,0},{24,8},{1,17},{9,25},{17,1},{25,9},{2,18},{10... | collective-permute-start | bytes 589832 | tf_op jit(solution)/shard_map/ppermute | solution.py:270
  177.0 4.8 %collective-permute-start.42 = (f32[8,768]{1,0:T(8,128)S(1)}, f32[8,768]{1,0:T(8,128)S(1)}, u32[]{:S(2)}, u32[]{:S(2)}) collective-permute-start(f32[8,768]{1,0:T(8,128)S(1)} %get-tuple-element.93), channel_id=1, source_target_pairs={{0,8},{8,0},{16,24},{24,16},{1,9},{9,1},{17,25},{25,17},{2,10},{10... | collective-permute-start | bytes 73736 | tf_op jit(solution)/shard_map/ppermute | solution.py:267
  177.0 19.2 %collective-permute-start.46 = (bf16[1552,384]{1,0:T(8,128)(2,1)S(1)}, bf16[1552,384]{1,0:T(8,128)(2,1)S(1)}, u32[]{:S(2)}, u32[]{:S(2)}) collective-permute-start(bf16[1552,384]{1,0:T(8,128)(2,1)S(1)} %get-tuple-element.130), channel_id=1, source_target_pairs={{2,0},{6,4},{9,11},{13,15},{19,17},{23,21},{24,26},{28,30}} | collective-permute-start | bytes 3575816 | tf_op jit(solution)/shard_map/ppermute | solution.py:548
  178.5 9.9 %collective-permute-start.37 = (bf16[2,128,384]{2,1,0:T(8,128)(2,1)S(1)}, bf16[2,128,384]{2,1,0:T(8,128)(2,1)S(1)}, u32[]{:S(2)}, u32[]{:S(2)}) collective-permute-start(bf16[2,128,384]{2,1,0:T(8,128)(2,1)S(1)} %slice.169), channel_id=1, source_target_pairs={{0,4},{1,5},{2,6},{3,7},{12,8},{13,9},{14,10},{15,11},{16,20},{17,... | collective-permute-start | bytes 589832 | tf_op jit(solution)/shard_map/ppermute | solution.py:353
  181.1 15.6 %collective-permute-start.39 = (bf16[2,128,384]{2,1,0:T(8,128)(2,1)S(1)}, bf16[2,128,384]{2,1,0:T(8,128)(2,1)S(1)}, u32[]{:S(2)}, u32[]{:S(2)}) collective-permute-start(bf16[2,128,384]{2,1,0:T(8,128)(2,1)S(1)} %slice.169), channel_id=1, source_target_pairs={{4,8},{5,9},{6,10},{7,11},{8,4},{9,5},{10,6},{11,7},{20,24},{21,25... | collective-permute-start | bytes 589832 | tf_op jit(solution)/shard_map/ppermute | solution.py:356
  181.8 4.3 %collective-permute-start.43 = (f32[8,768]{1,0:T(8,128)S(1)}, f32[8,768]{1,0:T(8,128)S(1)}, u32[]{:S(2)}, u32[]{:S(2)}) collective-permute-start(f32[8,768]{1,0:T(8,128)S(1)} %add.156), channel_id=1, source_target_pairs={{0,16},{8,24},{16,0},{24,8},{1,17},{9,25},{17,1},{25,9},{2,18},{10... | collective-permute-start | bytes 73736 | tf_op jit(solution)/shard_map/ppermute | solution.py:270
  184.8 19.7 %collective-permute-start.48 = (bf16[528,576]{1,0:T(8,128)(2,1)S(1)}, bf16[528,576]{1,0:T(8,128)(2,1)S(1)}, u32[]{:S(2)}, u32[]{:S(2)}) collective-permute-start(bf16[528,576]{1,0:T(8,128)(2,1)S(1)} %get-tuple-element.128), channel_id=1, source_target_pairs={{1,0},{3,2},{5,4},{7,6},{10,11},{8,9},{14,15},{12,13},{16,17},{18,... | collective-permute-start | bytes 1824776 | tf_op jit(solution)/shard_map/ppermute | solution.py:535
  186.1 10.5 %collective-permute-start.45 = (f32[16,384]{1,0:T(8,128)S(1)}, f32[16,384]{1,0:T(8,128)S(1)}, u32[]{:S(2)}, u32[]{:S(2)}) collective-permute-start(f32[16,384]{1,0:T(8,128)S(1)} %pad_maximum_fusion.6), channel_id=1, source_target_pairs={{0,4},{4,0},{1,5},{5,1},{2,6},{6,2},{3,7},{7,3},{8,12},{12,8},{9,1... | collective-permute-start | bytes 73736 | tf_op jit(solution)/shard_map/ppermute | solution.py:273
  188.5 8.2 %collective-permute-start.38 = (bf16[2,128,384]{2,1,0:T(8,128)(2,1)S(1)}, bf16[2,128,384]{2,1,0:T(8,128)(2,1)S(1)}, u32[]{:S(2)}, u32[]{:S(2)}) collective-permute-start(bf16[2,128,384]{2,1,0:T(8,128)(2,1)S(1)} %get-tuple-element.149), channel_id=1, source_target_pairs={{4,12},{5,13},{6,14},{7,15},{8,0},{9,1},{10,2},{11,3},{20,28},{21,... | collective-permute-start | bytes 589832 | tf_op jit(solution)/shard_map/ppermute | solution.py:350
  196.6 7.8 %collective-permute-start.47 = (f32[32,384]{1,0:T(8,128)S(1)}, f32[32,384]{1,0:T(8,128)S(1)}, u32[]{:S(2)}, u32[]{:S(2)}) collective-permute-start(f32[32,384]{1,0:T(8,128)S(1)} %pad_maximum_fusion.3), channel_id=1, source_target_pairs={{0,1},{1,0},{2,3},{3,2},{4,5},{5,4},{6,7},{7,6},{8,9},{9,8},{10,11... | collective-permute-start | bytes 147464 | tf_op jit(solution)/shard_map/ppermute | solution.py:279
  205.5 5.6 %collective-permute-start.49 = (f32[64,384]{1,0:T(8,128)S(1)}, f32[64,384]{1,0:T(8,128)S(1)}, u32[]{:S(2)}, u32[]{:S(2)}) collective-permute-start(f32[64,384]{1,0:T(8,128)S(1)} %pad_maximum_fusion.1), channel_id=1, source_target_pairs={{0,2},{1,3},{2,0},{3,1},{4,6},{5,7},{6,4},{7,5},{8,10},{9,11},{10,... | collective-permute-start | bytes 294920 | tf_op jit(solution)/shard_map/ppermute | solution.py:279
  205.7 15.4 %collective-permute-start.51 = (bf16[528,576]{1,0:T(8,128)(2,1)}, bf16[528,576]{1,0:T(8,128)(2,1)}, u32[]{:S(2)}, u32[]{:S(2)}) collective-permute-start(bf16[528,576]{1,0:T(8,128)(2,1)} %get-tuple-element.126), channel_id=1, source_target_pairs={{2,0},{6,4},{9,11},{13,15},{19,17},{23,21},{24,26},{28,30}} | collective-permute-start | bytes 1824776 | tf_op jit(solution)/shard_map/ppermute | solution.py:548
  211.9 9.1 %collective-permute-start.50 = (f32[16,192]{1,0:T(8,128)S(1)}, f32[16,192]{1,0:T(8,128)S(1)}, u32[]{:S(2)}, u32[]{:S(2)}) collective-permute-start(f32[16,192]{1,0:T(8,128)S(1)} %fusion.52), channel_id=1, source_target_pairs={{0,4},{4,0},{1,5},{5,1},{2,6},{6,2},{3,7},{7,3},{8,12},{12,8},{9,1... | collective-permute-start | bytes 36872 | tf_op jit(solution)/shard_map/ppermute | solution.py:273
  214.3 32.8 %collective-permute-start.56 = (bf16[1552,384]{1,0:T(8,128)(2,1)S(1)}, bf16[1552,384]{1,0:T(8,128)(2,1)}, u32[]{:S(2)}, u32[]{:S(2)}) collective-permute-start(bf16[1552,384]{1,0:T(8,128)(2,1)S(1)} %add_convert_fusion), channel_id=1, source_target_pairs={{0,16},{17,1},{26,10},{11,27},{4,20},{21,5},{30,14},{15,31}} | collective-permute-start | bytes 3575816 | tf_op jit(solution)/shard_map/ppermute | solution.py:562
  226.9 10.5 %collective-permute-start.53 = (f32[2,4,4,192]{3,2,1,0:T(4,128)S(1)}, f32[2,4,4,192]{3,2,1,0:T(4,128)S(1)}, u32[]{:S(2)}, u32[]{:S(2)}) collective-permute-start(f32[2,4,4,192]{3,2,1,0:T(4,128)S(1)} %get-tuple-element.153), channel_id=1, source_target_pairs={{0,2},{1,3},{2,0},{3,1},{4,6},{5,7},{6,4},{7,5},{8,10},{9,11},{10,... | collective-permute-start | bytes 73736 | tf_op jit(solution)/shard_map/ppermute | solution.py:279
  230.3 15.3 %collective-permute-start.54 = (bf16[528,576]{1,0:T(8,128)(2,1)S(1)}, bf16[528,576]{1,0:T(8,128)(2,1)S(1)}, u32[]{:S(2)}, u32[]{:S(2)}) collective-permute-start(bf16[528,576]{1,0:T(8,128)(2,1)S(1)} %add_convert_fusion.1), channel_id=1, source_target_pairs={{0,16},{17,1},{26,10},{11,27},{4,20},{21,5},{30,14},{15,31}} | collective-permute-start | bytes 1824776 | tf_op jit(solution)/shard_map/ppermute | solution.py:562
  245.7 5.4 %collective-permute-start.55 = (bf16[528,576]{1,0:T(8,128)(2,1)S(1)}, bf16[528,576]{1,0:T(8,128)(2,1)S(1)}, u32[]{:S(2)}, u32[]{:S(2)}) collective-permute-start(bf16[528,576]{1,0:T(8,128)(2,1)S(1)} %broadcast_select_fusion.4), channel_id=1, source_target_pairs={{0,8},{16,24},{17,25},{1,9},{26,18},{10,2},{11,3},{27,19},{4,12},{... | collective-permute-start | bytes 1824776 | tf_op jit(solution)/shard_map/ppermute | solution.py:574
  248.3 7.3 %collective-permute-start.57 = (bf16[1552,384]{1,0:T(8,128)(2,1)}, bf16[1552,384]{1,0:T(8,128)(2,1)S(1)}, u32[]{:S(2)}, u32[]{:S(2)}) collective-permute-start(bf16[1552,384]{1,0:T(8,128)(2,1)} %broadcast_select_fusion.1), channel_id=1, source_target_pairs={{0,8},{16,24},{17,25},{1,9},{26,18},{10,2},{11,3},{27,19},{4,12},{... | collective-permute-start | bytes 3575816 | tf_op jit(solution)/shard_map/ppermute | solution.py:574
  (50 other events, 331.4 us)

commit v2 on v1

v2 whole, which is shorter than its diff:
```python
import jax
import jax.numpy as jnp
from jax import lax
from jax.experimental import pallas as pl
from jax.experimental.pallas import tpu as pltpu
from jax.sharding import PartitionSpec as P

HEAD_DIM = 64
LENGTH = 256
PRECISE = lax.Precision.HIGHEST
NORM_EPSILON = 1e-06
F32 = jnp.float32
BF16 = jnp.bfloat16
ALL = ("dp", "row", "col")
GELU_A = 0.7978845608028654
GELU_B = 0.044715


def dot(left, right):
    return lax.dot_general(left, right, (((1,), (0,)), ((), ())), preferred_element_type=F32)


def dot_t(left, right):
    return lax.dot_general(left, right, (((1,), (1,)), ((), ())), preferred_element_type=F32)


def t_dot(left, right):
    return lax.dot_general(left, right, (((0,), (0,)), ((), ())), preferred_element_type=F32)


def call(kernel, outs, *args, scalar=None, flops=0, limit=28):
    total = sum(a.size * a.dtype.itemsize for a in args)
    total += sum(s[0][-1] * s[0][-2] * 4 for s in outs)
    specs = [pl.BlockSpec(memory_space=pltpu.VMEM)] * len(args)
    if scalar is not None:
        specs = [pl.BlockSpec(memory_space=pltpu.SMEM)] + specs
        args = (scalar,) + args
    return pl.pallas_call(
        kernel,
        in_specs=specs,
        out_specs=[pl.BlockSpec(memory_space=pltpu.VMEM)] * len(outs),
        out_shape=[jax.ShapeDtypeStruct(shape, dtype) for shape, dtype in outs],
        compiler_params=pltpu.CompilerParams(vmem_limit_bytes=limit * 1024 * 1024),
        cost_estimate=pl.CostEstimate(flops=flops, bytes_accessed=total, transcendentals=0),
    )(*args)


def layer_norm(values):
    center = values - jnp.mean(values, axis=1, keepdims=True)
    inverse = lax.rsqrt(jnp.mean(center * center, axis=1, keepdims=True) + NORM_EPSILON)
    return center * inverse, inverse


def norm_back(grad, normed, inverse):
    return inverse * (
        grad
        - jnp.mean(grad, axis=1, keepdims=True)
        - normed * jnp.mean(grad * normed, axis=1, keepdims=True)
    )


def pick(index, values):
    chosen = jnp.int32(values[0])
    for at, value in enumerate(values[1:], 1):
        chosen = jnp.where(index == at, jnp.int32(value), chosen)
    return chosen


def after(value, *earlier):
    return lax.optimization_barrier((value,) + earlier)[0]


def pieces_of(values):
    high = lax.reduce_precision(values, 8, 7)
    rest = values - high
    middle = lax.reduce_precision(rest, 8, 7)
    return jnp.stack([high, middle, rest - middle]).astype(BF16)


def column_sum(values):
    return jnp.sum(values, axis=0, keepdims=True)


def unfold(folded):
    rows = folded.shape[0] // 2
    return jnp.concatenate([folded[:rows], folded[rows:]], axis=1)


def fold(values):
    lanes = values.shape[1] // 2
    return jnp.concatenate([values[:, :lanes], values[:, lanes:]], axis=0)


def by_core(core_ref, body, mine, theirs):
    @pl.when(core_ref[0] == 0)
    def _():
        body(0, mine, theirs)

    @pl.when(core_ref[0] == 1)
    def _():
        body(1, theirs, mine)


def attention_kernel(
    core_ref, tok_ref, mod_ref, a0, a1, a2, a3, b_ref,
    hid_ref, oqkv_ref, p_ref, keep_ref, send_ref,
):
    half = a0.shape[1]
    width = half // 2
    heads = width // HEAD_DIM
    normed, _ = layer_norm(jnp.concatenate([tok_ref[0], tok_ref[2]], axis=0).astype(F32))
    hidden = (normed * (1.0 + mod_ref[1:2, :]) + mod_ref[0:1, :]).astype(BF16)
    hid_ref[...] = hidden

    def body(_, first, second):
        total_m = total_o = None
        blocks = (
            (first[0], second[0], first[2], second[2]),
            (first[1], second[1], first[3], second[3]),
        )
        for which, (qk_m, vo_m, qk_o, vo_o) in enumerate(blocks):
            left, right = hidden[:, :half], hidden[:, half:]
            qk = dot(left, qk_m[:half, :]) + dot(right, qk_o[:half, :])
            qk = (qk + qk_m[half : half + 1, :].astype(F32)).astype(BF16)
            v = dot(left, vo_m[:half, :width]) + dot(right, vo_o[:half, :width])
            v = (v + vo_m[half : half + 1, :width].astype(F32)).astype(BF16)
            parts = []
            for head in range(heads):
                at = head * HEAD_DIM
                scores = dot_t(qk[:, at : at + HEAD_DIM], qk[:, width + at : width + at + HEAD_DIM])
                scores = scores * HEAD_DIM ** (-0.5)
                powers = jnp.exp(scores - jnp.max(scores, axis=1, keepdims=True))
                soft = powers * (1.0 / jnp.sum(powers, axis=1, keepdims=True))
                p_ref[which * heads + head] = soft
                parts.append(dot(soft.astype(BF16), v[:, at : at + HEAD_DIM]))
            attended = jnp.concatenate(parts, axis=1).astype(BF16)
            oqkv_ref[:, which * 2 * half : (which + 1) * 2 * half] = jnp.concatenate([attended, qk, v], axis=1)
            part_m = dot(attended, unfold(vo_m[:half, width:]))
            part_o = dot(attended, unfold(vo_o[:half, width:]))
            total_m = part_m if total_m is None else total_m + part_m
            total_o = part_o if total_o is None else total_o + part_o
        split(keep_ref, send_ref, total_m, total_o)

    by_core(core_ref, body, (a0, a1, a2, a3), [b_ref.at[at] for at in range(4)])


def split(keep_ref, send_ref, first, second):
    rows, half = first.shape[0] // 2, first.shape[1]
    keep_ref[:, :half] = first[:rows]
    keep_ref[:, half:] = second[:rows]
    send_ref[:, :half] = first[rows:].astype(BF16)
    send_ref[:, half:] = second[rows:].astype(BF16)


def second_norm_kernel(keep, recv, x_ref, mod_ref, a_ref, x1_ref, h_ref):
    branch = keep[...] + recv[...].astype(F32) + mod_ref[6:7, :]
    middle = x_ref[0].astype(F32) + mod_ref[2:3, :] * branch
    normed, _ = layer_norm(middle)
    a_ref[...] = branch
    x1_ref[...] = middle
    h_ref[...] = (normed * (1.0 + mod_ref[4:5, :]) + mod_ref[3:4, :]).astype(BF16)


def mlp_kernel(
    h0, h1, tok_ref, mod_ref, a0, a1, a2, a3, b_ref, b3,
    keep_ref, send_ref, mkeep, msend, gkeep, gsend,
):
    half = a0.shape[1]
    hidden = jnp.concatenate([h0[...], h1[...]], axis=0)
    dm = jnp.concatenate([tok_ref[1], tok_ref[3]], axis=0).astype(F32) * mod_ref[5:6, :]
    dm = dm.astype(BF16)
    left, right = hidden[:, :half], hidden[:, half:]
    dleft, dright = dm[:, :half], dm[:, half:]
    sums = None
    for own, oth, grads, which in (
        (a0, a2, gkeep, 0),
        (a1, a3, gkeep, 1),
        (b_ref.at[0], b_ref.at[1], gsend, 0),
        (b_ref.at[2], b3, gsend, 1),
    ):
        up = dot(left, own[:half, :]) + dot(right, oth[:half, :])
        up = up + own[2 * half : 2 * half + 1, :].astype(F32)
        square = up * up
        tanh = jnp.tanh(GELU_A * (up + GELU_B * up * square))
        act = (0.5 * up * (1.0 + tanh)).astype(BF16)
        slope = 0.5 * (1.0 + tanh) + 0.5 * up * (1.0 - tanh * tanh) * (
            GELU_A * (1.0 + 3.0 * GELU_B * square)
        )
        dg = dot_t(dleft, own[half : 2 * half, :]) + dot_t(dright, oth[half : 2 * half, :])
        du = (dg * slope).astype(BF16)
        parts = (
            dot_t(du, own[:half, :]),
            dot_t(du, oth[:half, :]),
            dot(act, own[half : 2 * half, :]),
            dot(act, oth[half : 2 * half, :]),
        )
        sums = parts if sums is None else tuple(a + b for a, b in zip(sums, parts))
        bias = jnp.pad(column_sum(du.astype(F32)), ((0, 15), (0, 0))).astype(BF16)
        for side, (tokens, dtokens) in enumerate(((left, dleft), (right, dright))):
            grads[which, side, :half, :] = t_dot(tokens, du).astype(BF16)
            grads[which, side, half : 2 * half, :] = t_dot(act, dtokens).astype(BF16)
            grads[which, side, 2 * half : 2 * half + 16, :] = bias
    split(keep_ref, send_ref, sums[0], sums[1])
    split(mkeep, msend, sums[2], sums[3])


def second_back_kernel(keep, recv, x1_ref, a_ref, tok_ref, mod_ref, da_ref, dx1_ref, sums_ref):
    dh = keep[...] + recv[...].astype(F32)
    normed, inverse = layer_norm(x1_ref[...])
    dy = tok_ref[1].astype(F32)
    dx1 = dy + norm_back(dh * (1.0 + mod_ref[4:5, :]), normed, inverse)
    da = (mod_ref[2:3, :] * dx1).astype(BF16)
    dx1_ref[...] = dx1
    da_ref[...] = da
    sums_ref[0:1, :] = column_sum(dx1 * a_ref[...])
    sums_ref[1:2, :] = column_sum(dh)
    sums_ref[2:3, :] = column_sum(dh * normed)
    sums_ref[3:4, :] = column_sum((mod_ref[5:6, :] * dy).astype(BF16).astype(F32))
    sums_ref[4:5, :] = column_sum(da.astype(F32))
    sums_ref[5:8, :] = jnp.zeros((3, sums_ref.shape[1]), F32)


def attention_back_kernel(
    core_ref, hid_ref, da0, da1, oqkv_ref, p_ref, a0, a1, a2, a3, b_ref,
    keep_ref, send_ref, gkeep, gsend,
):
    half = a0.shape[1]
    width = half // 2
    heads = width // HEAD_DIM
    scale = HEAD_DIM ** (-0.5)
    hidden = hid_ref[...]
    da = jnp.concatenate([da0[...], da1[...]], axis=0)
    da_sides = (da[:, :half], da[:, half:])
    h_sides = (hidden[:, :half], hidden[:, half:])

    def body(core, first, second):
        pieces = (gkeep, gsend) if core == 0 else (gsend, gkeep)
        total_m = total_o = None
        blocks = (
            (first[0], second[0], first[2], second[2]),
            (first[1], second[1], first[3], second[3]),
        )
        for which, (qk_m, vo_m, qk_o, vo_o) in enumerate(blocks):
            base = which * 2 * half
            attended = oqkv_ref[:, base : base + width]
            qk = oqkv_ref[:, base + width : base + 3 * width]
            values = oqkv_ref[:, base + 3 * width : base + 4 * width]
            do = dot_t(da_sides[0], unfold(vo_m[:half, width:]))
            do = (do + dot_t(da_sides[1], unfold(vo_o[:half, width:]))).astype(BF16)
            dqs, dks, dvs = [], [], []
            for head in range(heads):
                at = head * HEAD_DIM
                q = qk[:, at : at + HEAD_DIM]
                k = qk[:, width + at : width + at + HEAD_DIM]
                do_head = do[:, at : at + HEAD_DIM]
                soft = p_ref[which * heads + head]
                dsoft = dot_t(do_head, values[:, at : at + HEAD_DIM])
                ds = (soft * (dsoft - jnp.sum(soft * dsoft, axis=1, keepdims=True))).astype(BF16)
                dqs.append(dot(ds, k) * scale)
                dks.append(t_dot(ds, q) * scale)
                dvs.append(t_dot(soft.astype(BF16), do_head))
            dqk = jnp.concatenate(dqs + dks, axis=1).astype(BF16)
            dv = jnp.concatenate(dvs, axis=1).astype(BF16)
            part_m = dot_t(dqk, qk_m[:half, :]) + dot_t(dv, vo_m[:half, :width])
            part_o = dot_t(dqk, qk_o[:half, :]) + dot_t(dv, vo_o[:half, :width])
            total_m = part_m if total_m is None else total_m + part_m
            total_o = part_o if total_o is None else total_o + part_o
            bias_qk = jnp.pad(column_sum(dqk.astype(F32)), ((0, 15), (0, 0))).astype(BF16)
            bias_v = jnp.pad(column_sum(dv.astype(F32)), ((0, 15), (0, width))).astype(BF16)
            for side in (0, 1):
                pieces[0][which, side, :half, :] = t_dot(h_sides[side], dqk).astype(BF16)
                pieces[0][which, side, half : half + 16, :] = bias_qk
                grad_v = t_dot(h_sides[side], dv)
                grad_o = fold(t_dot(attended, da_sides[side]))
                pieces[1][which, side, :half, :] = jnp.concatenate([grad_v, grad_o], axis=1).astype(BF16)
                pieces[1][which, side, half : half + 16, :] = bias_v
        split(keep_ref, send_ref, total_m, total_o)

    by_core(core_ref, body, (a0, a1, a2, a3), [b_ref.at[at] for at in range(4)])


def last_kernel(
    keep, recv, tok_ref, dx1_ref, mod_ref, x1_ref, mkeep, mrecv, two_ref, out_ref, sums_ref
):
    dh = keep[...] + recv[...].astype(F32)
    normed, inverse = layer_norm(tok_ref[0].astype(F32))
    dx = dx1_ref[...] + norm_back(dh * (1.0 + mod_ref[1:2, :]), normed, inverse)
    branch = mkeep[...] + mrecv[...].astype(F32) + mod_ref[7:8, :]
    out_ref[0] = (x1_ref[...] + mod_ref[5:6, :] * branch).astype(BF16)
    out_ref[1] = dx.astype(BF16)
    sums_ref[0:1, :] = column_sum(dh)
    sums_ref[1:2, :] = column_sum(dh * normed)
    sums_ref[2:5, :] = two_ref[0:3, :]
    sums_ref[5:6, :] = column_sum(tok_ref[1].astype(F32) * branch)
    sums_ref[6:8, :] = two_ref[3:5, :]


def make_body(n_dp, n_row, n_col):
    def flat(d, r, c):
        return (d * n_row + r) * n_col + c

    places = [(d, r, c) for d in range(n_dp) for r in range(n_row) for c in range(n_col)]

    def core_swap(v):
        return lax.ppermute(v, "dp", [(d, d ^ 1) for d in range(n_dp)])

    def chip_swap(v):
        return lax.ppermute(v, "dp", [(d, d ^ 2) for d in range(n_dp)])

    def row_swap(v):
        return lax.ppermute(v, "row", [(0, 1), (1, 0)])

    def col_swap(v, bits):
        return lax.ppermute(v, "col", [(c, c ^ bits) for c in range(n_col)])

    def total(*parts):
        out = parts[0].astype(F32)
        for part in parts[1:]:
            out = out + part.astype(F32)
        return out.astype(BF16)

    def body(
        latents,
        labels,
        step_ids,
        class_table,
        step_table,
        w_ada,
        b_ada,
        w_qkv,
        b_qkv,
        w_out,
        b_out,
        w_up,
        b_up,
        w_down,
        b_down,
        cotangent,
    ):
        tokens, width_row = latents.shape
        per_block = tokens // LENGTH
        sequences = labels.shape[0]
        width = class_table.shape[1]
        half = width // 2
        cols = w_qkv.shape[3]
        hid = w_up.shape[2]
        cond_cols = w_ada.shape[1]
        quick = n_row == 2 and per_block == 1
        dp_at = lax.axis_index("dp")
        row_at = lax.axis_index("row")
        col_at = lax.axis_index("col")
        core_at = dp_at % 2
        near_at = dp_at // 2
        block = LENGTH // 2
        core_arg = core_at.astype(jnp.int32).reshape(1)

        owner = near_at == row_at % 2

        def at_odd(condition, v, axis):
            return jnp.where(condition, jnp.flip(v, axis), v)

        def gather_owner(own, other, *earlier):
            across = lax.ppermute(
                own, ALL, [(flat(d, r, c), flat(d, 1 - r, c)) for d, r, c in places if d // 2 != r]
            )
            across_near = lax.ppermute(
                other, ALL, [(flat(d, r, c), flat(d ^ 2, 1 - r, c)) for d, r, c in places if d // 2 != r]
            )
            near = lax.ppermute(
                other, ALL, [(flat(d, r, c), flat(d ^ 2, r, c)) for d, r, c in places if d // 2 == r]
            )
            across = after(across, *earlier)
            return jnp.concatenate(
                [jnp.where(owner, own, near), jnp.where(owner, across, across_near)], axis=-1
            )

        def tokens_in(v):
            if quick:
                own = lax.dynamic_slice_in_dim(v, near_at * block, block, 1)
                other = lax.dynamic_slice_in_dim(v, (1 - near_at) * block, block, 1)
                return gather_owner(
                    jnp.concatenate([own, other], axis=0), jnp.concatenate([other, own], axis=0)
                )
            full = lax.all_gather(v, "row", axis=2, tiled=True)
            full = jnp.where(owner, full, chip_swap(full))
            start = (row_at // 2) * LENGTH
            own = lax.dynamic_slice_in_dim(full, start + near_at * block, block, 1)
            other = lax.dynamic_slice_in_dim(full, start + (1 - near_at) * block, block, 1)
            return jnp.concatenate([own, other], axis=0)

        def tokens_out(v):
            if quick:
                mine, theirs = v[:, :, :half], v[:, :, half:]
                near = lax.ppermute(
                    mine, ALL, [(flat(d, r, c), flat(d ^ 2, r, c)) for d, r, c in places if d // 2 != r]
                )
                across = lax.ppermute(
                    theirs, ALL, [(flat(d, r, c), flat(d, 1 - r, c)) for d, r, c in places if d // 2 == r]
                )
                across_near = lax.ppermute(
                    theirs, ALL, [(flat(d, r, c), flat(d ^ 2, 1 - r, c)) for d, r, c in places if d // 2 != r]
                )
                first = jnp.where(owner, mine, across)
                second = jnp.where(owner, near, across_near)
                return jnp.where(
                    near_at == 0,
                    jnp.concatenate([first, second], axis=1),
                    jnp.concatenate([second, first], axis=1),
                )
            other = chip_swap(v)
            full = jnp.where(
                near_at == 0, jnp.concatenate([v, other], axis=1), jnp.concatenate([other, v], axis=1)
            )
            rows = lax.all_gather(full, "row", axis=1)
            rows = rows.reshape(2, n_row // 2, 2, LENGTH, width)
            rows = lax.dynamic_index_in_dim(rows, near_at, 2, keepdims=False)
            rows = rows.reshape(2, tokens, width)
            return lax.dynamic_slice_in_dim(rows, row_at * width_row, width_row, 2)

        first_hop = [
            (flat(d, r, a), flat(d, r, b))
            for d in range(n_dp)
            for r in range(n_row)
            for a, b in (((0, 2), (3, 1)) if d // 2 == 0 else ((1, 3), (2, 0)))
        ]
        last_hop = [(b, a) for a, b in first_hop]
        held_at = jnp.where(near_at == 0, pick(col_at, (0, 3, 0, 3)), pick(col_at, (2, 1, 2, 1)))
        beside_at = jnp.where(near_at == 0, pick(col_at, (3, 0, 3, 0)), pick(col_at, (1, 2, 1, 2)))
        at_source = held_at == col_at

        def pack_attention(w, out):
            bias = jnp.concatenate(
                [b_qkv[0, 0], jnp.zeros((cols,), BF16), b_qkv[0, 1], jnp.zeros((cols,), BF16)]
            ).reshape(2, 1, 2 * cols)
            bias = jnp.pad(bias, ((0, 0), (0, 15), (0, 0)))
            second = jnp.concatenate([w[:, 2 * cols :], fold(out)], axis=1)
            return jnp.concatenate([jnp.stack([w[:, : 2 * cols], second]), bias], axis=1)

        def pack_mlp(up, down):
            bias = jnp.pad(b_up.reshape(2, 1, half), ((0, 0), (0, 15), (0, 0)))
            return jnp.concatenate(
                [jnp.stack([up[:, :half], up[:, half:]]), down.reshape(2, half, half), bias], axis=1
            )

        def by_piece(v):
            return jnp.where(core_at == 0, v[0], v[1]), jnp.where(core_at == 0, v[1], v[0])

        if quick:
            own_att = pack_attention(w_qkv[0].reshape(width_row, 3 * cols), w_out[0])
            piece = by_piece(own_att)[0]
            own_ids = jnp.stack([labels, step_ids], axis=1)
            other = chip_swap(own_ids)
            chips = jnp.where(near_at == 0, jnp.stack([own_ids, other]), jnp.stack([other, own_ids]))
            labels, step_ids = chips[:, :, 0].reshape(-1), chips[:, :, 1].reshape(-1)
            mlp_piece = by_piece(after(pack_mlp(w_up[0], w_down[0]), piece))[0]

        def to_chip(v):
            return lax.ppermute(
                v,
                ALL,
                [(flat(d, r, c), flat(d ^ 2, r, c)) for d, r, c in places if (d // 2 == 0) == (c in (0, 3))],
            )

        class_rows = class_table.shape[0]
        step_rows = step_table.shape[0]

        def hot(ids, rows):
            return ids[:, None] == (col_at * rows + jnp.arange(rows, dtype=jnp.int32))[None, :]

        partial_cond = dot(hot(labels, class_rows).astype(BF16), class_table) + dot(
            hot(step_ids, step_rows).astype(BF16), step_table
        )
        ada = w_ada[0]
        small_bias = jnp.concatenate([b_ada[0], b_out, b_down], axis=0).astype(F32)
        if quick:
            near = col_swap(partial_cond, 1)
            condition = (partial_cond + near) + (
                col_swap(partial_cond, 2) + col_swap(partial_cond, 3)
            )
        else:
            condition = lax.psum(partial_cond, "col")
        cond_part = lax.dynamic_slice_in_dim(condition, col_at * cond_cols, cond_cols, 1)
        act_part = cond_part * jax.nn.sigmoid(cond_part)
        if quick:
            own_tokens = tokens_in(after(jnp.stack([latents, cotangent]), condition))
            att_first = lax.ppermute(after(piece, condition), ALL, first_hop)
            held = jnp.where(at_source, piece, att_first)
            beside = col_swap(held, 1)
        mod_part = jnp.sum(
            jnp.einsum("pbd,djf->pbjf", pieces_of(act_part), ada, preferred_element_type=F32), axis=0
        ).reshape(act_part.shape[0], -1)
        if quick:
            turned = at_odd(col_at % 2 == 1, mod_part.reshape(2, 2, 2, -1), 2)
            turned = at_odd(col_at >= 2, turned, 1).reshape(2, n_col, -1)
            mod_sum = (turned[:, 0] + col_swap(turned[:, 1], 1)) + (
                col_swap(turned[:, 2], 2) + col_swap(turned[:, 3], 3)
            )
            mod_sum = after(mod_sum, held, own_tokens)
            both = jnp.concatenate([mod_sum.reshape(2, 6, width_row), jnp.zeros((2, 2, width_row), F32)], axis=1)
            both = both + small_bias[None]
            both = at_odd(row_at == 1, both, 0)
            other = row_swap(both[1])
            held_row = row_swap(after(held, other))
            beside_row = row_swap(after(beside, other))
            modulation = jnp.concatenate([both[0], other], axis=1)
        else:
            all_mod = lax.psum(mod_part, "col").reshape(sequences, 6, width_row)
            all_mod = jnp.concatenate([all_mod, jnp.zeros((sequences, 2, width_row), F32)], axis=1)
            all_mod = lax.all_gather(all_mod + small_bias[None], "row", axis=2, tiled=True)
            all_mod = jnp.where(owner, all_mod, chip_swap(all_mod))
            modulation = lax.dynamic_index_in_dim(
                all_mod, col_at * per_block + row_at // 2, 0, keepdims=False
            )

        def from_partner(mine):
            return core_swap(jnp.stack(mine))

        if quick:
            att_mine = (held, beside, held_row, beside_row)
            mlp_first = lax.ppermute(after(mlp_piece, beside), ALL, first_hop)
            held = jnp.where(at_source, mlp_piece, mlp_first)
            att_theirs = from_partner(att_mine[:3] + (after(att_mine[3], held),))
            beside = col_swap(held, 1)
            held_row = row_swap(held)
            own_tokens = after(own_tokens, beside, held_row)
            beside_row = row_swap(beside)
        else:
            own_tokens = tokens_in(jnp.stack([latents, cotangent]))
            full_qkv = lax.all_gather(w_qkv[0].reshape(width_row, 3 * cols), "row", axis=0, tiled=True)
            full_out = lax.all_gather(w_out[0], "row", axis=1, tiled=True)
            full_up = lax.all_gather(w_up[0], "row", axis=0, tiled=True)
            full_down = lax.all_gather(w_down[0], "row", axis=1, tiled=True)

            def fetch(first, second):
                every = lax.all_gather(jnp.stack([first, second]), "col")
                parts = [
                    by_piece(lax.dynamic_index_in_dim(every, at, 0, keepdims=False)[side])
                    for side in (0, 1)
                    for at in (held_at, beside_at)
                ]
                return tuple(v[0] for v in parts), jnp.stack([v[1] for v in parts])

            att_mine, att_theirs = fetch(
                pack_attention(full_qkv[:half], full_out[:, :half]),
                pack_attention(full_qkv[half:], full_out[:, half:]),
            )
            mlp_mine, mlp_theirs = fetch(
                pack_mlp(full_up[:half], full_down[:, :half]), pack_mlp(full_up[half:], full_down[:, half:])
            )
            mlp_theirs = mlp_theirs[jnp.array([0, 2, 1])], mlp_theirs[3]
        att_weights = att_mine + (att_theirs,)

        heads = 2 * cols // HEAD_DIM
        shard = (block, width)
        hidden_all, oqkv, soft, keep, send = call(
            attention_kernel,
            [
                ((LENGTH, width), BF16),
                ((LENGTH, 8 * cols), BF16),
                ((heads, LENGTH, LENGTH), F32),
                (shard, F32),
                (shard, BF16),
            ],
            own_tokens,
            modulation,
            *att_weights,
            scalar=core_arg,
            flops=2 * LENGTH * width * 8 * cols,
        )
        recv = chip_swap(send)
        branch_one, middle, hm_own = call(
            second_norm_kernel,
            [(shard, F32), (shard, F32), (shard, BF16)],
            keep,
            recv,
            own_tokens,
            modulation,
        )

        hm_far = chip_swap(hm_own)
        if quick:
            beside_row = after(beside_row, hm_far)
            mlp_mine = (held, beside, held_row, beside_row)
            mlp_theirs = from_partner((held, held_row, beside)), core_swap(beside_row)

        n_mlp = 2 * half + 16
        grads = ((2, 2, n_mlp, half), BF16)
        keep, send, mkeep, msend, mlp_keep, mlp_send = call(
            mlp_kernel,
            [(shard, F32), (shard, BF16), (shard, F32), (shard, BF16), grads, grads],
            hm_own,
            hm_far,
            own_tokens,
            modulation,
            *mlp_mine,
            *mlp_theirs,
            flops=24 * LENGTH * width * hid,
        )
        recv = chip_swap(send)
        if quick:
            mlp_sum = total(mlp_keep, after(core_swap(mlp_send), recv))
            recv = after(recv, mlp_sum)
            mlp_rows = row_swap(mlp_sum[:, 1])
        da_own, dmiddle, sums_two = call(
            second_back_kernel,
            [(shard, BF16), (shard, F32), ((8, width), F32)],
            keep,
            recv,
            middle,
            branch_one,
            own_tokens,
            modulation,
        )
        da_far = chip_swap(da_own)
        mrecv = chip_swap(after(msend, da_own))
        n_att = half + 16
        keep, send, att_keep, att_send = call(
            attention_back_kernel,
            [(shard, F32), (shard, BF16), ((2, 2, n_att, half), BF16), ((2, 2, n_att, half), BF16)],
            hidden_all,
            da_own,
            da_far,
            oqkv,
            soft,
            *att_weights,
            scalar=core_arg,
            flops=4 * LENGTH * width * 8 * cols,
            limit=58,
        )
        recv = chip_swap(send)
        if quick:
            att_core = core_swap(att_send)
            mlp_sum = total(mlp_sum[:, 0], after(mlp_rows, recv))
            recv = after(recv, mlp_sum)
            mlp_beside = col_swap(mlp_sum[1], 1)
        results, sums = call(
            last_kernel,
            [((2,) + shard, BF16), ((8, width), F32)],
            keep,
            recv,
            own_tokens,
            dmiddle,
            modulation,
            middle,
            mkeep,
            mrecv,
            sums_two,
        )

        ids = jnp.stack([labels, step_ids], axis=1).astype(F32)
        if quick:
            small = jnp.concatenate([cond_part, ids], axis=1)
            small = small.reshape(2, 2, 2, cond_cols + 2)
            small = at_odd(col_at % 2 == 1, small, 2)
            small = at_odd(col_at >= 2, small, 1)
            small = at_odd(row_at == 1, small, 0).reshape(2 * n_col, cond_cols + 2)
            small = jnp.concatenate([small, core_swap(after(small, middle))], axis=0)
            all_cond = small[:, :cond_cols]
            all_ids = small[:, cond_cols:]
            results = tokens_out(results)
            near = chip_swap(sums)
            att_sum = total(att_keep, after(att_core, near))
            att_rows = row_swap(att_sum[:, 1])
            sums = sums + near
            group = jnp.stack([sums, col_swap(sums, 1)])
            far = col_swap(group, 2)
            mlp_sum = total(mlp_sum[0], after(mlp_beside, far))
            mlp_last = lax.ppermute(mlp_sum, ALL, last_hop)
            att_sum = total(att_sum[:, 0], after(att_rows, far))
            far = after(far, mlp_sum, att_sum)
            att_beside = col_swap(att_sum[1], 1)
            group = jnp.stack([group, far]).reshape(n_col * 8, width)
            theirs = row_swap(group[:, half:])
            group = jnp.concatenate([group[:, :half], theirs], axis=0)
            other = core_swap(group)
            mlp_sum = total(mlp_sum, after(mlp_last, other))
            mlp_chip = to_chip(mlp_sum)
            other = after(other, mlp_sum, results)
            group = jnp.concatenate([group, other], axis=0)
            dmod = group.reshape(n_dp * n_col, 8, half)
        else:
            results = tokens_out(results)
            every = lax.all_gather(sums, ALL).reshape(2, 2, n_row // 2, 2, n_col, 8, width)
            every = jnp.sum(every, axis=0).transpose(2, 0, 3, 1, 4, 5)
            every = every.reshape(n_dp * sequences, 8, width)
            dmod = lax.dynamic_slice_in_dim(every, row_at * width_row, width_row, 2)
            all_cond = lax.all_gather(cond_part, "dp", axis=0, tiled=True)
            all_ids = lax.all_gather(ids, "dp", axis=0, tiled=True)

        gate = jax.nn.sigmoid(all_cond)
        all_act = all_cond * gate
        slope = gate * (1.0 + all_cond * (1.0 - gate))
        dmod_six = dmod[:, :6].reshape(-1, 6 * width_row)
        grad_ada = lax.dot_general(
            all_act, dmod_six, (((0,), (0,)), ((), ())), precision=PRECISE
        ).reshape(1, cond_cols, 6, width_row)
        totals = jnp.sum(dmod, axis=0)
        dact = jnp.sum(
            jnp.einsum("pbjf,djf->pbd", pieces_of(dmod[:, :6]), ada, preferred_element_type=F32), axis=0
        )
        if quick:
            flipped = row_swap(dact)
            flipped = flipped.reshape(2, 2, n_col, cond_cols)[:, ::-1]
            dcond = slope * (dact + flipped.reshape(-1, cond_cols))
            near = col_swap(dcond, 1)
            att_sum = total(att_sum[0], after(att_beside, near))
            att_last = lax.ppermute(att_sum, ALL, last_hop)
            near = near.reshape(-1, 2, cond_cols)[:, ::-1].reshape(dcond.shape)
            dcond = jnp.stack([dcond, near])
            far = col_swap(dcond, 2)
            far = far.reshape(-1, 2, 2, cond_cols)[:, ::-1]
            mlp_sum = jnp.where(at_source, mlp_sum, after(mlp_chip, far))
            mlp_core = core_swap(mlp_sum)
            att_sum = total(att_sum, after(att_last, far))
            att_chip = to_chip(att_sum)
            around = jnp.stack([dcond, far.reshape(dcond.shape)])
            around = at_odd(col_at % 2 == 1, around, 1)
            around = at_odd(col_at >= 2, around, 0)
            dcond = around.reshape(n_col, -1, cond_cols).transpose(1, 0, 2).reshape(-1, width)
        else:
            dcond = slope * lax.psum(dact, "row")
            dcond = lax.all_gather(dcond, "col", axis=1, tiled=True)
        all_ids = all_ids.astype(jnp.int32)
        grad_class = lax.dot_general(
            hot(all_ids[:, 0], class_rows).astype(F32), dcond, (((0,), (0,)), ((), ())), precision=PRECISE
        )
        grad_step = lax.dot_general(
            hot(all_ids[:, 1], step_rows).astype(F32), dcond, (((0,), (0,)), ((), ())), precision=PRECISE
        )

        def take(v, dim):
            return lax.dynamic_slice_in_dim(v, row_at * width_row, width_row, dim)

        def join(mine, theirs):
            return [
                jnp.where(core_at == 0, mine, theirs).astype(F32),
                jnp.where(core_at == 0, theirs, mine).astype(F32),
            ]

        def block_grads(att, mlp):
            qkv = jnp.concatenate([att[0][:half], att[1][:half, :cols]], axis=1)
            out = unfold(att[1][:half, cols:])
            up = jnp.concatenate([mlp[0][:half], mlp[1][:half]], axis=1)
            down = jnp.concatenate([mlp[0][half : 2 * half], mlp[1][half : 2 * half]], axis=0)
            bias_qkv = jnp.stack([att[0][half, :cols], att[1][half, :cols]])
            bias_up = jnp.stack([mlp[0][2 * half], mlp[1][2 * half]])
            return qkv, out, up, down, bias_qkv, bias_up

        if quick:
            att_sum = jnp.where(at_source, att_sum, att_chip)
            mlp_grads = join(mlp_sum, mlp_core)
            att_grads = join(att_sum, core_swap(att_sum))
            grad_qkv, grad_out, grad_up, grad_down, grad_bias_qkv, grad_bias_up = block_grads(
                att_grads, mlp_grads
            )
        else:

            def collect(keep, send):
                pieces = jnp.stack(join(keep, send))
                by_col = jnp.stack(
                    [
                        jnp.where(held_at == c, pieces[:, 0], 0.0) + jnp.where(beside_at == c, pieces[:, 1], 0.0)
                        for c in range(n_col)
                    ]
                )
                return lax.dynamic_index_in_dim(lax.psum(by_col, ALL), col_at, 0, keepdims=False)

            att = collect(att_keep, att_send)
            mlp = collect(mlp_keep, mlp_send)
            sides = [block_grads(att[:, side], mlp[:, side]) for side in (0, 1)]
            grad_qkv, grad_up = (
                take(jnp.concatenate([sides[0][at], sides[1][at]], axis=0), 0) for at in (0, 2)
            )
            grad_out, grad_down = (
                take(jnp.concatenate([sides[0][at], sides[1][at]], axis=1), 1) for at in (1, 3)
            )
            grad_bias_qkv, grad_bias_up = sides[0][4], sides[0][5]

        return (
            results[0],
            results[1],
            grad_class,
            grad_step,
            grad_ada,
            totals[None, :6],
            grad_qkv.reshape(1, width_row, 3, cols),
            grad_bias_qkv[None],
            grad_out[None],
            totals[None, 7],
            grad_up[None],
            grad_bias_up.reshape(1, hid),
            grad_down[None],
            totals[None, 6],
        )

    return body


def solution(mesh):
    return jax.shard_map(
        make_body(mesh.shape["dp"], mesh.shape["row"], mesh.shape["col"]),
        mesh=mesh,
        in_specs=(
            P(("dp", "col"), "row"),
            P("dp"),
            P("dp"),
            P("col", None),
            P("col", None),
            P(None, "col", None, "row"),
            P(None, None, "row"),
            P(None, "row", None, "col"),
            P(None, None, "col"),
            P(None, "col", "row"),
            P(None, "row"),
            P(None, "row", "col"),
            P(None, "col"),
            P(None, "col", "row"),
            P(None, "row"),
            P(("dp", "col"), "row"),
        ),
        out_specs=(
            P(("dp", "col"), "row"),
            P(("dp", "col"), "row"),
            P("col", None),
            P("col", None),
            P(None, "col", None, "row"),
            P(None, None, "row"),
            P(None, "row", None, "col"),
            P(None, None, "col"),
            P(None, "col", "row"),
            P(None, "row"),
            P(None, "row", "col"),
            P(None, "col"),
            P(None, "col", "row"),
            P(None, "row"),
        ),
        check_vma=False,
    )
```

time: 262 us -> 236 us (0.901)
  waiting for transfers between devices: 98.7 us -> 88.1 us
  local copies, waits for them, and re-layouts: 26.3 us -> 19.2 us
  starting transfers between devices: 83.7 us -> 78 us
  other arithmetic: 22.9 us -> 18.5 us
    ppermute x28 -> x24, starting transfers between devices: 54.4 us -> 47.7 us  [the longest x14 25.7 us: col_swap(): return lax.ppermute(v, 'col', [(c, c ^ bits) for c in range(n_col)])]
    unnamed x84 -> x76, local copies, waits for them, and re-layouts: 11.7 us -> 5.25 us
    ppermute x2 -> x1, waiting for transfers between devices: 6.85 us -> 1.09 us  [gather_owner(): lax.ppermute(own, ALL, [(flat(d, r, c), flat(d, 1 - r, c)) for d, r, c in...]
    ppermute x28 -> x24, waiting for transfers between devices: 39.3 us -> 34.5 us  [the longest x14 13.2 us: col_swap(): return lax.ppermute(v, 'col', [(c, c ^ bits) for c in range(n_col)])]
    ppermute x9 -> x8, starting transfers between devices: 10 us -> 14.8 us  [chip_swap(): return lax.ppermute(v, 'dp', [(d, d ^ 2) for d in range(n_dp)])]
    convert_element_type x12 -> x11, other arithmetic: 11.2 us -> 7.34 us  [the longest x8 6.01 us: total(): return out.astype(BF16)]
    ppermute x6 -> x9, waiting for transfers between devices: 21.3 us -> 24.9 us  [row_swap(): return lax.ppermute(v, 'row', [(0, 1), (1, 0)])]
    pallas_call x0 -> x2, local copies, waits for them, and re-layouts: none -> 3.48 us  [call(): pl.pallas_call(kernel, in_specs=specs, out_specs=[pl.BlockSpec(memory_spa...]
  transfers between devices with their start and end apart: 58 -> 52, of which waited for: 24 -> 31; matrix products, arithmetic and copies ran while one was open for 14% -> 11% of each run, Pallas kernels for 5% -> 6%
where the time goes in v2:
time: 236 us; the launch traced here: 234 us
  waiting for transfers between devices  88.1 us (37%)
  starting transfers between devices  78 us (33%)
  Pallas kernels  20.9 us (9%)
  local copies, waits for them, and re-layouts  19.2 us (8%)
  other arithmetic  18.5 us (8%)
  matrix products  7.81 us (3%)
    ppermute x14, starting transfers between devices, col_swap(): return lax.ppermute(v, 'col', [(c, c ^ bits) for c in range(n_col)])  25.7 us
    ppermute x8, waiting for transfers between devices, chip_swap(): return lax.ppermute(v, 'dp', [(d, d ^ 2) for d in range(n_dp)])  25.5 us
    ppermute x9, waiting for transfers between devices, row_swap(): return lax.ppermute(v, 'row', [(0, 1), (1, 0)])  24.9 us
    pallas_call x6, Pallas kernels, call(): pl.pallas_call(kernel, in_specs=specs, out_specs=[pl.BlockSpec(memory_spa...  20.9 us
    ppermute x8, starting transfers between devices, chip_swap(): return lax.ppermute(v, 'dp', [(d, d ^ 2) for d in range(n_dp)])  14.8 us
    ppermute x14, waiting for transfers between devices, col_swap(): return lax.ppermute(v, 'col', [(c, c ^ bits) for c in range(n_col)])  13.2 us
    ppermute x9, starting transfers between devices, row_swap(): return lax.ppermute(v, 'row', [(0, 1), (1, 0)])  9.36 us
    ppermute x1, waiting for transfers between devices, body(): att_last = lax.ppermute(att_sum, ALL, last_hop)  6.97 us
  transfers between devices with their start and end apart: 52, of which 31 were waited for; matrix products, arithmetic and copies ran while one was open for 11% of the time, Pallas kernels for 6%

profile of v2, /device:TPU:0, one launch (start us, length us, event | category | flops | bytes accessed | tf_op | source)
XLA Modules:
  0.0 234.4 jit_solution(14452953056407127752)
XLA Ops:
  1.5 2.9 %collective-permute-start = (s32[4,2]{0,1:T(2,128)S(1)}, s32[4,2]{0,1:T(2,128)S(1)}, u32[]{:S(2)}, u32[]{:S(2)}) collective-permute-start(s32[4,2]{0,1:T(2,128)S(1)} %get-tuple-element.175), channel_id=1, source_target_pairs={{0,16},{8,24},{16,0},{24,8},{1,17},{9,25},{17,1},{25,9},{2,18},{10... | collective-permute-start | bytes 104 | tf_op jit(solution)/shard_map/ppermute | solution.py:308
  12.0 1.6 collective-permute-start.1
  13.6 2.6 %collective-permute-start.2 = (f32[8,768]{1,0:T(8,128)S(1)}, f32[8,768]{1,0:T(8,128)S(1)}, u32[]{:S(2)}, u32[]{:S(2)}) collective-permute-start(f32[8,768]{1,0:T(8,128)S(1)} %convolution_add_fusion), channel_id=1, source_target_pairs={{0,2},{1,3},{2,0},{3,1},{4,6},{5,7},{6,4},{7,5},{8,10},{9,11},{10,... | collective-permute-start | bytes 73736 | tf_op jit(solution)/shard_map/ppermute | solution.py:314
  16.5 2.0 collective-permute-done.2
  18.5 3.3 %collective-permute-done.3 = f32[8,768]{1,0:T(8,128)S(1)} collective-permute-done((f32[8,768]{1,0:T(8,128)S(1)}, f32[8,768]{1,0:T(8,128)S(1)}, u32[]{:S(2)}, u32[]{:S(2)}) %collective-permute-start.3) | collective-permute-done | bytes 24608 | tf_op jit(solution)/shard_map/ppermute | solution.py:314
  22.6 1.8 pad_maximum_fusion.6
  24.4 3.2 %collective-permute-start.4 = (bf16[4,128,384]{2,1,0:T(8,128)(2,1)}, bf16[4,128,384]{2,1,0:T(8,128)(2,1)}, u32[]{:S(2)}, u32[]{:S(2)}) collective-permute-start(bf16[4,128,384]{2,1,0:T(8,128)(2,1)} %pad_maximum_fusion.6), channel_id=1, source_target_pairs={{0,16},{1,17},{2,18},{3,19},{8,24},{9,25},{10,26},{11,27},{20,4},{... | collective-permute-start | bytes 1179656 | tf_op jit(solution)/shard_map/ppermute | solution.py:369
  29.0 2.0 collective-permute-start.7
  32.3 2.4 %collective-permute-start.13 = (f32[2,2304]{1,0:T(2,128)S(1)}, f32[2,2304]{1,0:T(2,128)S(1)}, u32[]{:S(2)}, u32[]{:S(2)}) collective-permute-start(f32[2,2304]{1,0:T(2,128)S(1)} %get-tuple-element.160), channel_id=1, source_target_pairs={{0,2},{1,3},{2,0},{3,1},{4,6},{5,7},{6,4},{7,5},{8,10},{9,11},{10,... | collective-permute-start | bytes 55304 | tf_op jit(solution)/shard_map/ppermute | solution.py:314
  35.4 1.6 collective-permute-start.14
  37.2 3.4 %collective-permute-start.8 = (bf16[400,384]{1,0:T(8,128)(2,1)S(1)}, bf16[400,384]{1,0:T(8,128)(2,1)S(1)}, u32[]{:S(2)}, u32[]{:S(2)}) collective-permute-start(bf16[400,384]{1,0:T(8,128)(2,1)S(1)} %broadcast_select_fusion.5.a0), channel_id=1, source_target_pairs={{0,1},{1,0},{2,3},{3,2},{4,5},{5,4},{6,7},{7,6},{8,9},{9,8},{10,11... | collective-permute-start | bytes 921608 | tf_op jit(solution)/shard_map/ppermute | solution.py:314
  43.1 2.4 %collective-permute-done.8.a1 = bf16[400,384]{1,0:T(8,128)(2,1)S(1)} collective-permute-done((bf16[400,384]{1,0:T(8,128)(2,1)S(1)}, bf16[400,384]{1,0:T(8,128)(2,1)S(1)}, u32[]{:S(2)}, u32[]{:S(2)}) %collective-permute-start.8) | collective-permute-done | bytes 307232 | tf_op jit(solution)/shard_map/ppermute | solution.py:314
  45.4 5.0 %collective-permute-start.9 = (bf16[784,384]{1,0:T(8,128)(2,1)}, bf16[784,384]{1,0:T(8,128)(2,1)}, u32[]{:S(2)}, u32[]{:S(2)}) collective-permute-start(bf16[784,384]{1,0:T(8,128)(2,1)} %select_bitcast_fusion), channel_id=1, source_target_pairs={{0,2},{3,1},{4,6},{7,5},{8,10},{11,9},{12,14},{15,13},{17,19},{18,... | collective-permute-start | bytes 1806344 | tf_op jit(solution)/shard_map/ppermute | solution.py:520
  52.3 3.4 %collective-permute-done.15 = f32[8,384]{1,0:T(8,128)S(1)} collective-permute-done((f32[8,384]{1,0:T(8,128)S(1)}, f32[8,384]{1,0:T(8,128)S(1)}, u32[]{:S(2)}, u32[]{:S(2)}) %collective-permute-start.15) | collective-permute-done | bytes 12320 | tf_op jit(solution)/shard_map/ppermute | solution.py:311
  58.9 4.8 %collective-permute-start.10 = (bf16[784,384]{1,0:T(8,128)(2,1)S(1)}, bf16[784,384]{1,0:T(8,128)(2,1)S(1)}, u32[]{:S(2)}, u32[]{:S(2)}) collective-permute-start(bf16[784,384]{1,0:T(8,128)(2,1)S(1)} %broadcast_select_fusion.1.a0), channel_id=1, source_target_pairs={{0,1},{1,0},{2,3},{3,2},{4,5},{5,4},{6,7},{7,6},{8,9},{9,8},{10,11... | collective-permute-start | bytes 1806344 | tf_op jit(solution)/shard_map/ppermute | solution.py:314
  63.7 2.2 collective-permute-done.17.a3
  65.9 5.8 %collective-permute-done.16.a2 = bf16[400,384]{1,0:T(8,128)(2,1)S(1)} collective-permute-done((bf16[400,384]{1,0:T(8,128)(2,1)S(1)}, bf16[400,384]{1,0:T(8,128)(2,1)S(1)}, u32[]{:S(2)}, u32[]{:S(2)}) %collective-permute-start.16) | collective-permute-done | bytes 307232 | tf_op jit(solution)/shard_map/ppermute | solution.py:311
  71.9 6.2 %collective-permute-done.11.a2 = bf16[784,384]{1,0:T(8,128)(2,1)S(1)} collective-permute-done((bf16[784,384]{1,0:T(8,128)(2,1)S(1)}, bf16[784,384]{1,0:T(8,128)(2,1)S(1)}, u32[]{:S(2)}, u32[]{:S(2)}) %collective-permute-start.11) | collective-permute-done | bytes 602144 | tf_op jit(solution)/shard_map/ppermute | solution.py:311
  78.9 3.6 %shard_map.263 = (bf16[256,768]{1,0:T(8,128)(2,1)S(1)}, bf16[256,1536]{1,0:T(8,128)(2,1)S(1)}, f32[6,256,256]{2,1,0:T(8,128)S(1)}, f32[128,768]{1,0:T(8,128)S(1)}, bf16[128,768]{1,0:T(8,128)(2,1)S(1)}) custom-call(s32[1]{0:T(128)} %bitcast.core_ref, bf16[4,128,768]{2,1,0:T(8,128)(2,1)S(1)} %pad_maximum_fusion.3.tok_ref.x_ref, ...), custom_call_target="tpu_custom_call" | custom-call | flops 603979776 | bytes 6676480 | tf_op jit(solution)/shard_map/pallas_call | solution.py:38
  83.7 3.5 %collective-permute-start.19 = (bf16[128,768]{1,0:T(8,128)(2,1)S(1)}, bf16[128,768]{1,0:T(8,128)(2,1)S(1)}, u32[]{:S(2)}, u32[]{:S(2)}) collective-permute-start(bf16[128,768]{1,0:T(8,128)(2,1)S(1)} %get-tuple-element.73), channel_id=1, source_target_pairs={{0,16},{8,24},{16,0},{24,8},{1,17},{9,25},{17,1},{25,9},{2,18},{10... | collective-permute-start | bytes 589832 | tf_op jit(solution)/shard_map/ppermute | solution.py:308
  87.3 5.2 %collective-permute-done.19.recv = bf16[128,768]{1,0:T(8,128)(2,1)S(1)} collective-permute-done((bf16[128,768]{1,0:T(8,128)(2,1)S(1)}, bf16[128,768]{1,0:T(8,128)(2,1)S(1)}, u32[]{:S(2)}, u32[]{:S(2)}) %collective-permute-start.19) | collective-permute-done | bytes 196640 | tf_op jit(solution)/shard_map/ppermute | solution.py:308
  92.8 1.8 collective-permute-start.20
  94.6 4.7 %collective-permute-done.20.h1 = bf16[128,768]{1,0:T(8,128)(2,1)S(1)} collective-permute-done((bf16[128,768]{1,0:T(8,128)(2,1)S(1)}, bf16[128,768]{1,0:T(8,128)(2,1)S(1)}, u32[]{:S(2)}, u32[]{:S(2)}) %collective-permute-start.20) | collective-permute-done | bytes 196640 | tf_op jit(solution)/shard_map/ppermute | solution.py:308
  99.3 2.0 collective-permute-done.23.b3
  101.3 6.4 %shard_map.265 = (f32[128,768]{1,0:T(8,128)S(1)}, bf16[128,768]{1,0:T(8,128)(2,1)S(1)}, f32[128,768]{1,0:T(8,128)S(1)}, bf16[128,768]{1,0:T(8,128)(2,1)S(1)}, bf...) custom-call(bf16[128,768]{1,0:T(8,128)(2,1)S(1)} %get-tuple-element.74.h0, ...), custom_call_target="tpu_custom_call" | custom-call | flops 3623878656 | bytes 10002432 | tf_op jit(solution)/shard_map/pallas_call | solution.py:38
  107.8 2.0 copy.84
  112.2 5.7 %collective-permute-done.24.recv = bf16[128,768]{1,0:T(8,128)(2,1)S(1)} collective-permute-done((bf16[128,768]{1,0:T(8,128)(2,1)}, bf16[128,768]{1,0:T(8,128)(2,1)S(1)}, u32[]{:S(2)}, u32[]{:S(2)}) %collective-permute-start.24) | collective-permute-done | bytes 196640 | tf_op jit(solution)/shard_map/ppermute | solution.py:308
  117.9 3.1 %add_convert_fusion = bf16[2,2,784,384]{3,2,0,1:T(8,128)(2,1)S(1)} fusion(bf16[2,2,784,384]{3,2,0,1:T(8,128)(2,1)} %collective-permute-done.25, bf16[2,2,784,384]{3,2,1,0:T(8,128)(2,1)} %copy-done.6), kind=kLoop, calls=%fused_computation | loop fusion | flops 4816896 | bytes 7225344 | tf_op jit(solution)/shard_map/convert_element_type | solution.py:320
  126.4 5.9 %collective-permute-done.26.da1 = bf16[128,768]{1,0:T(8,128)(2,1)S(1)} collective-permute-done((bf16[128,768]{1,0:T(8,128)(2,1)S(1)}, bf16[128,768]{1,0:T(8,128)(2,1)S(1)}, u32[]{:S(2)}, u32[]{:S(2)}) %collective-permute-start.26) | collective-permute-done | bytes 196640 | tf_op jit(solution)/shard_map/ppermute | solution.py:308
  133.0 9.5 %shard_map.267 = (f32[128,768]{1,0:T(8,128)}, bf16[128,768]{1,0:T(8,128)(2,1)}, bf16[2,2,400,384]{3,2,1,0:T(8,128)(2,1)}, bf16[2,2,400,384]{3,2,1,0:T(8,128)(2,1)}) custom-call(s32[1]{0:T(128)} %bitcast.core_ref, bf16[256,768]{1,0:T(8,128)(2,1)} %copy-done.9, bf16[128,768]{1,0:T(8,128)(2,1)} %copy-done.11, bf16[128,768]{1,0:T(8,128)(2,1)} %copy-done.24, ...), custom_call_target="tpu_custom_call" | custom-call | flops 1207959552 | bytes 7618560 | tf_op jit(solution)/shard_map/pallas_call | solution.py:38
  146.1 3.8 %collective-permute-done.27.recv = bf16[128,768]{1,0:T(8,128)(2,1)S(1)} collective-permute-done((bf16[128,768]{1,0:T(8,128)(2,1)}, bf16[128,768]{1,0:T(8,128)(2,1)S(1)}, u32[]{:S(2)}, u32[]{:S(2)}) %collective-permute-start.27) | collective-permute-done | bytes 196640 | tf_op jit(solution)/shard_map/ppermute | solution.py:308
  151.2 1.9 fusion
  154.0 1.5 collective-permute-start.34
  155.8 3.7 %collective-permute-start.30 = (bf16[2,128,384]{2,1,0:T(8,128)(2,1)S(1)}, bf16[2,128,384]{2,1,0:T(8,128)(2,1)S(1)}, u32[]{:S(2)}, u32[]{:S(2)}) collective-permute-start(bf16[2,128,384]{2,1,0:T(8,128)(2,1)S(1)} %slice.189), channel_id=1, source_target_pairs={{0,4},{1,5},{2,6},{3,7},{8,12},{9,13},{10,14},{11,15},{20,16},{21,... | collective-permute-start | bytes 589832 | tf_op jit(solution)/shard_map/ppermute | solution.py:397
  159.5 2.2 collective-permute-start.35
  163.7 3.2 %collective-permute-start.36 = (f32[2,8,768]{2,1,0:T(8,128)S(1)}, f32[2,8,768]{2,1,0:T(8,128)S(1)}, u32[]{:S(2)}, u32[]{:S(2)}) collective-permute-start(f32[2,8,768]{2,1,0:T(8,128)S(1)} %get-tuple-element.163), channel_id=1, source_target_pairs={{0,2},{1,3},{2,0},{3,1},{4,6},{5,7},{6,4},{7,5},{8,10},{9,11},{10,... | collective-permute-start | bytes 147464 | tf_op jit(solution)/shard_map/ppermute | solution.py:314
  168.7 2.2 collective-permute-start.39
  170.9 3.7 %collective-permute-done.31 = bf16[2,128,384]{2,1,0:T(8,128)(2,1)S(1)} collective-permute-done((bf16[2,128,384]{2,1,0:T(8,128)(2,1)S(1)}, bf16[2,128,384]{2,1,0:T(8,128)(2,1)S(1)}, u32[]{:S(2)}, u32[]{:S(2)}) %collective-permute-start.31) | collective-permute-done | bytes 196640 | tf_op jit(solution)/shard_map/ppermute | solution.py:394
  175.2 2.2 collective-permute-done.37
  178.9 2.9 %collective-permute-done.39 = bf16[2,400,384]{2,1,0:T(8,128)(2,1)S(1)} collective-permute-done((bf16[2,400,384]{2,1,0:T(8,128)(2,1)S(1)}, bf16[2,400,384]{2,1,0:T(8,128)(2,1)S(1)}, u32[]{:S(2)}, u32[]{:S(2)}) %collective-permute-start.39) | collective-permute-done | bytes 614432 | tf_op jit(solution)/shard_map/ppermute | solution.py:311
  182.0 2.3 collective-permute-start.40
  187.8 6.2 %collective-permute-done.42 = bf16[784,384]{1,0:T(8,128)(2,1)S(1)} collective-permute-done((bf16[784,384]{1,0:T(8,128)(2,1)S(1)}, bf16[784,384]{1,0:T(8,128)(2,1)S(1)}, u32[]{:S(2)}, u32[]{:S(2)}) %collective-permute-start.42) | collective-permute-done | bytes 602144 | tf_op jit(solution)/shard_map/ppermute | solution.py:668
  194.1 4.6 %collective-permute-start.50 = (bf16[784,384]{1,0:T(8,128)(2,1)S(1)}, bf16[784,384]{1,0:T(8,128)(2,1)}, u32[]{:S(2)}, u32[]{:S(2)}) collective-permute-start(bf16[784,384]{1,0:T(8,128)(2,1)S(1)} %add_convert_fusion.2), channel_id=1, source_target_pairs={{0,16},{3,19},{4,20},{7,23},{8,24},{11,27},{12,28},{15,31},{17,1},... | collective-permute-start | bytes 1806344 | tf_op jit(solution)/shard_map/ppermute | solution.py:458
  201.2 1.8 collective-permute-done.43
  203.1 2.8 %convolution_bitcast_fusion = f32[1,192,6,384]{3,1,2,0:T(8,128)} fusion(f32[16,194]{1,0:T(8,128)S(1)} %constant_dynamic-update-slice_fusion, f32[2,8,6,384]{3,2,1,0:T(8,128)S(1)} %bitcast.175), kind=kOutput, calls=%fused_computation.7 | convolution fusion | flops 84946944 | bytes 1929344 | tf_op jit(solution)/shard_map/dot_general | solution.py:694
  207.0 2.4 %collective-permute-start.45 = (f32[2,16,192]{2,1,0:T(8,128)S(1)}, f32[2,16,192]{2,1,0:T(8,128)S(1)}, u32[]{:S(2)}, u32[]{:S(2)}) collective-permute-start(f32[2,16,192]{2,1,0:T(8,128)S(1)} %get-tuple-element.165), channel_id=1, source_target_pairs={{0,2},{1,3},{2,0},{3,1},{4,6},{5,7},{6,4},{7,5},{8,10},{9,11},{10,... | collective-permute-start | bytes 73736 | tf_op jit(solution)/shard_map/ppermute | solution.py:314
  212.1 7.0 %collective-permute-done.47 = bf16[400,384]{1,0:T(8,128)(2,1)S(1)} collective-permute-done((bf16[400,384]{1,0:T(8,128)(2,1)S(1)}, bf16[400,384]{1,0:T(8,128)(2,1)S(1)}, u32[]{:S(2)}, u32[]{:S(2)}) %collective-permute-start.47) | collective-permute-done | bytes 307232 | tf_op jit(solution)/shard_map/ppermute | solution.py:707
  222.1 2.7 %collective-permute-done.48 = bf16[400,384]{1,0:T(8,128)(2,1)S(1)} collective-permute-done((bf16[400,384]{1,0:T(8,128)(2,1)S(1)}, bf16[400,384]{1,0:T(8,128)(2,1)S(1)}, u32[]{:S(2)}, u32[]{:S(2)}) %collective-permute-start.48) | collective-permute-done | bytes 307232 | tf_op jit(solution)/shard_map/ppermute | solution.py:458
  (270 shorter events, 65.6 us)
Async XLA Ops:
  1.5 8.3 %collective-permute-start = (s32[4,2]{0,1:T(2,128)S(1)}, s32[4,2]{0,1:T(2,128)S(1)}, u32[]{:S(2)}, u32[]{:S(2)}) collective-permute-start(s32[4,2]{0,1:T(2,128)S(1)} %get-tuple-element.175), channel_id=1, source_target_pairs={{0,16},{8,24},{16,0},{24,8},{1,17},{9,25},{17,1},{25,9},{2,18},{10... | collective-permute-start | bytes 104 | tf_op jit(solution)/shard_map/ppermute | solution.py:308
  12.0 4.5 %collective-permute-start.1 = (f32[8,768]{1,0:T(8,128)S(1)}, f32[8,768]{1,0:T(8,128)S(1)}, u32[]{:S(2)}, u32[]{:S(2)}) collective-permute-start(f32[8,768]{1,0:T(8,128)S(1)} %convolution_add_fusion), channel_id=1, source_target_pairs={{0,1},{1,0},{2,3},{3,2},{4,5},{5,4},{6,7},{7,6},{8,9},{9,8},{10,11... | collective-permute-start | bytes 73736 | tf_op jit(solution)/shard_map/ppermute | solution.py:314
  13.6 4.9 %collective-permute-start.2 = (f32[8,768]{1,0:T(8,128)S(1)}, f32[8,768]{1,0:T(8,128)S(1)}, u32[]{:S(2)}, u32[]{:S(2)}) collective-permute-start(f32[8,768]{1,0:T(8,128)S(1)} %convolution_add_fusion), channel_id=1, source_target_pairs={{0,2},{1,3},{2,0},{3,1},{4,6},{5,7},{6,4},{7,5},{8,10},{9,11},{10,... | collective-permute-start | bytes 73736 | tf_op jit(solution)/shard_map/ppermute | solution.py:314
  16.2 5.6 %collective-permute-start.3 = (f32[8,768]{1,0:T(8,128)S(1)}, f32[8,768]{1,0:T(8,128)S(1)}, u32[]{:S(2)}, u32[]{:S(2)}) collective-permute-start(f32[8,768]{1,0:T(8,128)S(1)} %convolution_add_fusion), channel_id=1, source_target_pairs={{0,3},{1,2},{2,1},{3,0},{4,7},{5,6},{6,5},{7,4},{8,11},{9,10},{10,... | collective-permute-start | bytes 73736 | tf_op jit(solution)/shard_map/ppermute | solution.py:314
  24.4 12.7 %collective-permute-start.4 = (bf16[4,128,384]{2,1,0:T(8,128)(2,1)}, bf16[4,128,384]{2,1,0:T(8,128)(2,1)}, u32[]{:S(2)}, u32[]{:S(2)}) collective-permute-start(bf16[4,128,384]{2,1,0:T(8,128)(2,1)} %pad_maximum_fusion.6), channel_id=1, source_target_pairs={{0,16},{1,17},{2,18},{3,19},{8,24},{9,25},{10,26},{11,27},{20,4},{... | collective-permute-start | bytes 1179656 | tf_op jit(solution)/shard_map/ppermute | solution.py:369
  27.6 23.9 %collective-permute-start.6 = (bf16[4,128,384]{2,1,0:T(8,128)(2,1)}, bf16[4,128,384]{2,1,0:T(8,128)(2,1)}, u32[]{:S(2)}, u32[]{:S(2)}) collective-permute-start(bf16[4,128,384]{2,1,0:T(8,128)(2,1)} %pad_maximum_fusion.6), channel_id=1, source_target_pairs={{4,16},{5,17},{6,18},{7,19},{12,24},{13,25},{14,26},{15,27},{16,4}... | collective-permute-start | bytes 1179656 | tf_op jit(solution)/shard_map/ppermute | solution.py:366
  29.0 6.4 %collective-permute-start.7 = (bf16[400,384]{1,0:T(8,128)(2,1)S(1)}, bf16[400,384]{1,0:T(8,128)(2,1)}, u32[]{:S(2)}, u32[]{:S(2)}) collective-permute-start(bf16[400,384]{1,0:T(8,128)(2,1)S(1)} %copy-done.22), channel_id=1, source_target_pairs={{0,2},{3,1},{4,6},{7,5},{8,10},{11,9},{12,14},{15,13},{17,19},{18,... | collective-permute-start | bytes 921608 | tf_op jit(solution)/shard_map/ppermute | solution.py:486
  32.2 9.5 %collective-permute-start.12 = (f32[2,2304]{1,0:T(2,128)S(1)}, f32[2,2304]{1,0:T(2,128)S(1)}, u32[]{:S(2)}, u32[]{:S(2)}) collective-permute-start(f32[2,2304]{1,0:T(2,128)S(1)} %get-tuple-element.161), channel_id=1, source_target_pairs={{0,1},{1,0},{2,3},{3,2},{4,5},{5,4},{6,7},{7,6},{8,9},{9,8},{10,11... | collective-permute-start | bytes 55304 | tf_op jit(solution)/shard_map/ppermute | solution.py:314
  32.3 10.7 %collective-permute-start.13 = (f32[2,2304]{1,0:T(2,128)S(1)}, f32[2,2304]{1,0:T(2,128)S(1)}, u32[]{:S(2)}, u32[]{:S(2)}) collective-permute-start(f32[2,2304]{1,0:T(2,128)S(1)} %get-tuple-element.160), channel_id=1, source_target_pairs={{0,2},{1,3},{2,0},{3,1},{4,6},{5,7},{6,4},{7,5},{8,10},{9,11},{10,... | collective-permute-start | bytes 55304 | tf_op jit(solution)/shard_map/ppermute | solution.py:314
  35.4 7.6 %collective-permute-start.14 = (f32[2,2304]{1,0:T(2,128)S(1)}, f32[2,2304]{1,0:T(2,128)S(1)}, u32[]{:S(2)}, u32[]{:S(2)}) collective-permute-start(f32[2,2304]{1,0:T(2,128)S(1)} %get-tuple-element.159), channel_id=1, source_target_pairs={{0,3},{1,2},{2,1},{3,0},{4,7},{5,6},{6,5},{7,4},{8,11},{9,10},{10,... | collective-permute-start | bytes 55304 | tf_op jit(solution)/shard_map/ppermute | solution.py:314
  37.2 8.3 %collective-permute-start.8 = (bf16[400,384]{1,0:T(8,128)(2,1)S(1)}, bf16[400,384]{1,0:T(8,128)(2,1)S(1)}, u32[]{:S(2)}, u32[]{:S(2)}) collective-permute-start(bf16[400,384]{1,0:T(8,128)(2,1)S(1)} %broadcast_select_fusion.5.a0), channel_id=1, source_target_pairs={{0,1},{1,0},{2,3},{3,2},{4,5},{5,4},{6,7},{7,6},{8,9},{9,8},{10,11... | collective-permute-start | bytes 921608 | tf_op jit(solution)/shard_map/ppermute | solution.py:314
  41.7 9.8 %collective-permute-start.5 = (bf16[4,128,384]{2,1,0:T(8,128)(2,1)S(1)}, bf16[4,128,384]{2,1,0:T(8,128)(2,1)S(1)}, u32[]{:S(2)}, u32[]{:S(2)}) collective-permute-start(bf16[4,128,384]{2,1,0:T(8,128)(2,1)S(1)} %get-tuple-element.149), channel_id=1, source_target_pairs={{4,0},{5,1},{6,2},{7,3},{12,8},{13,9},{14,10},{15,11},{16,20},{17,... | collective-permute-start | bytes 1179656 | tf_op jit(solution)/shard_map/ppermute | solution.py:363
  45.4 13.3 %collective-permute-start.9 = (bf16[784,384]{1,0:T(8,128)(2,1)}, bf16[784,384]{1,0:T(8,128)(2,1)}, u32[]{:S(2)}, u32[]{:S(2)}) collective-permute-start(bf16[784,384]{1,0:T(8,128)(2,1)} %select_bitcast_fusion), channel_id=1, source_target_pairs={{0,2},{3,1},{4,6},{7,5},{8,10},{11,9},{12,14},{15,13},{17,19},{18,... | collective-permute-start | bytes 1806344 | tf_op jit(solution)/shard_map/ppermute | solution.py:520
  51.7 4.0 %collective-permute-start.15 = (f32[8,384]{1,0:T(8,128)S(1)}, f32[8,384]{1,0:T(8,128)S(1)}, u32[]{:S(2)}, u32[]{:S(2)}) collective-permute-start(f32[8,384]{1,0:T(8,128)S(1)} %get-tuple-element.167), channel_id=1, source_target_pairs={{0,4},{4,0},{1,5},{5,1},{2,6},{6,2},{3,7},{7,3},{8,12},{12,8},{9,1... | collective-permute-start | bytes 36872 | tf_op jit(solution)/shard_map/ppermute | solution.py:311
  55.7 10.2 %collective-permute-start.17 = (bf16[400,384]{1,0:T(8,128)(2,1)S(1)}, bf16[400,384]{1,0:T(8,128)(2,1)S(1)}, u32[]{:S(2)}, u32[]{:S(2)}) collective-permute-start(bf16[400,384]{1,0:T(8,128)(2,1)S(1)} %collective-permute-done.8.a1), channel_id=1, source_target_pairs={{0,4},{4,0},{1,5},{5,1},{2,6},{6,2},{3,7},{7,3},{8,12},{12,8},{9,1... | collective-permute-start | bytes 921608 | tf_op jit(solution)/shard_map/ppermute | solution.py:311
  56.2 15.5 %collective-permute-start.16 = (bf16[400,384]{1,0:T(8,128)(2,1)S(1)}, bf16[400,384]{1,0:T(8,128)(2,1)S(1)}, u32[]{:S(2)}, u32[]{:S(2)}) collective-permute-start(bf16[400,384]{1,0:T(8,128)(2,1)S(1)} %broadcast_select_fusion.5.a0), channel_id=1, source_target_pairs={{0,4},{4,0},{1,5},{5,1},{2,6},{6,2},{3,7},{7,3},{8,12},{12,8},{9,1... | collective-permute-start | bytes 921608 | tf_op jit(solution)/shard_map/ppermute | solution.py:311
  58.8 19.3 %collective-permute-start.11 = (bf16[784,384]{1,0:T(8,128)(2,1)S(1)}, bf16[784,384]{1,0:T(8,128)(2,1)S(1)}, u32[]{:S(2)}, u32[]{:S(2)}) collective-permute-start(bf16[784,384]{1,0:T(8,128)(2,1)S(1)} %broadcast_select_fusion.1.a0), channel_id=1, source_target_pairs={{0,4},{4,0},{1,5},{5,1},{2,6},{6,2},{3,7},{7,3},{8,12},{12,8},{9,1... | collective-permute-start | bytes 1806344 | tf_op jit(solution)/shard_map/ppermute | solution.py:311
  58.9 19.2 %collective-permute-start.10 = (bf16[784,384]{1,0:T(8,128)(2,1)S(1)}, bf16[784,384]{1,0:T(8,128)(2,1)S(1)}, u32[]{:S(2)}, u32[]{:S(2)}) collective-permute-start(bf16[784,384]{1,0:T(8,128)(2,1)S(1)} %broadcast_select_fusion.1.a0), channel_id=1, source_target_pairs={{0,1},{1,0},{2,3},{3,2},{4,5},{5,4},{6,7},{7,6},{8,9},{9,8},{10,11... | collective-permute-start | bytes 1806344 | tf_op jit(solution)/shard_map/ppermute | solution.py:314
  71.9 7.0 %collective-permute-start.18 = (bf16[4,400,384]{2,1,0:T(8,128)(2,1)S(1)}, bf16[4,400,384]{2,1,0:T(8,128)(2,1)S(1)}, u32[]{:S(2)}, u32[]{:S(2)}) collective-permute-start(bf16[4,400,384]{2,1,0:T(8,128)(2,1)S(1)} %pad_maximum_fusion.1), channel_id=1, source_target_pairs={{0,8},{8,0},{16,24},{24,16},{1,9},{9,1},{17,25},{25,17},{2,10},{10... | collective-permute-start | bytes 3686408 | tf_op jit(solution)/shard_map/ppermute | solution.py:305
  78.4 22.9 %collective-permute-start.22 = (bf16[3,784,384]{2,1,0:T(8,128)(2,1)S(1)}, bf16[3,784,384]{2,1,0:T(8,128)(2,1)S(1)}, u32[]{:S(2)}, u32[]{:S(2)}) collective-permute-start(bf16[3,784,384]{2,1,0:T(8,128)(2,1)S(1)} %pad_maximum_fusion), channel_id=1, source_target_pairs={{0,8},{8,0},{16,24},{24,16},{1,9},{9,1},{17,25},{25,17},{2,10},{10... | collective-permute-start | bytes 5419016 | tf_op jit(solution)/shard_map/ppermute | solution.py:305
  78.4 16.1 %collective-permute-start.21 = (bf16[784,384]{1,0:T(8,128)(2,1)S(1)}, bf16[784,384]{1,0:T(8,128)(2,1)S(1)}, u32[]{:S(2)}, u32[]{:S(2)}) collective-permute-start(bf16[784,384]{1,0:T(8,128)(2,1)S(1)} %collective-permute-done.10.a1), channel_id=1, source_target_pairs={{0,4},{4,0},{1,5},{5,1},{2,6},{6,2},{3,7},{7,3},{8,12},{12,8},{9,1... | collective-permute-start | bytes 1806344 | tf_op jit(solution)/shard_map/ppermute | solution.py:311
  83.7 8.8 %collective-permute-start.19 = (bf16[128,768]{1,0:T(8,128)(2,1)S(1)}, bf16[128,768]{1,0:T(8,128)(2,1)S(1)}, u32[]{:S(2)}, u32[]{:S(2)}) collective-permute-start(bf16[128,768]{1,0:T(8,128)(2,1)S(1)} %get-tuple-element.73), channel_id=1, source_target_pairs={{0,16},{8,24},{16,0},{24,8},{1,17},{9,25},{17,1},{25,9},{2,18},{10... | collective-permute-start | bytes 589832 | tf_op jit(solution)/shard_map/ppermute | solution.py:308
  92.8 6.5 %collective-permute-start.20 = (bf16[128,768]{1,0:T(8,128)(2,1)S(1)}, bf16[128,768]{1,0:T(8,128)(2,1)S(1)}, u32[]{:S(2)}, u32[]{:S(2)}) collective-permute-start(bf16[128,768]{1,0:T(8,128)(2,1)S(1)} %get-tuple-element.74.h0), channel_id=1, source_target_pairs={{0,16},{8,24},{16,0},{24,8},{1,17},{9,25},{17,1},{25,9},{2,18},{10... | collective-permute-start | bytes 589832 | tf_op jit(solution)/shard_map/ppermute | solution.py:308
  110.2 7.7 %collective-permute-start.25 = (bf16[2,2,784,384]{3,2,0,1:T(8,128)(2,1)}, bf16[2,2,784,384]{3,2,0,1:T(8,128)(2,1)}, u32[]{:S(2)}, u32[]{:S(2)}) collective-permute-start(bf16[2,2,784,384]{3,2,0,1:T(8,128)(2,1)} %copy.84), channel_id=1, source_target_pairs={{0,8},{8,0},{16,24},{24,16},{1,9},{9,1},{17,25},{25,17},{2,10},{10... | collective-permute-start | bytes 7225352 | tf_op jit(solution)/shard_map/ppermute | solution.py:305
  110.5 7.4 %collective-permute-start.24 = (bf16[128,768]{1,0:T(8,128)(2,1)}, bf16[128,768]{1,0:T(8,128)(2,1)S(1)}, u32[]{:S(2)}, u32[]{:S(2)}) collective-permute-start(bf16[128,768]{1,0:T(8,128)(2,1)} %copy-done.16), channel_id=1, source_target_pairs={{0,16},{8,24},{16,0},{24,8},{1,17},{9,25},{17,1},{25,9},{2,18},{10... | collective-permute-start | bytes 589832 | tf_op jit(solution)/shard_map/ppermute | solution.py:308
  123.0 28.3 %collective-permute-start.28 = (bf16[2,784,384]{2,1,0:T(8,128)(2,1)}, bf16[2,784,384]{2,1,0:T(8,128)(2,1)}, u32[]{:S(2)}, u32[]{:S(2)}) collective-permute-start(bf16[2,784,384]{2,1,0:T(8,128)(2,1)} %slice_bitcast_fusion), channel_id=1, source_target_pairs={{0,4},{4,0},{1,5},{5,1},{2,6},{6,2},{3,7},{7,3},{8,12},{12,8},{9,1... | collective-permute-start | bytes 3612680 | tf_op jit(solution)/shard_map/ppermute | solution.py:311
  124.9 7.4 %collective-permute-start.26 = (bf16[128,768]{1,0:T(8,128)(2,1)S(1)}, bf16[128,768]{1,0:T(8,128)(2,1)S(1)}, u32[]{:S(2)}, u32[]{:S(2)}) collective-permute-start(bf16[128,768]{1,0:T(8,128)(2,1)S(1)} %get-tuple-element.84.da0), channel_id=1, source_target_pairs={{0,16},{8,24},{16,0},{24,8},{1,17},{9,25},{17,1},{25,9},{2,18},{10... | collective-permute-start | bytes 589832 | tf_op jit(solution)/shard_map/ppermute | solution.py:308
  142.4 7.5 %collective-permute-start.27 = (bf16[128,768]{1,0:T(8,128)(2,1)}, bf16[128,768]{1,0:T(8,128)(2,1)S(1)}, u32[]{:S(2)}, u32[]{:S(2)}) collective-permute-start(bf16[128,768]{1,0:T(8,128)(2,1)} %get-tuple-element.88), channel_id=1, source_target_pairs={{0,16},{8,24},{16,0},{24,8},{1,17},{9,25},{17,1},{25,9},{2,18},{10... | collective-permute-start | bytes 589832 | tf_op jit(solution)/shard_map/ppermute | solution.py:308
  145.3 23.0 %collective-permute-start.38 = (bf16[2,2,400,384]{3,2,0,1:T(8,128)(2,1)S(1)}, bf16[2,2,400,384]{3,2,0,1:T(8,128)(2,1)S(1)}, u32[]{:S(2)}, u32[]{:S(2)}) collective-permute-start(bf16[2,2,400,384]{3,2,0,1:T(8,128)(2,1)S(1)} %copy.87), channel_id=1, source_target_pairs={{0,8},{8,0},{16,24},{24,16},{1,9},{9,1},{17,25},{25,17},{2,10},{10... | collective-permute-start | bytes 3686408 | tf_op jit(solution)/shard_map/ppermute | solution.py:305
  145.4 8.0 %collective-permute-start.29 = (bf16[128,768]{1,0:T(8,128)(2,1)S(1)}, bf16[128,768]{1,0:T(8,128)(2,1)S(1)}, u32[]{:S(2)}, u32[]{:S(2)}) collective-permute-start(bf16[128,768]{1,0:T(8,128)(2,1)S(1)} %copy-done.15), channel_id=1, source_target_pairs={{0,16},{8,24},{16,0},{24,8},{1,17},{9,25},{17,1},{25,9},{2,18},{10... | collective-permute-start | bytes 589832 | tf_op jit(solution)/shard_map/ppermute | solution.py:308
  154.0 5.4 %collective-permute-start.34 = (f32[8,768]{1,0:T(8,128)S(1)}, f32[8,768]{1,0:T(8,128)S(1)}, u32[]{:S(2)}, u32[]{:S(2)}) collective-permute-start(f32[8,768]{1,0:T(8,128)S(1)} %get-tuple-element.98), channel_id=1, source_target_pairs={{0,16},{8,24},{16,0},{24,8},{1,17},{9,25},{17,1},{25,9},{2,18},{10... | collective-permute-start | bytes 73736 | tf_op jit(solution)/shard_map/ppermute | solution.py:308
  155.8 11.2 %collective-permute-start.30 = (bf16[2,128,384]{2,1,0:T(8,128)(2,1)S(1)}, bf16[2,128,384]{2,1,0:T(8,128)(2,1)S(1)}, u32[]{:S(2)}, u32[]{:S(2)}) collective-permute-start(bf16[2,128,384]{2,1,0:T(8,128)(2,1)S(1)} %slice.189), channel_id=1, source_target_pairs={{0,4},{1,5},{2,6},{3,7},{8,12},{9,13},{10,14},{11,15},{20,16},{21,... | collective-permute-start | bytes 589832 | tf_op jit(solution)/shard_map/ppermute | solution.py:397
  159.5 4.2 %collective-permute-start.35 = (f32[8,768]{1,0:T(8,128)S(1)}, f32[8,768]{1,0:T(8,128)S(1)}, u32[]{:S(2)}, u32[]{:S(2)}) collective-permute-start(f32[8,768]{1,0:T(8,128)S(1)} %add.134), channel_id=1, source_target_pairs={{0,1},{1,0},{2,3},{3,2},{4,5},{5,4},{6,7},{7,6},{8,9},{9,8},{10,11... | collective-permute-start | bytes 73736 | tf_op jit(solution)/shard_map/ppermute | solution.py:314
  161.7 9.1 %collective-permute-start.32 = (bf16[2,128,384]{2,1,0:T(8,128)(2,1)S(1)}, bf16[2,128,384]{2,1,0:T(8,128)(2,1)S(1)}, u32[]{:S(2)}, u32[]{:S(2)}) collective-permute-start(bf16[2,128,384]{2,1,0:T(8,128)(2,1)S(1)} %slice.189), channel_id=1, source_target_pairs={{4,16},{5,17},{6,18},{7,19},{12,24},{13,25},{14,26},{15,27},{16,4}... | collective-permute-start | bytes 589832 | tf_op jit(solution)/shard_map/ppermute | solution.py:400
  162.4 15.0 %collective-permute-start.37 = (bf16[784,384]{1,0:T(8,128)(2,1)S(1)}, bf16[784,384]{1,0:T(8,128)(2,1)S(1)}, u32[]{:S(2)}, u32[]{:S(2)}) collective-permute-start(bf16[784,384]{1,0:T(8,128)(2,1)S(1)} %slice_bitcast_fusion.4), channel_id=1, source_target_pairs={{0,1},{1,0},{2,3},{3,2},{4,5},{5,4},{6,7},{7,6},{8,9},{9,8},{10,11... | collective-permute-start | bytes 1806344 | tf_op jit(solution)/shard_map/ppermute | solution.py:314
  163.7 11.5 %collective-permute-start.36 = (f32[2,8,768]{2,1,0:T(8,128)S(1)}, f32[2,8,768]{2,1,0:T(8,128)S(1)}, u32[]{:S(2)}, u32[]{:S(2)}) collective-permute-start(f32[2,8,768]{2,1,0:T(8,128)S(1)} %get-tuple-element.163), channel_id=1, source_target_pairs={{0,2},{1,3},{2,0},{3,1},{4,6},{5,7},{6,4},{7,5},{8,10},{9,11},{10,... | collective-permute-start | bytes 147464 | tf_op jit(solution)/shard_map/ppermute | solution.py:314
  167.0 7.6 %collective-permute-start.31 = (bf16[2,128,384]{2,1,0:T(8,128)(2,1)S(1)}, bf16[2,128,384]{2,1,0:T(8,128)(2,1)S(1)}, u32[]{:S(2)}, u32[]{:S(2)}) collective-permute-start(bf16[2,128,384]{2,1,0:T(8,128)(2,1)S(1)} %get-tuple-element.147), channel_id=1, source_target_pairs={{4,20},{5,21},{6,22},{7,23},{12,28},{13,29},{14,30},{15,31},{16,0}... | collective-permute-start | bytes 589832 | tf_op jit(solution)/shard_map/ppermute | solution.py:394
  168.7 13.1 %collective-permute-start.39 = (bf16[2,400,384]{2,1,0:T(8,128)(2,1)S(1)}, bf16[2,400,384]{2,1,0:T(8,128)(2,1)S(1)}, u32[]{:S(2)}, u32[]{:S(2)}) collective-permute-start(bf16[2,400,384]{2,1,0:T(8,128)(2,1)S(1)} %slice_bitcast_fusion.2), channel_id=1, source_target_pairs={{0,4},{4,0},{1,5},{5,1},{2,6},{6,2},{3,7},{7,3},{8,12},{12,8},{9,1... | collective-permute-start | bytes 1843208 | tf_op jit(solution)/shard_map/ppermute | solution.py:311
  177.6 16.4 %collective-permute-start.42 = (bf16[784,384]{1,0:T(8,128)(2,1)S(1)}, bf16[784,384]{1,0:T(8,128)(2,1)S(1)}, u32[]{:S(2)}, u32[]{:S(2)}) collective-permute-start(bf16[784,384]{1,0:T(8,128)(2,1)S(1)} %fusion.5), channel_id=1, source_target_pairs={{2,0},{1,3},{6,4},{5,7},{10,8},{9,11},{14,12},{13,15},{19,17},{16,... | collective-permute-start | bytes 1806344 | tf_op jit(solution)/shard_map/ppermute | solution.py:668
  182.0 4.4 %collective-permute-start.40 = (f32[32,384]{1,0:T(8,128)S(1)}, f32[32,384]{1,0:T(8,128)S(1)}, u32[]{:S(2)}, u32[]{:S(2)}) collective-permute-start(f32[32,384]{1,0:T(8,128)S(1)} %get-tuple-element.158), channel_id=1, source_target_pairs={{0,4},{4,0},{1,5},{5,1},{2,6},{6,2},{3,7},{7,3},{8,12},{12,8},{9,1... | collective-permute-start | bytes 147464 | tf_op jit(solution)/shard_map/ppermute | solution.py:311
  186.5 22.9 %collective-permute-start.46 = (bf16[400,384]{1,0:T(8,128)(2,1)S(1)}, bf16[400,384]{1,0:T(8,128)(2,1)S(1)}, u32[]{:S(2)}, u32[]{:S(2)}) collective-permute-start(bf16[400,384]{1,0:T(8,128)(2,1)S(1)} %slice_bitcast_fusion.6), channel_id=1, source_target_pairs={{0,1},{1,0},{2,3},{3,2},{4,5},{5,4},{6,7},{7,6},{8,9},{9,8},{10,11... | collective-permute-start | bytes 921608 | tf_op jit(solution)/shard_map/ppermute | solution.py:314
  194.1 32.3 %collective-permute-start.50 = (bf16[784,384]{1,0:T(8,128)(2,1)S(1)}, bf16[784,384]{1,0:T(8,128)(2,1)}, u32[]{:S(2)}, u32[]{:S(2)}) collective-permute-start(bf16[784,384]{1,0:T(8,128)(2,1)S(1)} %add_convert_fusion.2), channel_id=1, source_target_pairs={{0,16},{3,19},{4,20},{7,23},{8,24},{11,27},{12,28},{15,31},{17,1},... | collective-permute-start | bytes 1806344 | tf_op jit(solution)/shard_map/ppermute | solution.py:458
  199.1 3.8 %collective-permute-start.43 = (f32[16,192]{1,0:T(8,128)S(1)}, f32[16,192]{1,0:T(8,128)S(1)}, u32[]{:S(2)}, u32[]{:S(2)}) collective-permute-start(f32[16,192]{1,0:T(8,128)S(1)} %fusion.6), channel_id=1, source_target_pairs={{0,4},{4,0},{1,5},{5,1},{2,6},{6,2},{3,7},{7,3},{8,12},{12,8},{9,1... | collective-permute-start | bytes 36872 | tf_op jit(solution)/shard_map/ppermute | solution.py:311
  203.0 3.8 %collective-permute-start.44 = (f32[16,192]{1,0:T(8,128)S(1)}, f32[16,192]{1,0:T(8,128)S(1)}, u32[]{:S(2)}, u32[]{:S(2)}) collective-permute-start(f32[16,192]{1,0:T(8,128)S(1)} %add_multiply_fusion), channel_id=1, source_target_pairs={{0,1},{1,0},{2,3},{3,2},{4,5},{5,4},{6,7},{7,6},{8,9},{9,8},{10,11... | collective-permute-start | bytes 36872 | tf_op jit(solution)/shard_map/ppermute | solution.py:314
  207.0 5.0 %collective-permute-start.45 = (f32[2,16,192]{2,1,0:T(8,128)S(1)}, f32[2,16,192]{2,1,0:T(8,128)S(1)}, u32[]{:S(2)}, u32[]{:S(2)}) collective-permute-start(f32[2,16,192]{2,1,0:T(8,128)S(1)} %get-tuple-element.165), channel_id=1, source_target_pairs={{0,2},{1,3},{2,0},{3,1},{4,6},{5,7},{6,4},{7,5},{8,10},{9,11},{10,... | collective-permute-start | bytes 73736 | tf_op jit(solution)/shard_map/ppermute | solution.py:314
  209.5 9.6 %collective-permute-start.47 = (bf16[400,384]{1,0:T(8,128)(2,1)S(1)}, bf16[400,384]{1,0:T(8,128)(2,1)S(1)}, u32[]{:S(2)}, u32[]{:S(2)}) collective-permute-start(bf16[400,384]{1,0:T(8,128)(2,1)S(1)} %fusion.10), channel_id=1, source_target_pairs={{2,0},{1,3},{6,4},{5,7},{10,8},{9,11},{14,12},{13,15},{19,17},{16,... | collective-permute-start | bytes 921608 | tf_op jit(solution)/shard_map/ppermute | solution.py:707
  219.2 5.7 %collective-permute-start.48 = (bf16[400,384]{1,0:T(8,128)(2,1)S(1)}, bf16[400,384]{1,0:T(8,128)(2,1)S(1)}, u32[]{:S(2)}, u32[]{:S(2)}) collective-permute-start(bf16[400,384]{1,0:T(8,128)(2,1)S(1)} %add_convert_fusion.3), channel_id=1, source_target_pairs={{0,16},{3,19},{4,20},{7,23},{8,24},{11,27},{12,28},{15,31},{17,1},... | collective-permute-start | bytes 921608 | tf_op jit(solution)/shard_map/ppermute | solution.py:458
  226.5 3.7 %collective-permute-start.51 = (bf16[784,384]{1,0:T(8,128)(2,1)S(1)}, bf16[784,384]{1,0:T(8,128)(2,1)}, u32[]{:S(2)}, u32[]{:S(2)}) collective-permute-start(bf16[784,384]{1,0:T(8,128)(2,1)S(1)} %broadcast_select_fusion), channel_id=1, source_target_pairs={{0,8},{8,0},{16,24},{24,16},{1,9},{9,1},{17,25},{25,17},{2,10},{10... | collective-permute-start | bytes 1806344 | tf_op jit(solution)/shard_map/ppermute | solution.py:305
  (40 other events, 304.9 us)

commit v3 on v2

--- a/solution.py
+++ b/solution.py
@@ -631,7 +631,6 @@
         if quick:
             att_core = core_swap(att_send)
             mlp_sum = total(mlp_sum[:, 0], after(mlp_rows, recv))
-            recv = after(recv, mlp_sum)
             mlp_beside = col_swap(mlp_sum[1], 1)
         results, sums = call(
             last_kernel,
@@ -738,21 +737,21 @@
             ]
 
         def block_grads(att, mlp):
+            if att is None:
+                up = jnp.concatenate([mlp[0][:half], mlp[1][:half]], axis=1)
+                down = jnp.concatenate([mlp[0][half : 2 * half], mlp[1][half : 2 * half]], axis=0)
+                return up, down, jnp.stack([mlp[0][2 * half], mlp[1][2 * half]])
             qkv = jnp.concatenate([att[0][:half], att[1][:half, :cols]], axis=1)
             out = unfold(att[1][:half, cols:])
-            up = jnp.concatenate([mlp[0][:half], mlp[1][:half]], axis=1)
-            down = jnp.concatenate([mlp[0][half : 2 * half], mlp[1][half : 2 * half]], axis=0)
-            bias_qkv = jnp.stack([att[0][half, :cols], att[1][half, :cols]])
-            bias_up = jnp.stack([mlp[0][2 * half], mlp[1][2 * half]])
-            return qkv, out, up, down, bias_qkv, bias_up
-
-        if quick:
-            att_sum = jnp.where(at_source, att_sum, att_chip)
+            return qkv, out, jnp.stack([att[0][half, :cols], att[1][half, :cols]])
+
+        if quick:
             mlp_grads = join(mlp_sum, mlp_core)
+            mlp_grads = block_grads(None, mlp_grads)
+            grad_up, grad_down, grad_bias_up = mlp_grads
+            att_sum = jnp.where(at_source, att_sum, after(att_chip, grad_up, grad_down))
             att_grads = join(att_sum, core_swap(att_sum))
-            grad_qkv, grad_out, grad_up, grad_down, grad_bias_qkv, grad_bias_up = block_grads(
-                att_grads, mlp_grads
-            )
+            grad_qkv, grad_out, grad_bias_qkv = block_grads(att_grads, None)
         else:
 
             def collect(keep, send):
@@ -767,7 +766,11 @@
 
             att = collect(att_keep, att_send)
             mlp = collect(mlp_keep, mlp_send)
-            sides = [block_grads(att[:, side], mlp[:, side]) for side in (0, 1)]
+            sides = []
+            for side in (0, 1):
+                qkv_part, out_part, bias_part = block_grads(att[:, side], None)
+                up_part, down_part, up_bias = block_grads(None, mlp[:, side])
+                sides.append((qkv_part, out_part, up_part, down_part, bias_part, up_bias))
             grad_qkv, grad_up = (
                 take(jnp.concatenate([sides[0][at], sides[1][at]], axis=0), 0) for at in (0, 2)
             )

time: 236 us -> 232 us (0.983)
  waiting for transfers between devices: 88.1 us -> 82.5 us
  starting transfers between devices: 78 us -> 82.3 us
  local copies, waits for them, and re-layouts: 19.2 us -> 16.8 us
    ppermute x14, waiting for transfers between devices: 13.2 us -> 18.8 us  [col_swap(): return lax.ppermute(v, 'col', [(c, c ^ bits) for c in range(n_col)])]
    ppermute x1, waiting for transfers between devices: 3.67 us -> 0.01 us  [tokens_out(): lax.ppermute(mine, ALL, [(flat(d, r, c), flat(d ^ 2, r, c)) for d, r, c i...]
    ppermute x8, waiting for transfers between devices: 25.5 us -> 22.4 us  [chip_swap(): return lax.ppermute(v, 'dp', [(d, d ^ 2) for d in range(n_dp)])]
    ppermute x14, starting transfers between devices: 25.7 us -> 28.6 us  [col_swap(): return lax.ppermute(v, 'col', [(c, c ^ bits) for c in range(n_col)])]
    ppermute x2, starting transfers between devices: 5.9 us -> 8.47 us  [to_chip(): lax.ppermute(v, ALL, [(flat(d, r, c), flat(d ^ 2, r, c)) for d, r, c in p...]
    unnamed x76 -> x72, local copies, waits for them, and re-layouts: 5.25 us -> 3.72 us
  transfers between devices with their start and end apart: 52 -> 52, of which waited for: 31 -> 28; matrix products, arithmetic and copies ran while one was open for 11% -> 11% of each run, Pallas kernels for 6% -> 6%
where the time goes in v3:
time: 232 us; the launch traced here: 229 us
  waiting for transfers between devices  82.5 us (36%)
  starting transfers between devices  82.3 us (35%)
  Pallas kernels  20.9 us (9%)
  local copies, waits for them, and re-layouts  16.8 us (7%)
  other arithmetic  16.8 us (7%)
  matrix products  7.76 us (3%)
    ppermute x14, starting transfers between devices, col_swap(): return lax.ppermute(v, 'col', [(c, c ^ bits) for c in range(n_col)])  28.6 us
    ppermute x9, waiting for transfers between devices, row_swap(): return lax.ppermute(v, 'row', [(0, 1), (1, 0)])  22.6 us
    ppermute x8, waiting for transfers between devices, chip_swap(): return lax.ppermute(v, 'dp', [(d, d ^ 2) for d in range(n_dp)])  22.4 us
    pallas_call x6, Pallas kernels, call(): pl.pallas_call(kernel, in_specs=specs, out_specs=[pl.BlockSpec(memory_spa...  20.9 us
    ppermute x14, waiting for transfers between devices, col_swap(): return lax.ppermute(v, 'col', [(c, c ^ bits) for c in range(n_col)])  18.8 us
    ppermute x8, starting transfers between devices, chip_swap(): return lax.ppermute(v, 'dp', [(d, d ^ 2) for d in range(n_dp)])  15.2 us
    ppermute x9, starting transfers between devices, row_swap(): return lax.ppermute(v, 'row', [(0, 1), (1, 0)])  9.82 us
    ppermute x2, starting transfers between devices, to_chip(): lax.ppermute(v, ALL, [(flat(d, r, c), flat(d ^ 2, r, c)) for d, r, c in p...  8.47 us
  transfers between devices with their start and end apart: 52, of which 28 were waited for; matrix products, arithmetic and copies ran while one was open for 11% of the time, Pallas kernels for 6%

profile of v3, /device:TPU:0, one launch (start us, length us, event | category | flops | bytes accessed | tf_op | source)
XLA Modules:
  0.0 229.0 jit_solution(18312149015637256944)
XLA Ops:
  1.5 2.9 %collective-permute-start = (s32[4,2]{0,1:T(2,128)S(1)}, s32[4,2]{0,1:T(2,128)S(1)}, u32[]{:S(2)}, u32[]{:S(2)}) collective-permute-start(s32[4,2]{0,1:T(2,128)S(1)} %get-tuple-element.175), channel_id=1, source_target_pairs={{0,16},{8,24},{16,0},{24,8},{1,17},{9,25},{17,1},{25,9},{2,18},{10... | collective-permute-start | bytes 104 | tf_op jit(solution)/shard_map/ppermute | solution.py:308
  11.9 1.6 collective-permute-start.1
  13.5 2.6 %collective-permute-start.2 = (f32[8,768]{1,0:T(8,128)S(1)}, f32[8,768]{1,0:T(8,128)S(1)}, u32[]{:S(2)}, u32[]{:S(2)}) collective-permute-start(f32[8,768]{1,0:T(8,128)S(1)} %convolution_add_fusion), channel_id=1, source_target_pairs={{0,2},{1,3},{2,0},{3,1},{4,6},{5,7},{6,4},{7,5},{8,10},{9,11},{10,... | collective-permute-start | bytes 73736 | tf_op jit(solution)/shard_map/ppermute | solution.py:314
  18.4 3.3 %collective-permute-done.3 = f32[8,768]{1,0:T(8,128)S(1)} collective-permute-done((f32[8,768]{1,0:T(8,128)S(1)}, f32[8,768]{1,0:T(8,128)S(1)}, u32[]{:S(2)}, u32[]{:S(2)}) %collective-permute-start.3) | collective-permute-done | bytes 24608 | tf_op jit(solution)/shard_map/ppermute | solution.py:314
  22.6 3.2 %collective-permute-start.4 = (bf16[4,128,384]{2,1,0:T(8,128)(2,1)}, bf16[4,128,384]{2,1,0:T(8,128)(2,1)}, u32[]{:S(2)}, u32[]{:S(2)}) collective-permute-start(bf16[4,128,384]{2,1,0:T(8,128)(2,1)} %pad_maximum_fusion.8), channel_id=1, source_target_pairs={{0,16},{1,17},{2,18},{3,19},{8,24},{9,25},{10,26},{11,27},{20,4},{... | collective-permute-start | bytes 1179656 | tf_op jit(solution)/shard_map/ppermute | solution.py:369
  27.2 2.0 collective-permute-start.7
  30.5 2.4 %collective-permute-start.13 = (f32[2,2304]{1,0:T(2,128)S(1)}, f32[2,2304]{1,0:T(2,128)S(1)}, u32[]{:S(2)}, u32[]{:S(2)}) collective-permute-start(f32[2,2304]{1,0:T(2,128)S(1)} %get-tuple-element.160), channel_id=1, source_target_pairs={{0,2},{1,3},{2,0},{3,1},{4,6},{5,7},{6,4},{7,5},{8,10},{9,11},{10,... | collective-permute-start | bytes 55304 | tf_op jit(solution)/shard_map/ppermute | solution.py:314
  33.9 1.6 collective-permute-start.14
  35.6 3.3 %collective-permute-start.8 = (bf16[400,384]{1,0:T(8,128)(2,1)S(1)}, bf16[400,384]{1,0:T(8,128)(2,1)S(1)}, u32[]{:S(2)}, u32[]{:S(2)}) collective-permute-start(bf16[400,384]{1,0:T(8,128)(2,1)S(1)} %broadcast_select_fusion.5.a0), channel_id=1, source_target_pairs={{0,1},{1,0},{2,3},{3,2},{4,5},{5,4},{6,7},{7,6},{8,9},{9,8},{10,11... | collective-permute-start | bytes 921608 | tf_op jit(solution)/shard_map/ppermute | solution.py:314
  40.4 3.4 %collective-permute-done.8.a1 = bf16[400,384]{1,0:T(8,128)(2,1)S(1)} collective-permute-done((bf16[400,384]{1,0:T(8,128)(2,1)S(1)}, bf16[400,384]{1,0:T(8,128)(2,1)S(1)}, u32[]{:S(2)}, u32[]{:S(2)}) %collective-permute-start.8) | collective-permute-done | bytes 307232 | tf_op jit(solution)/shard_map/ppermute | solution.py:314
  43.8 5.0 %collective-permute-start.9 = (bf16[784,384]{1,0:T(8,128)(2,1)}, bf16[784,384]{1,0:T(8,128)(2,1)}, u32[]{:S(2)}, u32[]{:S(2)}) collective-permute-start(bf16[784,384]{1,0:T(8,128)(2,1)} %select_bitcast_fusion), channel_id=1, source_target_pairs={{0,2},{3,1},{4,6},{7,5},{8,10},{11,9},{12,14},{15,13},{17,19},{18,... | collective-permute-start | bytes 1806344 | tf_op jit(solution)/shard_map/ppermute | solution.py:520
  49.1 1.6 collective-permute-start.15
  50.6 2.4 %collective-permute-done.15 = f32[8,384]{1,0:T(8,128)S(1)} collective-permute-done((f32[8,384]{1,0:T(8,128)S(1)}, f32[8,384]{1,0:T(8,128)S(1)}, u32[]{:S(2)}, u32[]{:S(2)}) %collective-permute-start.15) | collective-permute-done | bytes 12320 | tf_op jit(solution)/shard_map/ppermute | solution.py:311
  55.1 2.1 collective-permute-done.9
  57.3 4.7 %collective-permute-start.10 = (bf16[784,384]{1,0:T(8,128)(2,1)S(1)}, bf16[784,384]{1,0:T(8,128)(2,1)S(1)}, u32[]{:S(2)}, u32[]{:S(2)}) collective-permute-start(bf16[784,384]{1,0:T(8,128)(2,1)S(1)} %broadcast_select_fusion.1.a0), channel_id=1, source_target_pairs={{0,1},{1,0},{2,3},{3,2},{4,5},{5,4},{6,7},{7,6},{8,9},{9,8},{10,11... | collective-permute-start | bytes 1806344 | tf_op jit(solution)/shard_map/ppermute | solution.py:314
  63.2 6.1 %collective-permute-done.16.a2 = bf16[400,384]{1,0:T(8,128)(2,1)S(1)} collective-permute-done((bf16[400,384]{1,0:T(8,128)(2,1)S(1)}, bf16[400,384]{1,0:T(8,128)(2,1)S(1)}, u32[]{:S(2)}, u32[]{:S(2)}) %collective-permute-start.16) | collective-permute-done | bytes 307232 | tf_op jit(solution)/shard_map/ppermute | solution.py:311
  69.6 6.2 %collective-permute-done.11.a2 = bf16[784,384]{1,0:T(8,128)(2,1)S(1)} collective-permute-done((bf16[784,384]{1,0:T(8,128)(2,1)S(1)}, bf16[784,384]{1,0:T(8,128)(2,1)S(1)}, u32[]{:S(2)}, u32[]{:S(2)}) %collective-permute-start.11) | collective-permute-done | bytes 602144 | tf_op jit(solution)/shard_map/ppermute | solution.py:311
  77.3 3.6 %shard_map.263 = (bf16[256,768]{1,0:T(8,128)(2,1)S(1)}, bf16[256,1536]{1,0:T(8,128)(2,1)S(1)}, f32[6,256,256]{2,1,0:T(8,128)S(1)}, f32[128,768]{1,0:T(8,128)S(1)}, bf16[128,768]{1,0:T(8,128)(2,1)S(1)}) custom-call(s32[1]{0:T(128)} %bitcast.core_ref, bf16[4,128,768]{2,1,0:T(8,128)(2,1)S(1)} %pad_maximum_fusion.5.tok_ref.x_ref, ...), custom_call_target="tpu_custom_call" | custom-call | flops 603979776 | bytes 6676480 | tf_op jit(solution)/shard_map/pallas_call | solution.py:38
  82.1 2.6 %collective-permute-start.19 = (bf16[128,768]{1,0:T(8,128)(2,1)S(1)}, bf16[128,768]{1,0:T(8,128)(2,1)S(1)}, u32[]{:S(2)}, u32[]{:S(2)}) collective-permute-start(bf16[128,768]{1,0:T(8,128)(2,1)S(1)} %get-tuple-element.73), channel_id=1, source_target_pairs={{0,16},{8,24},{16,0},{24,8},{1,17},{9,25},{17,1},{25,9},{2,18},{10... | collective-permute-start | bytes 589832 | tf_op jit(solution)/shard_map/ppermute | solution.py:308
  84.7 5.2 %collective-permute-done.19.recv = bf16[128,768]{1,0:T(8,128)(2,1)S(1)} collective-permute-done((bf16[128,768]{1,0:T(8,128)(2,1)S(1)}, bf16[128,768]{1,0:T(8,128)(2,1)S(1)}, u32[]{:S(2)}, u32[]{:S(2)}) %collective-permute-start.19) | collective-permute-done | bytes 196640 | tf_op jit(solution)/shard_map/ppermute | solution.py:308
  90.2 1.8 collective-permute-start.20
  92.1 4.6 %collective-permute-done.20.h1 = bf16[128,768]{1,0:T(8,128)(2,1)S(1)} collective-permute-done((bf16[128,768]{1,0:T(8,128)(2,1)S(1)}, bf16[128,768]{1,0:T(8,128)(2,1)S(1)}, u32[]{:S(2)}, u32[]{:S(2)}) %collective-permute-start.20) | collective-permute-done | bytes 196640 | tf_op jit(solution)/shard_map/ppermute | solution.py:308
  96.7 2.0 collective-permute-done.23.b3
  98.8 6.4 %shard_map.265 = (f32[128,768]{1,0:T(8,128)S(1)}, bf16[128,768]{1,0:T(8,128)(2,1)S(1)}, f32[128,768]{1,0:T(8,128)S(1)}, bf16[128,768]{1,0:T(8,128)(2,1)S(1)}, bf...) custom-call(bf16[128,768]{1,0:T(8,128)(2,1)S(1)} %get-tuple-element.74.h0, ...), custom_call_target="tpu_custom_call" | custom-call | flops 3623878656 | bytes 10002432 | tf_op jit(solution)/shard_map/pallas_call | solution.py:38
  105.2 2.0 copy.84
  109.7 5.7 %collective-permute-done.24.recv = bf16[128,768]{1,0:T(8,128)(2,1)S(1)} collective-permute-done((bf16[128,768]{1,0:T(8,128)(2,1)S(1)}, bf16[128,768]{1,0:T(8,128)(2,1)S(1)}, u32[]{:S(2)}, u32[]{:S(2)}) %collective-permute-start.24) | collective-permute-done | bytes 196640 | tf_op jit(solution)/shard_map/ppermute | solution.py:308
  115.4 3.0 %add_convert_fusion = bf16[2,2,784,384]{3,2,0,1:T(8,128)(2,1)S(1)} fusion(bf16[2,2,784,384]{3,2,0,1:T(8,128)(2,1)} %collective-permute-done.25, bf16[2,2,784,384]{3,2,1,0:T(8,128)(2,1)} %copy-done.6), kind=kLoop, calls=%fused_computation | loop fusion | flops 4816896 | bytes 7225344 | tf_op jit(solution)/shard_map/convert_element_type | solution.py:320
  123.1 4.5 %collective-permute-done.26.da1 = bf16[128,768]{1,0:T(8,128)(2,1)S(1)} collective-permute-done((bf16[128,768]{1,0:T(8,128)(2,1)S(1)}, bf16[128,768]{1,0:T(8,128)(2,1)S(1)}, u32[]{:S(2)}, u32[]{:S(2)}) %collective-permute-start.26) | collective-permute-done | bytes 196640 | tf_op jit(solution)/shard_map/ppermute | solution.py:308
  128.3 9.5 %shard_map.267 = (f32[128,768]{1,0:T(8,128)}, bf16[128,768]{1,0:T(8,128)(2,1)}, bf16[2,2,400,384]{3,2,1,0:T(8,128)(2,1)}, bf16[2,2,400,384]{3,2,1,0:T(8,128)(2,1)}) custom-call(s32[1]{0:T(128)} %bitcast.core_ref, bf16[256,768]{1,0:T(8,128)(2,1)} %copy-done.9, bf16[128,768]{1,0:T(8,128)(2,1)} %copy-done.13, bf16[128,768]{1,0:T(8,128)(2,1)} %copy-done.24, ...), custom_call_target="tpu_custom_call" | custom-call | flops 1207959552 | bytes 7618560 | tf_op jit(solution)/shard_map/pallas_call | solution.py:38
  137.8 2.0 collective-permute-start.27
  141.3 2.3 %collective-permute-done.27.recv = bf16[128,768]{1,0:T(8,128)(2,1)S(1)} collective-permute-done((bf16[128,768]{1,0:T(8,128)(2,1)}, bf16[128,768]{1,0:T(8,128)(2,1)S(1)}, u32[]{:S(2)}, u32[]{:S(2)}) %collective-permute-start.27) | collective-permute-done | bytes 196640 | tf_op jit(solution)/shard_map/ppermute | solution.py:308
  144.2 2.2 collective-permute-start.33
  146.5 1.7 collective-permute-start.29
  148.3 4.8 %collective-permute-start.34 = (f32[8,768]{1,0:T(8,128)S(1)}, f32[8,768]{1,0:T(8,128)S(1)}, u32[]{:S(2)}, u32[]{:S(2)}) collective-permute-start(f32[8,768]{1,0:T(8,128)S(1)} %add.133), channel_id=1, source_target_pairs={{0,1},{1,0},{2,3},{3,2},{4,5},{5,4},{6,7},{7,6},{8,9},{9,8},{10,11... | collective-permute-start | bytes 73736 | tf_op jit(solution)/shard_map/ppermute | solution.py:314
  157.1 1.7 fusion
  158.9 4.4 %collective-permute-start.37 = (bf16[784,384]{1,0:T(8,128)(2,1)S(1)}, bf16[784,384]{1,0:T(8,128)(2,1)S(1)}, u32[]{:S(2)}, u32[]{:S(2)}) collective-permute-start(bf16[784,384]{1,0:T(8,128)(2,1)S(1)} %slice_bitcast_fusion.4), channel_id=1, source_target_pairs={{0,1},{1,0},{2,3},{3,2},{4,5},{5,4},{6,7},{7,6},{8,9},{9,8},{10,11... | collective-permute-start | bytes 1806344 | tf_op jit(solution)/shard_map/ppermute | solution.py:314
  163.7 2.6 %collective-permute-start.39 = (bf16[2,400,384]{2,1,0:T(8,128)(2,1)S(1)}, bf16[2,400,384]{2,1,0:T(8,128)(2,1)S(1)}, u32[]{:S(2)}, u32[]{:S(2)}) collective-permute-start(bf16[2,400,384]{2,1,0:T(8,128)(2,1)S(1)} %slice_bitcast_fusion.2), channel_id=1, source_target_pairs={{0,4},{4,0},{1,5},{5,1},{2,6},{6,2},{3,7},{7,3},{8,12},{12,8},{9,1... | collective-permute-start | bytes 1843208 | tf_op jit(solution)/shard_map/ppermute | solution.py:311
  166.5 6.9 %collective-permute-done.37 = bf16[784,384]{1,0:T(8,128)(2,1)S(1)} collective-permute-done((bf16[784,384]{1,0:T(8,128)(2,1)S(1)}, bf16[784,384]{1,0:T(8,128)(2,1)S(1)}, u32[]{:S(2)}, u32[]{:S(2)}) %collective-permute-start.37) | collective-permute-done | bytes 602144 | tf_op jit(solution)/shard_map/ppermute | solution.py:314
  174.8 2.0 collective-permute-done.39
  177.0 1.8 collective-permute-start.40
  179.6 1.6 collective-permute-done.40
  182.5 5.0 %collective-permute-done.42 = bf16[784,384]{1,0:T(8,128)(2,1)S(1)} collective-permute-done((bf16[784,384]{1,0:T(8,128)(2,1)S(1)}, bf16[784,384]{1,0:T(8,128)(2,1)S(1)}, u32[]{:S(2)}, u32[]{:S(2)}) %collective-permute-start.42) | collective-permute-done | bytes 602144 | tf_op jit(solution)/shard_map/ppermute | solution.py:667
  187.7 7.2 %collective-permute-start.49 = (bf16[784,384]{1,0:T(8,128)(2,1)S(1)}, bf16[784,384]{1,0:T(8,128)(2,1)}, u32[]{:S(2)}, u32[]{:S(2)}) collective-permute-start(bf16[784,384]{1,0:T(8,128)(2,1)S(1)} %add_convert_fusion.2), channel_id=1, source_target_pairs={{0,16},{3,19},{4,20},{7,23},{8,24},{11,27},{12,28},{15,31},{17,1},... | collective-permute-start | bytes 1806344 | tf_op jit(solution)/shard_map/ppermute | solution.py:458
  196.0 3.1 %collective-permute-done.43 = f32[16,192]{1,0:T(8,128)S(1)} collective-permute-done((f32[16,192]{1,0:T(8,128)S(1)}, f32[16,192]{1,0:T(8,128)S(1)}, u32[]{:S(2)}, u32[]{:S(2)}) %collective-permute-start.43) | collective-permute-done | bytes 12320 | tf_op jit(solution)/shard_map/ppermute | solution.py:311
  199.2 2.8 %convolution_bitcast_fusion = f32[1,192,6,384]{3,1,2,0:T(8,128)} fusion(f32[16,194]{1,0:T(8,128)S(1)} %constant_dynamic-update-slice_fusion, f32[2,8,6,384]{3,2,1,0:T(8,128)S(1)} %bitcast.175), kind=kOutput, calls=%fused_computation.7 | convolution fusion | flops 84946944 | bytes 1929344 | tf_op jit(solution)/shard_map/dot_general | solution.py:693
  205.3 2.7 %collective-permute-done.45 = f32[2,16,192]{2,1,0:T(8,128)S(1)} collective-permute-done((f32[2,16,192]{2,1,0:T(8,128)S(1)}, f32[2,16,192]{2,1,0:T(8,128)S(1)}, u32[]{:S(2)}, u32[]{:S(2)}) %collective-permute-start.45) | collective-permute-done | bytes 24608 | tf_op jit(solution)/shard_map/ppermute | solution.py:314
  208.2 5.5 %collective-permute-done.47 = bf16[400,384]{1,0:T(8,128)(2,1)S(1)} collective-permute-done((bf16[400,384]{1,0:T(8,128)(2,1)S(1)}, bf16[400,384]{1,0:T(8,128)(2,1)S(1)}, u32[]{:S(2)}, u32[]{:S(2)}) %collective-permute-start.47) | collective-permute-done | bytes 307232 | tf_op jit(solution)/shard_map/ppermute | solution.py:706
  216.7 2.7 %collective-permute-done.48 = bf16[400,384]{1,0:T(8,128)(2,1)S(1)} collective-permute-done((bf16[400,384]{1,0:T(8,128)(2,1)S(1)}, bf16[400,384]{1,0:T(8,128)(2,1)S(1)}, u32[]{:S(2)}, u32[]{:S(2)}) %collective-permute-start.48) | collective-permute-done | bytes 307232 | tf_op jit(solution)/shard_map/ppermute | solution.py:458
  (266 shorter events, 58.7 us)
Async XLA Ops:
  1.5 8.2 %collective-permute-start = (s32[4,2]{0,1:T(2,128)S(1)}, s32[4,2]{0,1:T(2,128)S(1)}, u32[]{:S(2)}, u32[]{:S(2)}) collective-permute-start(s32[4,2]{0,1:T(2,128)S(1)} %get-tuple-element.175), channel_id=1, source_target_pairs={{0,16},{8,24},{16,0},{24,8},{1,17},{9,25},{17,1},{25,9},{2,18},{10... | collective-permute-start | bytes 104 | tf_op jit(solution)/shard_map/ppermute | solution.py:308
  11.9 5.2 %collective-permute-start.1 = (f32[8,768]{1,0:T(8,128)S(1)}, f32[8,768]{1,0:T(8,128)S(1)}, u32[]{:S(2)}, u32[]{:S(2)}) collective-permute-start(f32[8,768]{1,0:T(8,128)S(1)} %convolution_add_fusion), channel_id=1, source_target_pairs={{0,1},{1,0},{2,3},{3,2},{4,5},{5,4},{6,7},{7,6},{8,9},{9,8},{10,11... | collective-permute-start | bytes 73736 | tf_op jit(solution)/shard_map/ppermute | solution.py:314
  13.5 4.9 %collective-permute-start.2 = (f32[8,768]{1,0:T(8,128)S(1)}, f32[8,768]{1,0:T(8,128)S(1)}, u32[]{:S(2)}, u32[]{:S(2)}) collective-permute-start(f32[8,768]{1,0:T(8,128)S(1)} %convolution_add_fusion), channel_id=1, source_target_pairs={{0,2},{1,3},{2,0},{3,1},{4,6},{5,7},{6,4},{7,5},{8,10},{9,11},{10,... | collective-permute-start | bytes 73736 | tf_op jit(solution)/shard_map/ppermute | solution.py:314
  16.1 5.6 %collective-permute-start.3 = (f32[8,768]{1,0:T(8,128)S(1)}, f32[8,768]{1,0:T(8,128)S(1)}, u32[]{:S(2)}, u32[]{:S(2)}) collective-permute-start(f32[8,768]{1,0:T(8,128)S(1)} %convolution_add_fusion), channel_id=1, source_target_pairs={{0,3},{1,2},{2,1},{3,0},{4,7},{5,6},{6,5},{7,4},{8,11},{9,10},{10,... | collective-permute-start | bytes 73736 | tf_op jit(solution)/shard_map/ppermute | solution.py:314
  22.6 13.1 %collective-permute-start.4 = (bf16[4,128,384]{2,1,0:T(8,128)(2,1)}, bf16[4,128,384]{2,1,0:T(8,128)(2,1)}, u32[]{:S(2)}, u32[]{:S(2)}) collective-permute-start(bf16[4,128,384]{2,1,0:T(8,128)(2,1)} %pad_maximum_fusion.8), channel_id=1, source_target_pairs={{0,16},{1,17},{2,18},{3,19},{8,24},{9,25},{10,26},{11,27},{20,4},{... | collective-permute-start | bytes 1179656 | tf_op jit(solution)/shard_map/ppermute | solution.py:369
  25.8 23.1 %collective-permute-start.6 = (bf16[4,128,384]{2,1,0:T(8,128)(2,1)}, bf16[4,128,384]{2,1,0:T(8,128)(2,1)}, u32[]{:S(2)}, u32[]{:S(2)}) collective-permute-start(bf16[4,128,384]{2,1,0:T(8,128)(2,1)} %pad_maximum_fusion.8), channel_id=1, source_target_pairs={{4,16},{5,17},{6,18},{7,19},{12,24},{13,25},{14,26},{15,27},{16,4}... | collective-permute-start | bytes 1179656 | tf_op jit(solution)/shard_map/ppermute | solution.py:366
  27.2 6.7 %collective-permute-start.7 = (bf16[400,384]{1,0:T(8,128)(2,1)}, bf16[400,384]{1,0:T(8,128)(2,1)}, u32[]{:S(2)}, u32[]{:S(2)}) collective-permute-start(bf16[400,384]{1,0:T(8,128)(2,1)} %fusion.11), channel_id=1, source_target_pairs={{0,2},{3,1},{4,6},{7,5},{8,10},{11,9},{12,14},{15,13},{17,19},{18,... | collective-permute-start | bytes 921608 | tf_op jit(solution)/shard_map/ppermute | solution.py:486
  30.4 8.6 %collective-permute-start.12 = (f32[2,2304]{1,0:T(2,128)S(1)}, f32[2,2304]{1,0:T(2,128)S(1)}, u32[]{:S(2)}, u32[]{:S(2)}) collective-permute-start(f32[2,2304]{1,0:T(2,128)S(1)} %get-tuple-element.161), channel_id=1, source_target_pairs={{0,1},{1,0},{2,3},{3,2},{4,5},{5,4},{6,7},{7,6},{8,9},{9,8},{10,11... | collective-permute-start | bytes 55304 | tf_op jit(solution)/shard_map/ppermute | solution.py:314
  30.5 9.9 %collective-permute-start.13 = (f32[2,2304]{1,0:T(2,128)S(1)}, f32[2,2304]{1,0:T(2,128)S(1)}, u32[]{:S(2)}, u32[]{:S(2)}) collective-permute-start(f32[2,2304]{1,0:T(2,128)S(1)} %get-tuple-element.160), channel_id=1, source_target_pairs={{0,2},{1,3},{2,0},{3,1},{4,6},{5,7},{6,4},{7,5},{8,10},{9,11},{10,... | collective-permute-start | bytes 55304 | tf_op jit(solution)/shard_map/ppermute | solution.py:314
  33.9 6.5 %collective-permute-start.14 = (f32[2,2304]{1,0:T(2,128)S(1)}, f32[2,2304]{1,0:T(2,128)S(1)}, u32[]{:S(2)}, u32[]{:S(2)}) collective-permute-start(f32[2,2304]{1,0:T(2,128)S(1)} %get-tuple-element.159), channel_id=1, source_target_pairs={{0,3},{1,2},{2,1},{3,0},{4,7},{5,6},{6,5},{7,4},{8,11},{9,10},{10,... | collective-permute-start | bytes 55304 | tf_op jit(solution)/shard_map/ppermute | solution.py:314
  35.6 8.2 %collective-permute-start.8 = (bf16[400,384]{1,0:T(8,128)(2,1)S(1)}, bf16[400,384]{1,0:T(8,128)(2,1)S(1)}, u32[]{:S(2)}, u32[]{:S(2)}) collective-permute-start(bf16[400,384]{1,0:T(8,128)(2,1)S(1)} %broadcast_select_fusion.5.a0), channel_id=1, source_target_pairs={{0,1},{1,0},{2,3},{3,2},{4,5},{5,4},{6,7},{7,6},{8,9},{9,8},{10,11... | collective-permute-start | bytes 921608 | tf_op jit(solution)/shard_map/ppermute | solution.py:314
  39.1 9.8 %collective-permute-start.5 = (bf16[4,128,384]{2,1,0:T(8,128)(2,1)S(1)}, bf16[4,128,384]{2,1,0:T(8,128)(2,1)S(1)}, u32[]{:S(2)}, u32[]{:S(2)}) collective-permute-start(bf16[4,128,384]{2,1,0:T(8,128)(2,1)S(1)} %get-tuple-element.149), channel_id=1, source_target_pairs={{4,0},{5,1},{6,2},{7,3},{12,8},{13,9},{14,10},{15,11},{16,20},{17,... | collective-permute-start | bytes 1179656 | tf_op jit(solution)/shard_map/ppermute | solution.py:363
  43.8 13.3 %collective-permute-start.9 = (bf16[784,384]{1,0:T(8,128)(2,1)}, bf16[784,384]{1,0:T(8,128)(2,1)}, u32[]{:S(2)}, u32[]{:S(2)}) collective-permute-start(bf16[784,384]{1,0:T(8,128)(2,1)} %select_bitcast_fusion), channel_id=1, source_target_pairs={{0,2},{3,1},{4,6},{7,5},{8,10},{11,9},{12,14},{15,13},{17,19},{18,... | collective-permute-start | bytes 1806344 | tf_op jit(solution)/shard_map/ppermute | solution.py:520
  49.1 4.0 %collective-permute-start.15 = (f32[8,384]{1,0:T(8,128)S(1)}, f32[8,384]{1,0:T(8,128)S(1)}, u32[]{:S(2)}, u32[]{:S(2)}) collective-permute-start(f32[8,384]{1,0:T(8,128)S(1)} %get-tuple-element.167), channel_id=1, source_target_pairs={{0,4},{4,0},{1,5},{5,1},{2,6},{6,2},{3,7},{7,3},{8,12},{12,8},{9,1... | collective-permute-start | bytes 36872 | tf_op jit(solution)/shard_map/ppermute | solution.py:311
  53.0 10.2 %collective-permute-start.17 = (bf16[400,384]{1,0:T(8,128)(2,1)S(1)}, bf16[400,384]{1,0:T(8,128)(2,1)S(1)}, u32[]{:S(2)}, u32[]{:S(2)}) collective-permute-start(bf16[400,384]{1,0:T(8,128)(2,1)S(1)} %collective-permute-done.8.a1), channel_id=1, source_target_pairs={{0,4},{4,0},{1,5},{5,1},{2,6},{6,2},{3,7},{7,3},{8,12},{12,8},{9,1... | collective-permute-start | bytes 921608 | tf_op jit(solution)/shard_map/ppermute | solution.py:311
  54.5 14.8 %collective-permute-start.16 = (bf16[400,384]{1,0:T(8,128)(2,1)S(1)}, bf16[400,384]{1,0:T(8,128)(2,1)S(1)}, u32[]{:S(2)}, u32[]{:S(2)}) collective-permute-start(bf16[400,384]{1,0:T(8,128)(2,1)S(1)} %broadcast_select_fusion.5.a0), channel_id=1, source_target_pairs={{0,4},{4,0},{1,5},{5,1},{2,6},{6,2},{3,7},{7,3},{8,12},{12,8},{9,1... | collective-permute-start | bytes 921608 | tf_op jit(solution)/shard_map/ppermute | solution.py:311
  57.2 18.5 %collective-permute-start.11 = (bf16[784,384]{1,0:T(8,128)(2,1)S(1)}, bf16[784,384]{1,0:T(8,128)(2,1)S(1)}, u32[]{:S(2)}, u32[]{:S(2)}) collective-permute-start(bf16[784,384]{1,0:T(8,128)(2,1)S(1)} %broadcast_select_fusion.1.a0), channel_id=1, source_target_pairs={{0,4},{4,0},{1,5},{5,1},{2,6},{6,2},{3,7},{7,3},{8,12},{12,8},{9,1... | collective-permute-start | bytes 1806344 | tf_op jit(solution)/shard_map/ppermute | solution.py:311
  57.3 18.5 %collective-permute-start.10 = (bf16[784,384]{1,0:T(8,128)(2,1)S(1)}, bf16[784,384]{1,0:T(8,128)(2,1)S(1)}, u32[]{:S(2)}, u32[]{:S(2)}) collective-permute-start(bf16[784,384]{1,0:T(8,128)(2,1)S(1)} %broadcast_select_fusion.1.a0), channel_id=1, source_target_pairs={{0,1},{1,0},{2,3},{3,2},{4,5},{5,4},{6,7},{7,6},{8,9},{9,8},{10,11... | collective-permute-start | bytes 1806344 | tf_op jit(solution)/shard_map/ppermute | solution.py:314
  69.5 7.7 %collective-permute-start.18 = (bf16[4,400,384]{2,1,0:T(8,128)(2,1)S(1)}, bf16[4,400,384]{2,1,0:T(8,128)(2,1)S(1)}, u32[]{:S(2)}, u32[]{:S(2)}) collective-permute-start(bf16[4,400,384]{2,1,0:T(8,128)(2,1)S(1)} %pad_maximum_fusion.1), channel_id=1, source_target_pairs={{0,8},{8,0},{16,24},{24,16},{1,9},{9,1},{17,25},{25,17},{2,10},{10... | collective-permute-start | bytes 3686408 | tf_op jit(solution)/shard_map/ppermute | solution.py:305
  76.0 22.7 %collective-permute-start.22 = (bf16[3,784,384]{2,1,0:T(8,128)(2,1)S(1)}, bf16[3,784,384]{2,1,0:T(8,128)(2,1)S(1)}, u32[]{:S(2)}, u32[]{:S(2)}) collective-permute-start(bf16[3,784,384]{2,1,0:T(8,128)(2,1)S(1)} %pad_maximum_fusion), channel_id=1, source_target_pairs={{0,8},{8,0},{16,24},{24,16},{1,9},{9,1},{17,25},{25,17},{2,10},{10... | collective-permute-start | bytes 5419016 | tf_op jit(solution)/shard_map/ppermute | solution.py:305
  76.1 16.0 %collective-permute-start.21 = (bf16[784,384]{1,0:T(8,128)(2,1)S(1)}, bf16[784,384]{1,0:T(8,128)(2,1)S(1)}, u32[]{:S(2)}, u32[]{:S(2)}) collective-permute-start(bf16[784,384]{1,0:T(8,128)(2,1)S(1)} %collective-permute-done.10.a1), channel_id=1, source_target_pairs={{0,4},{4,0},{1,5},{5,1},{2,6},{6,2},{3,7},{7,3},{8,12},{12,8},{9,1... | collective-permute-start | bytes 1806344 | tf_op jit(solution)/shard_map/ppermute | solution.py:311
  82.1 7.8 %collective-permute-start.19 = (bf16[128,768]{1,0:T(8,128)(2,1)S(1)}, bf16[128,768]{1,0:T(8,128)(2,1)S(1)}, u32[]{:S(2)}, u32[]{:S(2)}) collective-permute-start(bf16[128,768]{1,0:T(8,128)(2,1)S(1)} %get-tuple-element.73), channel_id=1, source_target_pairs={{0,16},{8,24},{16,0},{24,8},{1,17},{9,25},{17,1},{25,9},{2,18},{10... | collective-permute-start | bytes 589832 | tf_op jit(solution)/shard_map/ppermute | solution.py:308
  90.2 6.5 %collective-permute-start.20 = (bf16[128,768]{1,0:T(8,128)(2,1)S(1)}, bf16[128,768]{1,0:T(8,128)(2,1)S(1)}, u32[]{:S(2)}, u32[]{:S(2)}) collective-permute-start(bf16[128,768]{1,0:T(8,128)(2,1)S(1)} %get-tuple-element.74.h0), channel_id=1, source_target_pairs={{0,16},{8,24},{16,0},{24,8},{1,17},{9,25},{17,1},{25,9},{2,18},{10... | collective-permute-start | bytes 589832 | tf_op jit(solution)/shard_map/ppermute | solution.py:308
  107.6 7.9 %collective-permute-start.25 = (bf16[2,2,784,384]{3,2,0,1:T(8,128)(2,1)}, bf16[2,2,784,384]{3,2,0,1:T(8,128)(2,1)}, u32[]{:S(2)}, u32[]{:S(2)}) collective-permute-start(bf16[2,2,784,384]{3,2,0,1:T(8,128)(2,1)} %copy.84), channel_id=1, source_target_pairs={{0,8},{8,0},{16,24},{24,16},{1,9},{9,1},{17,25},{25,17},{2,10},{10... | collective-permute-start | bytes 7225352 | tf_op jit(solution)/shard_map/ppermute | solution.py:305
  108.2 7.2 %collective-permute-start.24 = (bf16[128,768]{1,0:T(8,128)(2,1)S(1)}, bf16[128,768]{1,0:T(8,128)(2,1)S(1)}, u32[]{:S(2)}, u32[]{:S(2)}) collective-permute-start(bf16[128,768]{1,0:T(8,128)(2,1)S(1)} %get-tuple-element.77), channel_id=1, source_target_pairs={{0,16},{8,24},{16,0},{24,8},{1,17},{9,25},{17,1},{25,9},{2,18},{10... | collective-permute-start | bytes 589832 | tf_op jit(solution)/shard_map/ppermute | solution.py:308
  120.3 7.3 %collective-permute-start.26 = (bf16[128,768]{1,0:T(8,128)(2,1)S(1)}, bf16[128,768]{1,0:T(8,128)(2,1)S(1)}, u32[]{:S(2)}, u32[]{:S(2)}) collective-permute-start(bf16[128,768]{1,0:T(8,128)(2,1)S(1)} %get-tuple-element.84.da0), channel_id=1, source_target_pairs={{0,16},{8,24},{16,0},{24,8},{1,17},{9,25},{17,1},{25,9},{2,18},{10... | collective-permute-start | bytes 589832 | tf_op jit(solution)/shard_map/ppermute | solution.py:308
  121.8 35.3 %collective-permute-start.36 = (bf16[2,784,384]{2,1,0:T(8,128)(2,1)}, bf16[2,784,384]{2,1,0:T(8,128)(2,1)}, u32[]{:S(2)}, u32[]{:S(2)}) collective-permute-start(bf16[2,784,384]{2,1,0:T(8,128)(2,1)} %slice_bitcast_fusion), channel_id=1, source_target_pairs={{0,4},{4,0},{1,5},{5,1},{2,6},{6,2},{3,7},{7,3},{8,12},{12,8},{9,1... | collective-permute-start | bytes 3612680 | tf_op jit(solution)/shard_map/ppermute | solution.py:311
  122.4 17.4 %collective-permute-start.32 = (f32[8,194]{1,0:T(8,128)S(1)}, f32[8,194]{1,0:T(8,128)S(1)}, u32[]{:S(2)}, u32[]{:S(2)}) collective-permute-start(f32[8,194]{1,0:T(8,128)S(1)} %reshape.134), channel_id=1, source_target_pairs={{0,8},{8,0},{16,24},{24,16},{1,9},{9,1},{17,25},{25,17},{2,10},{10... | collective-permute-start | bytes 18632 | tf_op jit(solution)/shard_map/ppermute | solution.py:305
  122.5 18.9 %collective-permute-start.28 = (bf16[128,768]{1,0:T(8,128)(2,1)}, bf16[128,768]{1,0:T(8,128)(2,1)S(1)}, u32[]{:S(2)}, u32[]{:S(2)}) collective-permute-start(bf16[128,768]{1,0:T(8,128)(2,1)} %copy-done.14), channel_id=1, source_target_pairs={{0,16},{8,24},{16,0},{24,8},{1,17},{9,25},{17,1},{25,9},{2,18},{10... | collective-permute-start | bytes 589832 | tf_op jit(solution)/shard_map/ppermute | solution.py:308
  137.8 5.9 %collective-permute-start.27 = (bf16[128,768]{1,0:T(8,128)(2,1)}, bf16[128,768]{1,0:T(8,128)(2,1)S(1)}, u32[]{:S(2)}, u32[]{:S(2)}) collective-permute-start(bf16[128,768]{1,0:T(8,128)(2,1)} %get-tuple-element.88), channel_id=1, source_target_pairs={{0,16},{8,24},{16,0},{24,8},{1,17},{9,25},{17,1},{25,9},{2,18},{10... | collective-permute-start | bytes 589832 | tf_op jit(solution)/shard_map/ppermute | solution.py:308
  141.2 22.1 %collective-permute-start.38 = (bf16[2,2,400,384]{3,2,0,1:T(8,128)(2,1)S(1)}, bf16[2,2,400,384]{3,2,0,1:T(8,128)(2,1)S(1)}, u32[]{:S(2)}, u32[]{:S(2)}) collective-permute-start(bf16[2,2,400,384]{3,2,0,1:T(8,128)(2,1)S(1)} %copy.87), channel_id=1, source_target_pairs={{0,8},{8,0},{16,24},{24,16},{1,9},{9,1},{17,25},{25,17},{2,10},{10... | collective-permute-start | bytes 3686408 | tf_op jit(solution)/shard_map/ppermute | solution.py:305
  144.2 4.0 %collective-permute-start.33 = (f32[8,768]{1,0:T(8,128)S(1)}, f32[8,768]{1,0:T(8,128)S(1)}, u32[]{:S(2)}, u32[]{:S(2)}) collective-permute-start(f32[8,768]{1,0:T(8,128)S(1)} %get-tuple-element.96), channel_id=1, source_target_pairs={{0,16},{8,24},{16,0},{24,8},{1,17},{9,25},{17,1},{25,9},{2,18},{10... | collective-permute-start | bytes 73736 | tf_op jit(solution)/shard_map/ppermute | solution.py:308
  146.5 9.2 %collective-permute-start.29 = (bf16[2,128,384]{2,1,0:T(8,128)(2,1)S(1)}, bf16[2,128,384]{2,1,0:T(8,128)(2,1)S(1)}, u32[]{:S(2)}, u32[]{:S(2)}) collective-permute-start(bf16[2,128,384]{2,1,0:T(8,128)(2,1)S(1)} %slice.187), channel_id=1, source_target_pairs={{0,4},{1,5},{2,6},{3,7},{8,12},{9,13},{10,14},{11,15},{20,16},{21,... | collective-permute-start | bytes 589832 | tf_op jit(solution)/shard_map/ppermute | solution.py:397
  148.3 6.6 %collective-permute-start.34 = (f32[8,768]{1,0:T(8,128)S(1)}, f32[8,768]{1,0:T(8,128)S(1)}, u32[]{:S(2)}, u32[]{:S(2)}) collective-permute-start(f32[8,768]{1,0:T(8,128)S(1)} %add.133), channel_id=1, source_target_pairs={{0,1},{1,0},{2,3},{3,2},{4,5},{5,4},{6,7},{7,6},{8,9},{9,8},{10,11... | collective-permute-start | bytes 73736 | tf_op jit(solution)/shard_map/ppermute | solution.py:314
  153.2 13.1 %collective-permute-start.31 = (bf16[2,128,384]{2,1,0:T(8,128)(2,1)S(1)}, bf16[2,128,384]{2,1,0:T(8,128)(2,1)S(1)}, u32[]{:S(2)}, u32[]{:S(2)}) collective-permute-start(bf16[2,128,384]{2,1,0:T(8,128)(2,1)S(1)} %slice.187), channel_id=1, source_target_pairs={{4,16},{5,17},{6,18},{7,19},{12,24},{13,25},{14,26},{15,27},{16,4}... | collective-permute-start | bytes 589832 | tf_op jit(solution)/shard_map/ppermute | solution.py:400
  154.8 11.6 %collective-permute-start.35 = (f32[2,8,768]{2,1,0:T(8,128)S(1)}, f32[2,8,768]{2,1,0:T(8,128)S(1)}, u32[]{:S(2)}, u32[]{:S(2)}) collective-permute-start(f32[2,8,768]{2,1,0:T(8,128)S(1)} %get-tuple-element.163), channel_id=1, source_target_pairs={{0,2},{1,3},{2,0},{3,1},{4,6},{5,7},{6,4},{7,5},{8,10},{9,11},{10,... | collective-permute-start | bytes 147464 | tf_op jit(solution)/shard_map/ppermute | solution.py:314
  155.8 10.5 %collective-permute-start.30 = (bf16[2,128,384]{2,1,0:T(8,128)(2,1)S(1)}, bf16[2,128,384]{2,1,0:T(8,128)(2,1)S(1)}, u32[]{:S(2)}, u32[]{:S(2)}) collective-permute-start(bf16[2,128,384]{2,1,0:T(8,128)(2,1)S(1)} %get-tuple-element.147), channel_id=1, source_target_pairs={{4,20},{5,21},{6,22},{7,23},{12,28},{13,29},{14,30},{15,31},{16,0}... | collective-permute-start | bytes 589832 | tf_op jit(solution)/shard_map/ppermute | solution.py:394
  158.9 14.5 %collective-permute-start.37 = (bf16[784,384]{1,0:T(8,128)(2,1)S(1)}, bf16[784,384]{1,0:T(8,128)(2,1)S(1)}, u32[]{:S(2)}, u32[]{:S(2)}) collective-permute-start(bf16[784,384]{1,0:T(8,128)(2,1)S(1)} %slice_bitcast_fusion.4), channel_id=1, source_target_pairs={{0,1},{1,0},{2,3},{3,2},{4,5},{5,4},{6,7},{7,6},{8,9},{9,8},{10,11... | collective-permute-start | bytes 1806344 | tf_op jit(solution)/shard_map/ppermute | solution.py:314
  163.7 13.1 %collective-permute-start.39 = (bf16[2,400,384]{2,1,0:T(8,128)(2,1)S(1)}, bf16[2,400,384]{2,1,0:T(8,128)(2,1)S(1)}, u32[]{:S(2)}, u32[]{:S(2)}) collective-permute-start(bf16[2,400,384]{2,1,0:T(8,128)(2,1)S(1)} %slice_bitcast_fusion.2), channel_id=1, source_target_pairs={{0,4},{4,0},{1,5},{5,1},{2,6},{6,2},{3,7},{7,3},{8,12},{12,8},{9,1... | collective-permute-start | bytes 1843208 | tf_op jit(solution)/shard_map/ppermute | solution.py:311
  173.5 14.0 %collective-permute-start.42 = (bf16[784,384]{1,0:T(8,128)(2,1)S(1)}, bf16[784,384]{1,0:T(8,128)(2,1)S(1)}, u32[]{:S(2)}, u32[]{:S(2)}) collective-permute-start(bf16[784,384]{1,0:T(8,128)(2,1)S(1)} %fusion.5), channel_id=1, source_target_pairs={{2,0},{1,3},{6,4},{5,7},{10,8},{9,11},{14,12},{13,15},{19,17},{16,... | collective-permute-start | bytes 1806344 | tf_op jit(solution)/shard_map/ppermute | solution.py:667
  177.0 4.2 %collective-permute-start.40 = (f32[32,384]{1,0:T(8,128)S(1)}, f32[32,384]{1,0:T(8,128)S(1)}, u32[]{:S(2)}, u32[]{:S(2)}) collective-permute-start(f32[32,384]{1,0:T(8,128)S(1)} %get-tuple-element.158), channel_id=1, source_target_pairs={{0,4},{4,0},{1,5},{5,1},{2,6},{6,2},{3,7},{7,3},{8,12},{12,8},{9,1... | collective-permute-start | bytes 147464 | tf_op jit(solution)/shard_map/ppermute | solution.py:311
  181.3 22.7 %collective-permute-start.46 = (bf16[400,384]{1,0:T(8,128)(2,1)S(1)}, bf16[400,384]{1,0:T(8,128)(2,1)S(1)}, u32[]{:S(2)}, u32[]{:S(2)}) collective-permute-start(bf16[400,384]{1,0:T(8,128)(2,1)S(1)} %slice_bitcast_fusion.6), channel_id=1, source_target_pairs={{0,1},{1,0},{2,3},{3,2},{4,5},{5,4},{6,7},{7,6},{8,9},{9,8},{10,11... | collective-permute-start | bytes 921608 | tf_op jit(solution)/shard_map/ppermute | solution.py:314
  187.7 33.3 %collective-permute-start.49 = (bf16[784,384]{1,0:T(8,128)(2,1)S(1)}, bf16[784,384]{1,0:T(8,128)(2,1)}, u32[]{:S(2)}, u32[]{:S(2)}) collective-permute-start(bf16[784,384]{1,0:T(8,128)(2,1)S(1)} %add_convert_fusion.2), channel_id=1, source_target_pairs={{0,16},{3,19},{4,20},{7,23},{8,24},{11,27},{12,28},{15,31},{17,1},... | collective-permute-start | bytes 1806344 | tf_op jit(solution)/shard_map/ppermute | solution.py:458
  195.3 3.8 %collective-permute-start.43 = (f32[16,192]{1,0:T(8,128)S(1)}, f32[16,192]{1,0:T(8,128)S(1)}, u32[]{:S(2)}, u32[]{:S(2)}) collective-permute-start(f32[16,192]{1,0:T(8,128)S(1)} %fusion.6), channel_id=1, source_target_pairs={{0,4},{4,0},{1,5},{5,1},{2,6},{6,2},{3,7},{7,3},{8,12},{12,8},{9,1... | collective-permute-start | bytes 36872 | tf_op jit(solution)/shard_map/ppermute | solution.py:311
  199.2 3.8 %collective-permute-start.44 = (f32[16,192]{1,0:T(8,128)S(1)}, f32[16,192]{1,0:T(8,128)S(1)}, u32[]{:S(2)}, u32[]{:S(2)}) collective-permute-start(f32[16,192]{1,0:T(8,128)S(1)} %add_multiply_fusion), channel_id=1, source_target_pairs={{0,1},{1,0},{2,3},{3,2},{4,5},{5,4},{6,7},{7,6},{8,9},{9,8},{10,11... | collective-permute-start | bytes 36872 | tf_op jit(solution)/shard_map/ppermute | solution.py:314
  203.2 4.9 %collective-permute-start.45 = (f32[2,16,192]{2,1,0:T(8,128)S(1)}, f32[2,16,192]{2,1,0:T(8,128)S(1)}, u32[]{:S(2)}, u32[]{:S(2)}) collective-permute-start(f32[2,16,192]{2,1,0:T(8,128)S(1)} %get-tuple-element.165), channel_id=1, source_target_pairs={{0,2},{1,3},{2,0},{3,1},{4,6},{5,7},{6,4},{7,5},{8,10},{9,11},{10,... | collective-permute-start | bytes 73736 | tf_op jit(solution)/shard_map/ppermute | solution.py:314
  204.0 9.6 %collective-permute-start.47 = (bf16[400,384]{1,0:T(8,128)(2,1)S(1)}, bf16[400,384]{1,0:T(8,128)(2,1)S(1)}, u32[]{:S(2)}, u32[]{:S(2)}) collective-permute-start(bf16[400,384]{1,0:T(8,128)(2,1)S(1)} %fusion.10), channel_id=1, source_target_pairs={{2,0},{1,3},{6,4},{5,7},{10,8},{9,11},{14,12},{13,15},{19,17},{16,... | collective-permute-start | bytes 921608 | tf_op jit(solution)/shard_map/ppermute | solution.py:706
  213.8 5.7 %collective-permute-start.48 = (bf16[400,384]{1,0:T(8,128)(2,1)S(1)}, bf16[400,384]{1,0:T(8,128)(2,1)S(1)}, u32[]{:S(2)}, u32[]{:S(2)}) collective-permute-start(bf16[400,384]{1,0:T(8,128)(2,1)S(1)} %add_convert_fusion.3), channel_id=1, source_target_pairs={{0,16},{3,19},{4,20},{7,23},{8,24},{11,27},{12,28},{15,31},{17,1},... | collective-permute-start | bytes 921608 | tf_op jit(solution)/shard_map/ppermute | solution.py:458
  (38 other events, 284.9 us)
